TPU v7x, 32 devices: a whole 2x2x4 slice. The times are simulated.
32 devices in a mesh: px: 8 (over y, x, core), py: 4 (over z).
Axes of the slice: x: 2, y: 2, z: 4, core: 2. Of those that a mesh axis runs over, the one named last changes fastest.
Arguments:
- source: float32 [8, 256, 512], P(None, 'px', 'py'), may hold values from -12 to 12
- coefficient: float32 [8, 256, 512], P(None, 'px', 'py'), may hold values from 0.25 to 4
- strip_rows: int32 [4], replicated, may hold values from 1 to 40, 64 in all
Outputs:
- solution: float32 [8, 256, 512], P(None, 'px', 'py')
Inputs may be any that keep to these rules, and one draw needn't show every extreme that they name: `strip_rows`: the entries sum to 64 and the largest is exactly 40.
All inputs are finite; a program needn't handle non-finite values.
Results may differ from a plain program's by a relative error of at most 0.00027.
Values sent between devices are 32-bit elements; how exact they have to be, the bound alone decides.
No kernel may reach another device: no remote copies, remote signals or barrier semaphores. Data moves between devices by JAX's collectives and lax.ppermute only.
A program may use at most 128 MiB of HBM per device.

v0:
```python
import jax
import jax.numpy as jnp
from jax import lax
from jax.sharding import PartitionSpec as P

CYCLES = 2
PRE = 2
POST = 2
COARSE_SWEEPS = 6


relaxation = 0.8
z_coupling = 0.25


def extended(array, sides, width):
    for axis, dim in sides:
        peers, length = (lax.axis_size(axis), array.shape[dim])
        up = [(i, (i + 1) % peers) for i in range(peers - 1)]
        down = [(j, i) for i, j in up]
        last = lax.slice_in_dim(array, length - width, length, axis=dim)
        initial = lax.slice_in_dim(array, 0, width, axis=dim)
        before = lax.ppermute(last, axis, up)
        after = lax.ppermute(initial, axis, down)
        array = jnp.concatenate([before, array, after], axis=dim)
    return array


def pad_plain(values):
    return jnp.pad(values, ((0, 0), (1, 1), (1, 1)))


def extend(values, margin_width):
    return extended(values[None], (("px", 2), ("py", 3)), margin_width)[0]


def face_arrays(conduct, z_factor):
    padded = pad_plain(conduct)
    face_west = 0.5 * (conduct + padded[:, :-2, 1:-1])
    face_east = 0.5 * (conduct + padded[:, 2:, 1:-1])
    face_south = 0.5 * (conduct + padded[:, 1:-1, :-2])
    face_north = 0.5 * (conduct + padded[:, 1:-1, 2:])
    vertical = z_factor * 0.5 * (conduct[:-1] + conduct[1:])
    zero_layer = jnp.zeros_like(conduct[:1])
    face_down = jnp.concatenate([zero_layer, vertical], axis=0)
    face_up = jnp.concatenate([vertical, zero_layer], axis=0)
    diagonal = face_west + face_east + face_south + face_north + face_down + face_up
    return [face_west, face_east, face_south, face_north, face_down, face_up, diagonal]


def invert(diagonal, inside):
    safe_diag = jnp.where(inside, diagonal, 1.0)
    return jnp.where(inside, 1.0 / safe_diag, 0.0)


def update(values, values_pad, faces, source_term):
    face_west, face_east, face_south, face_north, face_down, face_up, diagonal, inverse = faces
    zero_layer = jnp.zeros_like(values[:1])
    value_down = jnp.concatenate([zero_layer, values[:-1]], axis=0)
    value_up = jnp.concatenate([values[1:], zero_layer], axis=0)
    beside = (
        face_west * values_pad[:, :-2, 1:-1]
        + face_east * values_pad[:, 2:, 1:-1]
        + face_south * values_pad[:, 1:-1, :-2]
        + face_north * values_pad[:, 1:-1, 2:]
        + face_down * value_down
        + face_up * value_up
    )
    return source_term - diagonal * values + beside


def relax_sweep(values, values_pad, faces, source_term):
    return values + relaxation * faces[7] * update(values, values_pad, faces, source_term)


def residual(values, source_term, faces_int):
    return update(values, extend(values, 1), faces_int, source_term)


def coarsen(values):
    layers, row_count, col_count = values.shape
    return 0.25 * values.reshape(layers, row_count // 2, 2, col_count // 2, 2).sum(axis=(2, 4))


def restrict(values):
    layers, row_count, col_count = values.shape
    return values.reshape(layers, row_count // 2, 2, col_count // 2, 2).sum(axis=(2, 4))


def prolong(values):
    return jnp.repeat(jnp.repeat(values, 2, axis=1), 2, axis=2)


def prepare(conduct, z_factor, margin_width):
    wide = extend(conduct, margin_width)
    faces_ext = face_arrays(wide, z_factor)
    faces_ext.append(invert(faces_ext[6], wide > 0.0))
    faces_int = [
        member[:, margin_width:-margin_width, margin_width:-margin_width] for member in faces_ext
    ]
    return (faces_int, faces_ext)


def smooth_level(values, source_term, faces_int, count):
    for sweep_index in range(count):
        values = relax_sweep(values, extend(values, 1), faces_int, source_term)
    return values


def to_strips(level_values, starts, most_rows):
    gathered = lax.all_gather(level_values, "px", axis=1, tiled=True)
    padded = jnp.pad(gathered, ((0, 0), (1, most_rows + 1), (0, 0)))

    def cut_strip(first_row):
        return lax.dynamic_slice_in_dim(padded, first_row, most_rows + 2, 1)

    pieces = jax.vmap(cut_strip)(starts)
    return lax.all_to_all(pieces, "py", split_axis=0, concat_axis=3, tiled=True)[0]


def from_strips(strip_values, starts, block_x, quarter_x):
    returned = lax.all_to_all(strip_values[None], "py", split_axis=3, concat_axis=0, tiled=True)
    pieces_count = returned.shape[0]
    strip_span = returned.shape[2]
    width_y = returned.shape[3]
    rows_total = quarter_x * lax.axis_size("px")
    canvas = jnp.zeros((returned.shape[1], rows_total + strip_span, width_y), jnp.float32)

    def place_strip(strip_index, canvas_now):
        first_row = starts[strip_index]
        current = lax.dynamic_slice_in_dim(canvas_now, first_row, strip_span, 1)
        piece = lax.dynamic_index_in_dim(returned, strip_index, 0, keepdims=False)
        return lax.dynamic_update_slice_in_dim(canvas_now, current + piece, first_row, 1)

    canvas = lax.fori_loop(0, pieces_count, place_strip, canvas)
    return lax.dynamic_slice_in_dim(canvas, 1 + block_x * quarter_x, quarter_x, 1)


def shards(source, coefficient, strip_rows):
    block_x = lax.axis_index("px")
    block_y = lax.axis_index("py")
    margin_width = max(PRE, POST)
    fine_int, fine_ext = prepare(coefficient, z_coupling, margin_width)
    mid_conduct = coarsen(coefficient)
    mid_int, mid_ext = prepare(mid_conduct, 4.0 * z_coupling, margin_width)
    low_conduct = coarsen(mid_conduct)
    starts = jnp.cumsum(strip_rows) - strip_rows
    quarter = low_conduct.shape[1]
    rows_total = quarter * lax.axis_size("px")
    most_rows = min(rows_total // 2 + quarter, rows_total - lax.axis_size("py") + 1)
    strip_conduct = to_strips(low_conduct, starts, most_rows)
    row_iota = jnp.arange(strip_conduct.shape[1], dtype=jnp.int32)
    own_rows = strip_rows[block_y]
    inside = jnp.broadcast_to(
        ((row_iota >= 1) & (row_iota <= own_rows))[None, :, None], strip_conduct.shape
    )
    inside_weight = inside.astype(jnp.float32)
    low_faces = face_arrays(strip_conduct, 16.0 * z_coupling)
    low_faces.append(invert(low_faces[6], inside))
    diag_total = jnp.sum(low_faces[6] * inside_weight)
    solution = jnp.zeros_like(source)
    for cycle_index in range(CYCLES):
        solution = smooth_level(solution, source, fine_int, PRE)
        mid_source = restrict(residual(solution, source, fine_int))
        middle = smooth_level(jnp.zeros_like(mid_source), mid_source, mid_int, PRE)
        low_source = restrict(residual(middle, mid_source, mid_int))
        strip_source = to_strips(low_source, starts, most_rows)
        strip_values = jnp.zeros_like(strip_source)
        for sweep_index in range(COARSE_SWEEPS):
            strip_values = relax_sweep(
                strip_values, pad_plain(strip_values), low_faces, strip_source
            )
        left_over = update(strip_values, pad_plain(strip_values), low_faces, strip_source)
        shift_strip = jnp.sum(left_over * inside_weight) / diag_total
        strip_values = strip_values + shift_strip * inside_weight
        correction = from_strips(strip_values, starts, block_x, quarter)
        middle = smooth_level(middle + prolong(correction), mid_source, mid_int, POST)
        solution = smooth_level(solution + prolong(middle), source, fine_int, POST)
    return solution


def solution(mesh):
    placed = (P(None, "px", "py"), P(None, "px", "py"), P())
    return jax.shard_map(
        shards, mesh=mesh, in_specs=placed, out_specs=P(None, "px", "py"), check_vma=False
    )
```

profile of v0, /device:TPU:28, one launch (start us, length us, event | category | flops | bytes accessed | tf_op | source)
XLA Modules:
  0.0 558.0 jit_solution(16253076059954286768)
XLA Ops:
  4.7 4.5 collective-permute-start.21
  12.2 4.5 collective-permute-start.1
  34.9 4.5 collective-permute-start.7
  41.0 4.6 collective-permute-start.15
  47.6 4.3 collective-permute-done.14
  57.4 4.4 collective-permute-done.2
  68.1 3.7 collective-permute-done.8
  77.2 4.4 collective-permute-done.10
  95.5 4.4 collective-permute-done.18
  113.5 20.6 %all_gather.9 = f32[8,64,32]{2,0,1:T(8,128)S(1)} all-gather(f32[8,8,32]{2,0,1:T(8,128)S(1)} %copy.556), channel_id=1, replica_groups=mesh['px'=8,'py'=4] {'px'}, dimensions={1}, use_global_device_ids=true | all-gather | bytes 73728 | tf_op jit(solution)/shard_map/all_gather | solution.py:111
  138.2 5.1 all-to-all-start
  149.1 4.3 collective-permute-done.26
  166.8 4.3 collective-permute-done.30
  172.2 7.9 %all_gather.10 = f32[8,64,32]{2,0,1:T(8,128)S(1)} all-gather(f32[8,8,32]{2,0,1:T(8,128)S(1)} %copy.568), channel_id=1, replica_groups=mesh['px'=8,'py'=4] {'px'}, dimensions={1}, use_global_device_ids=true | all-gather | bytes 73728 | tf_op jit(solution)/shard_map/all_gather | solution.py:111
  184.2 5.1 all-to-all-start.1
  212.9 5.1 all-to-all-start.2
  218.0 4.5 all-to-all-done.2
  228.4 26.5 %while.26 = (s32[]{:T(128)}, f32[8,106,32]{2,1,0:T(8,128)}, s32[4]{0:T(128)S(1)}, f32[4,8,42,32]{3,0,1,2:T(4,128)}, s32[]{:T(128)}, /*index=5*/s32[]{:T(128)}, s32[]{:T(128)}) while((s32[]{:T(128)}, f32[8,106,32]{2,1,0:T(8,128)}, s32[4]{0:T(128)S(1)}, f32[4,8,42,32]{3,0,1,2:T(4,128)}, s32[]{:T(128)}, /*index=5*/s32[]{:T(128)}, ...), condition=%wide.region_8.9_spmd, body=%wide.region_7.8_spmd.sunk | while | flops 10757 | bytes 301199 | solution.py:135
  260.4 3.6 collective-permute-done.32
  267.9 4.3 collective-permute-done.34
  280.5 3.8 collective-permute-start.39
  286.3 4.3 collective-permute-done.38
  299.3 3.4 collective-permute-done.40
  302.9 3.4 collective-permute-start.43
  309.1 4.4 collective-permute-done.42
  318.6 3.4 collective-permute-done.44
  327.1 4.4 collective-permute-done.46
  336.6 3.4 collective-permute-done.48
  344.8 4.4 collective-permute-done.50
  354.3 3.4 collective-permute-done.52
  362.6 4.4 collective-permute-done.54
  372.1 3.4 collective-permute-done.56
  380.4 4.4 collective-permute-done.58
  397.4 3.4 collective-permute-done.60
  404.8 4.3 collective-permute-done.62
  421.2 4.3 collective-permute-done.66
  426.6 7.9 %all_gather.11 = f32[8,64,32]{2,0,1:T(8,128)S(1)} all-gather(f32[8,8,32]{2,0,1:T(8,128)S(1)} %copy.603), channel_id=1, replica_groups=mesh['px'=8,'py'=4] {'px'}, dimensions={1}, use_global_device_ids=true | all-gather | bytes 73728 | tf_op jit(solution)/shard_map/all_gather | solution.py:111
  437.9 10.1 %all_to_all.81 = f32[4,1,10752]{2,1,0:T(1,128)S(1)} all-to-all(f32[4,1,10752]{2,1,0:T(1,128)S(1)} %reshape.149), channel_id=1, replica_groups=mesh['px'=8,'py'=4] {'py'}, dimensions={0} | all-to-all | bytes 344064 | tf_op jit(solution)/shard_map/all_to_all | solution.py:118
  459.2 5.7 %all-to-all-start.4 = ((f32[4,1,10752]{2,1,0:T(1,128)}), f32[4,1,10752]{2,1,0:T(1,128)S(1)}, u32[]{:S(2)}, u32[]{:S(2)}) async-start(f32[4,1,10752]{2,1,0:T(1,128)} %reshape.151), calls=%async_computation.4 | async-start | bytes 344064 | tf_op jit(solution)/shard_map/all_to_all | solution.py:122
  464.9 4.1 all-to-all-done.4
  471.6 12.7 %while.27 = (s32[]{:T(128)}, f32[8,106,32]{2,1,0:T(8,128)S(1)}, s32[4]{0:T(128)S(1)}, f32[4,8,42,32]{3,0,1,2:T(4,128)S(1)}, s32[]{:T(128)}, /*index=5*/s32[]{:T(128)}, s32[]{:T(128)}) while((s32[]{:T(128)}, f32[8,106,32]{2,1,0:T(8,128)S(1)}, s32[4]{0:T(128)S(1)}, f32[4,8,42,32]{3,0,1,2:T(4,128)S(1)}, s32[]{:T(128)}, /*index=5*/s32[]{:T(128)}, ...), condition=%wide.region_13.14_spmd, body=%wide.region_12.13_spmd.sunk | while | flops 10757 | bytes 301199 | solution.py:135
  497.0 4.3 collective-permute-done.70
  509.5 3.8 collective-permute-start.75
  515.3 4.3 collective-permute-done.74
  525.1 3.4 collective-permute-done.76
  534.1 4.4 collective-permute-done.78
  543.6 3.4 collective-permute-done.80
  552.1 4.4 collective-permute-done.82
  (522 shorter events, 315.0 us)
Async XLA Ops:
  0.0 32.7 %collective-permute-start.5 = (f32[1,8,1,128]{3,1,2,0:T(8,128)S(1)}, f32[1,8,1,128]{3,1,2,0:T(8,128)S(1)}, u32[]{:S(2)}, u32[]{:S(2)}) collective-permute-start(f32[1,8,1,128]{3,1,2,0:T(8,128)S(1)} %broadcast.253), channel_id=1, source_target_pairs={{4,0},{8,4},{12,8},{16,12},{20,16},{24,20},{28,24},{5,1},{9,5},{13... | collective-permute-start | bytes 12296 | tf_op jit(solution)/shard_map/ppermute | solution.py:24
  2.8 31.9 %collective-permute-start.4 = (f32[1,8,1,128]{3,1,2,0:T(8,128)S(1)}, f32[1,8,1,128]{3,1,2,0:T(8,128)S(1)}, u32[]{:S(2)}, u32[]{:S(2)}) collective-permute-start(f32[1,8,1,128]{3,1,2,0:T(8,128)S(1)} %broadcast.253), channel_id=1, source_target_pairs={{0,4},{4,8},{8,12},{12,16},{16,20},{20,24},{24,28},{1,5},{5,9},{9,... | collective-permute-start | bytes 12296 | tf_op jit(solution)/shard_map/ppermute | solution.py:23
  4.7 16.2 %collective-permute-start.21 = (f32[1,8,1,64]{3,1,2,0:T(8,128)S(1)}, f32[1,8,1,64]{3,1,2,0:T(8,128)S(1)}, u32[]{:S(2)}, u32[]{:S(2)}) collective-permute-start(f32[1,8,1,64]{3,1,2,0:T(8,128)S(1)} %broadcast.257), channel_id=1, source_target_pairs={{4,0},{8,4},{12,8},{16,12},{20,16},{24,20},{28,24},{5,1},{9,5},{13... | collective-permute-start | bytes 6152 | tf_op jit(solution)/shard_map/ppermute | solution.py:24
  9.3 11.6 %collective-permute-start.20 = (f32[1,8,1,64]{3,1,2,0:T(8,128)S(1)}, f32[1,8,1,64]{3,1,2,0:T(8,128)S(1)}, u32[]{:S(2)}, u32[]{:S(2)}) collective-permute-start(f32[1,8,1,64]{3,1,2,0:T(8,128)S(1)} %broadcast.257), channel_id=1, source_target_pairs={{0,4},{4,8},{8,12},{12,16},{16,20},{20,24},{24,28},{1,5},{5,9},{9,... | collective-permute-start | bytes 6152 | tf_op jit(solution)/shard_map/ppermute | solution.py:23
  12.2 39.8 %collective-permute-start.1 = (f32[1,8,2,128]{3,1,2,0:T(8,128)S(1)}, f32[1,8,2,128]{3,1,2,0:T(8,128)S(1)}, u32[]{:S(2)}, u32[]{:S(2)}) collective-permute-start(f32[1,8,2,128]{3,1,2,0:T(8,128)S(1)} %get-tuple-element.348), channel_id=1, source_target_pairs={{4,0},{8,4},{12,8},{16,12},{20,16},{24,20},{28,24},{5,1},{9,5},{13... | collective-permute-start | bytes 24584 | tf_op jit(solution)/shard_map/ppermute | solution.py:24
  23.3 6.2 %collective-permute-start.22 = (f32[1,8,18,1]{3,1,2,0:T(8,128)S(1)}, f32[1,8,18,1]{3,1,2,0:T(8,128)S(1)}, u32[]{:S(2)}, u32[]{:S(2)}) collective-permute-start(f32[1,8,18,1]{3,1,2,0:T(8,128)S(1)} %get-tuple-element.369), channel_id=1, source_target_pairs={{0,1},{1,2},{2,3},{4,5},{5,6},{6,7},{8,9},{9,10},{10,11},{12,13},{... | collective-permute-start | bytes 1736 | tf_op jit(solution)/shard_map/ppermute | solution.py:23
  25.4 26.6 %collective-permute-start = (f32[1,8,2,128]{3,1,2,0:T(8,128)S(1)}, f32[1,8,2,128]{3,1,2,0:T(8,128)S(1)}, u32[]{:S(2)}, u32[]{:S(2)}) collective-permute-start(f32[1,8,2,128]{3,1,2,0:T(8,128)S(1)} %get-tuple-element.347), channel_id=1, source_target_pairs={{0,4},{4,8},{8,12},{12,16},{16,20},{20,24},{24,28},{1,5},{5,9},{9,... | collective-permute-start | bytes 24584 | tf_op jit(solution)/shard_map/ppermute | solution.py:23
  29.6 9.8 %collective-permute-start.13 = (f32[1,8,2,64]{1,3,2,0:T(8,128)S(1)}, f32[1,8,2,64]{1,3,2,0:T(8,128)S(1)}, u32[]{:S(2)}, u32[]{:S(2)}) collective-permute-start(f32[1,8,2,64]{1,3,2,0:T(8,128)S(1)} %get-tuple-element.264), channel_id=1, source_target_pairs={{4,0},{8,4},{12,8},{16,12},{20,16},{24,20},{28,24},{5,1},{9,5},{13... | collective-permute-start | bytes 12296 | tf_op jit(solution)/shard_map/ppermute | solution.py:24
  32.7 8.1 %collective-permute-start.12 = (f32[1,8,2,64]{1,3,2,0:T(8,128)S(1)}, f32[1,8,2,64]{1,3,2,0:T(8,128)S(1)}, u32[]{:S(2)}, u32[]{:S(2)}) collective-permute-start(f32[1,8,2,64]{1,3,2,0:T(8,128)S(1)} %get-tuple-element.263), channel_id=1, source_target_pairs={{0,4},{4,8},{8,12},{12,16},{16,20},{20,24},{24,28},{1,5},{5,9},{9,... | collective-permute-start | bytes 12296 | tf_op jit(solution)/shard_map/ppermute | solution.py:23
  34.9 10.6 %collective-permute-start.7 = (f32[1,8,34,1]{3,2,1,0:T(8,128)S(1)}, f32[1,8,34,1]{3,2,1,0:T(8,128)S(1)}, u32[]{:S(2)}, u32[]{:S(2)}) collective-permute-start(f32[1,8,34,1]{3,2,1,0:T(8,128)S(1)} %get-tuple-element.310), channel_id=1, source_target_pairs={{1,0},{2,1},{3,2},{5,4},{6,5},{7,6},{9,8},{10,9},{11,10},{13,12},{... | collective-permute-start | bytes 3272 | tf_op jit(solution)/shard_map/ppermute | solution.py:24
  39.4 7.4 %collective-permute-start.6 = (f32[1,8,34,1]{3,2,1,0:T(8,128)S(1)}, f32[1,8,34,1]{3,2,1,0:T(8,128)S(1)}, u32[]{:S(2)}, u32[]{:S(2)}) collective-permute-start(f32[1,8,34,1]{3,2,1,0:T(8,128)S(1)} %get-tuple-element.309), channel_id=1, source_target_pairs={{0,1},{1,2},{2,3},{4,5},{5,6},{6,7},{8,9},{9,10},{10,11},{12,13},{... | collective-permute-start | bytes 3272 | tf_op jit(solution)/shard_map/ppermute | solution.py:23
  41.0 6.6 %collective-permute-start.15 = (f32[1,8,20,2]{3,1,2,0:T(8,128)S(1)}, f32[1,8,20,2]{3,1,2,0:T(8,128)S(1)}, u32[]{:S(2)}, u32[]{:S(2)}) collective-permute-start(f32[1,8,20,2]{3,1,2,0:T(8,128)S(1)} %get-tuple-element.352), channel_id=1, source_target_pairs={{1,0},{2,1},{3,2},{5,4},{6,5},{7,6},{9,8},{10,9},{11,10},{13,12},{... | collective-permute-start | bytes 3848 | tf_op jit(solution)/shard_map/ppermute | solution.py:24
  45.5 6.3 %collective-permute-start.14 = (f32[1,8,20,2]{3,1,2,0:T(8,128)S(1)}, f32[1,8,20,2]{3,1,2,0:T(8,128)S(1)}, u32[]{:S(2)}, u32[]{:S(2)}) collective-permute-start(f32[1,8,20,2]{3,1,2,0:T(8,128)S(1)} %get-tuple-element.351), channel_id=1, source_target_pairs={{0,1},{1,2},{2,3},{4,5},{5,6},{6,7},{8,9},{9,10},{10,11},{12,13},{... | collective-permute-start | bytes 3848 | tf_op jit(solution)/shard_map/ppermute | solution.py:23
  54.5 7.2 %collective-permute-start.2 = (f32[1,8,36,2]{3,2,1,0:T(8,128)S(1)}, f32[1,8,36,2]{3,2,1,0:T(8,128)S(1)}, u32[]{:S(2)}, u32[]{:S(2)}) collective-permute-start(f32[1,8,36,2]{3,2,1,0:T(8,128)S(1)} %get-tuple-element.307), channel_id=1, source_target_pairs={{0,1},{1,2},{2,3},{4,5},{5,6},{6,7},{8,9},{9,10},{10,11},{12,13},{... | collective-permute-start | bytes 6920 | tf_op jit(solution)/shard_map/ppermute | solution.py:23
  66.0 5.8 %collective-permute-start.8 = (f32[1,8,1,128]{3,2,1,0:T(1,128)S(1)}, f32[1,8,1,128]{3,2,1,0:T(1,128)S(1)}, u32[]{:S(2)}, u32[]{:S(2)}) collective-permute-start(f32[1,8,1,128]{3,2,1,0:T(1,128)S(1)} %get-tuple-element.345), channel_id=1, source_target_pairs={{0,4},{4,8},{8,12},{12,16},{16,20},{20,24},{24,28},{1,5},{5,9},{9,... | collective-permute-start | bytes 12296 | tf_op jit(solution)/shard_map/ppermute | solution.py:23
  74.4 7.2 %collective-permute-start.10 = (f32[1,8,34,1]{3,2,1,0:T(8,128)S(1)}, f32[1,8,34,1]{3,2,1,0:T(8,128)S(1)}, u32[]{:S(2)}, u32[]{:S(2)}) collective-permute-start(f32[1,8,34,1]{3,2,1,0:T(8,128)S(1)} %get-tuple-element.305), channel_id=1, source_target_pairs={{0,1},{1,2},{2,3},{4,5},{5,6},{6,7},{8,9},{9,10},{10,11},{12,13},{... | collective-permute-start | bytes 3272 | tf_op jit(solution)/shard_map/ppermute | solution.py:23
  84.2 5.8 %collective-permute-start.16 = (f32[1,8,1,128]{3,2,1,0:T(1,128)S(1)}, f32[1,8,1,128]{3,2,1,0:T(1,128)S(1)}, u32[]{:S(2)}, u32[]{:S(2)}) collective-permute-start(f32[1,8,1,128]{3,2,1,0:T(1,128)S(1)} %get-tuple-element.341), channel_id=1, source_target_pairs={{0,4},{4,8},{8,12},{12,16},{16,20},{20,24},{24,28},{1,5},{5,9},{9,... | collective-permute-start | bytes 12296 | tf_op jit(solution)/shard_map/ppermute | solution.py:23
  92.7 7.2 %collective-permute-start.18 = (f32[1,8,34,1]{3,2,1,0:T(8,128)S(1)}, f32[1,8,34,1]{3,2,1,0:T(8,128)S(1)}, u32[]{:S(2)}, u32[]{:S(2)}) collective-permute-start(f32[1,8,34,1]{3,2,1,0:T(8,128)S(1)} %get-tuple-element.303), channel_id=1, source_target_pairs={{0,1},{1,2},{2,3},{4,5},{5,6},{6,7},{8,9},{9,10},{10,11},{12,13},{... | collective-permute-start | bytes 3272 | tf_op jit(solution)/shard_map/ppermute | solution.py:23
  109.2 34.7 %collective-permute-start.25 = (f32[1,8,1,64]{3,2,1,0:T(1,128)S(1)}, f32[1,8,1,64]{3,2,1,0:T(1,128)S(1)}, u32[]{:S(2)}, u32[]{:S(2)}) collective-permute-start(f32[1,8,1,64]{3,2,1,0:T(1,128)S(1)} %get-tuple-element.402), channel_id=1, source_target_pairs={{4,0},{8,4},{12,8},{16,12},{20,16},{24,20},{28,24},{5,1},{9,5},{13... | collective-permute-start | bytes 6152 | tf_op jit(solution)/shard_map/ppermute | solution.py:24
  111.1 32.8 %collective-permute-start.24 = (f32[1,8,1,64]{3,2,1,0:T(1,128)S(1)}, f32[1,8,1,64]{3,2,1,0:T(1,128)S(1)}, u32[]{:S(2)}, u32[]{:S(2)}) collective-permute-start(f32[1,8,1,64]{3,2,1,0:T(1,128)S(1)} %get-tuple-element.401), channel_id=1, source_target_pairs={{0,4},{4,8},{8,12},{12,16},{16,20},{20,24},{24,28},{1,5},{5,9},{9,... | collective-permute-start | bytes 6152 | tf_op jit(solution)/shard_map/ppermute | solution.py:23
  138.2 46.0 %all-to-all-start = ((f32[4,1,10752]{2,1,0:T(1,128)}), f32[4,1,10752]{2,1,0:T(1,128)}, u32[]{:S(2)}, u32[]{:S(2)}) async-start(f32[4,1,10752]{2,1,0:T(1,128)} %reshape.145), calls=%async_computation | async-start | bytes 344064 | tf_op jit(solution)/shard_map/all_to_all | solution.py:118
  147.1 6.2 %collective-permute-start.26 = (f32[1,8,18,1]{3,1,2,0:T(8,128)S(1)}, f32[1,8,18,1]{3,1,2,0:T(8,128)S(1)}, u32[]{:S(2)}, u32[]{:S(2)}) collective-permute-start(f32[1,8,18,1]{3,1,2,0:T(8,128)S(1)} %get-tuple-element.367), channel_id=1, source_target_pairs={{0,1},{1,2},{2,3},{4,5},{5,6},{6,7},{8,9},{9,10},{10,11},{12,13},{... | collective-permute-start | bytes 1736 | tf_op jit(solution)/shard_map/ppermute | solution.py:23
  156.5 5.8 %collective-permute-start.28 = (f32[1,8,1,64]{3,2,1,0:T(1,128)S(1)}, f32[1,8,1,64]{3,2,1,0:T(1,128)S(1)}, u32[]{:S(2)}, u32[]{:S(2)}) collective-permute-start(f32[1,8,1,64]{3,2,1,0:T(1,128)S(1)} %get-tuple-element.397), channel_id=1, source_target_pairs={{0,4},{4,8},{8,12},{12,16},{16,20},{20,24},{24,28},{1,5},{5,9},{9,... | collective-permute-start | bytes 6152 | tf_op jit(solution)/shard_map/ppermute | solution.py:23
  164.9 6.2 %collective-permute-start.30 = (f32[1,8,18,1]{3,1,2,0:T(8,128)S(1)}, f32[1,8,18,1]{3,1,2,0:T(8,128)S(1)}, u32[]{:S(2)}, u32[]{:S(2)}) collective-permute-start(f32[1,8,18,1]{3,1,2,0:T(8,128)S(1)} %get-tuple-element.365), channel_id=1, source_target_pairs={{0,1},{1,2},{2,3},{4,5},{5,6},{6,7},{8,9},{9,10},{10,11},{12,13},{... | collective-permute-start | bytes 1736 | tf_op jit(solution)/shard_map/ppermute | solution.py:23
  184.2 14.5 %all-to-all-start.1 = ((f32[4,1,10752]{2,1,0:T(1,128)}), f32[4,1,10752]{2,1,0:T(1,128)S(1)}, u32[]{:S(2)}, u32[]{:S(2)}) async-start(f32[4,1,10752]{2,1,0:T(1,128)} %reshape.143), calls=%async_computation.1 | async-start | bytes 344064 | tf_op jit(solution)/shard_map/all_to_all | solution.py:118
  212.9 9.6 %all-to-all-start.2 = ((f32[4,1,10752]{2,1,0:T(1,128)}), f32[4,1,10752]{2,1,0:T(1,128)S(1)}, u32[]{:S(2)}, u32[]{:S(2)}) async-start(f32[4,1,10752]{2,1,0:T(1,128)} %reshape.147), calls=%async_computation.2 | async-start | bytes 344064 | tf_op jit(solution)/shard_map/all_to_all | solution.py:122
  258.2 5.8 %collective-permute-start.32 = (f32[1,8,1,64]{3,2,1,0:T(1,128)S(1)}, f32[1,8,1,64]{3,2,1,0:T(1,128)S(1)}, u32[]{:S(2)}, u32[]{:S(2)}) collective-permute-start(f32[1,8,1,64]{3,2,1,0:T(1,128)S(1)} %get-tuple-element.393), channel_id=1, source_target_pairs={{0,4},{4,8},{8,12},{12,16},{16,20},{20,24},{24,28},{1,5},{5,9},{9,... | collective-permute-start | bytes 6152 | tf_op jit(solution)/shard_map/ppermute | solution.py:23
  266.0 6.2 %collective-permute-start.34 = (f32[1,8,18,1]{3,1,2,0:T(8,128)S(1)}, f32[1,8,18,1]{3,1,2,0:T(8,128)S(1)}, u32[]{:S(2)}, u32[]{:S(2)}) collective-permute-start(f32[1,8,18,1]{3,1,2,0:T(8,128)S(1)} %get-tuple-element.363), channel_id=1, source_target_pairs={{0,1},{1,2},{2,3},{4,5},{5,6},{6,7},{8,9},{9,10},{10,11},{12,13},{... | collective-permute-start | bytes 1736 | tf_op jit(solution)/shard_map/ppermute | solution.py:23
  274.5 5.8 %collective-permute-start.36 = (f32[1,8,1,64]{3,2,1,0:T(1,128)S(1)}, f32[1,8,1,64]{3,2,1,0:T(1,128)S(1)}, u32[]{:S(2)}, u32[]{:S(2)}) collective-permute-start(f32[1,8,1,64]{3,2,1,0:T(1,128)S(1)} %get-tuple-element.389), channel_id=1, source_target_pairs={{0,4},{4,8},{8,12},{12,16},{16,20},{20,24},{24,28},{1,5},{5,9},{9,... | collective-permute-start | bytes 6152 | tf_op jit(solution)/shard_map/ppermute | solution.py:23
  284.3 6.2 %collective-permute-start.38 = (f32[1,8,18,1]{3,1,2,0:T(8,128)S(1)}, f32[1,8,18,1]{3,1,2,0:T(8,128)S(1)}, u32[]{:S(2)}, u32[]{:S(2)}) collective-permute-start(f32[1,8,18,1]{3,1,2,0:T(8,128)S(1)} %get-tuple-element.361), channel_id=1, source_target_pairs={{0,1},{1,2},{2,3},{4,5},{5,6},{6,7},{8,9},{9,10},{10,11},{12,13},{... | collective-permute-start | bytes 1736 | tf_op jit(solution)/shard_map/ppermute | solution.py:23
  296.9 5.8 %collective-permute-start.40 = (f32[1,8,1,128]{3,2,1,0:T(1,128)S(1)}, f32[1,8,1,128]{3,2,1,0:T(1,128)S(1)}, u32[]{:S(2)}, u32[]{:S(2)}) collective-permute-start(f32[1,8,1,128]{3,2,1,0:T(1,128)S(1)} %get-tuple-element.337), channel_id=1, source_target_pairs={{0,4},{4,8},{8,12},{12,16},{16,20},{20,24},{24,28},{1,5},{5,9},{9,... | collective-permute-start | bytes 12296 | tf_op jit(solution)/shard_map/ppermute | solution.py:23
  302.9 6.2 %collective-permute-start.43 = (f32[1,8,34,1]{3,2,1,0:T(8,128)S(1)}, f32[1,8,34,1]{3,2,1,0:T(8,128)S(1)}, u32[]{:S(2)}, u32[]{:S(2)}) collective-permute-start(f32[1,8,34,1]{3,2,1,0:T(8,128)S(1)} %get-tuple-element.302), channel_id=1, source_target_pairs={{1,0},{2,1},{3,2},{5,4},{6,5},{7,6},{9,8},{10,9},{11,10},{13,12},{... | collective-permute-start | bytes 3272 | tf_op jit(solution)/shard_map/ppermute | solution.py:24
  306.3 7.2 %collective-permute-start.42 = (f32[1,8,34,1]{3,2,1,0:T(8,128)S(1)}, f32[1,8,34,1]{3,2,1,0:T(8,128)S(1)}, u32[]{:S(2)}, u32[]{:S(2)}) collective-permute-start(f32[1,8,34,1]{3,2,1,0:T(8,128)S(1)} %get-tuple-element.301), channel_id=1, source_target_pairs={{0,1},{1,2},{2,3},{4,5},{5,6},{6,7},{8,9},{9,10},{10,11},{12,13},{... | collective-permute-start | bytes 3272 | tf_op jit(solution)/shard_map/ppermute | solution.py:23
  316.2 5.8 %collective-permute-start.44 = (f32[1,8,1,128]{3,2,1,0:T(1,128)S(1)}, f32[1,8,1,128]{3,2,1,0:T(1,128)S(1)}, u32[]{:S(2)}, u32[]{:S(2)}) collective-permute-start(f32[1,8,1,128]{3,2,1,0:T(1,128)S(1)} %get-tuple-element.333), channel_id=1, source_target_pairs={{0,4},{4,8},{8,12},{12,16},{16,20},{20,24},{24,28},{1,5},{5,9},{9,... | collective-permute-start | bytes 12296 | tf_op jit(solution)/shard_map/ppermute | solution.py:23
  324.3 7.2 %collective-permute-start.46 = (f32[1,8,34,1]{3,2,1,0:T(8,128)S(1)}, f32[1,8,34,1]{3,2,1,0:T(8,128)S(1)}, u32[]{:S(2)}, u32[]{:S(2)}) collective-permute-start(f32[1,8,34,1]{3,2,1,0:T(8,128)S(1)} %get-tuple-element.299), channel_id=1, source_target_pairs={{0,1},{1,2},{2,3},{4,5},{5,6},{6,7},{8,9},{9,10},{10,11},{12,13},{... | collective-permute-start | bytes 3272 | tf_op jit(solution)/shard_map/ppermute | solution.py:23
  334.1 5.8 %collective-permute-start.48 = (f32[1,8,1,128]{3,2,1,0:T(1,128)S(1)}, f32[1,8,1,128]{3,2,1,0:T(1,128)S(1)}, u32[]{:S(2)}, u32[]{:S(2)}) collective-permute-start(f32[1,8,1,128]{3,2,1,0:T(1,128)S(1)} %get-tuple-element.329), channel_id=1, source_target_pairs={{0,4},{4,8},{8,12},{12,16},{16,20},{20,24},{24,28},{1,5},{5,9},{9,... | collective-permute-start | bytes 12296 | tf_op jit(solution)/shard_map/ppermute | solution.py:23
  342.0 7.2 %collective-permute-start.50 = (f32[1,8,34,1]{3,2,1,0:T(8,128)S(1)}, f32[1,8,34,1]{3,2,1,0:T(8,128)S(1)}, u32[]{:S(2)}, u32[]{:S(2)}) collective-permute-start(f32[1,8,34,1]{3,2,1,0:T(8,128)S(1)} %get-tuple-element.297), channel_id=1, source_target_pairs={{0,1},{1,2},{2,3},{4,5},{5,6},{6,7},{8,9},{9,10},{10,11},{12,13},{... | collective-permute-start | bytes 3272 | tf_op jit(solution)/shard_map/ppermute | solution.py:23
  351.9 5.8 %collective-permute-start.52 = (f32[1,8,1,128]{3,2,1,0:T(1,128)S(1)}, f32[1,8,1,128]{3,2,1,0:T(1,128)S(1)}, u32[]{:S(2)}, u32[]{:S(2)}) collective-permute-start(f32[1,8,1,128]{3,2,1,0:T(1,128)S(1)} %get-tuple-element.325), channel_id=1, source_target_pairs={{0,4},{4,8},{8,12},{12,16},{16,20},{20,24},{24,28},{1,5},{5,9},{9,... | collective-permute-start | bytes 12296 | tf_op jit(solution)/shard_map/ppermute | solution.py:23
  359.8 7.2 %collective-permute-start.54 = (f32[1,8,34,1]{3,2,1,0:T(8,128)S(1)}, f32[1,8,34,1]{3,2,1,0:T(8,128)S(1)}, u32[]{:S(2)}, u32[]{:S(2)}) collective-permute-start(f32[1,8,34,1]{3,2,1,0:T(8,128)S(1)} %get-tuple-element.295), channel_id=1, source_target_pairs={{0,1},{1,2},{2,3},{4,5},{5,6},{6,7},{8,9},{9,10},{10,11},{12,13},{... | collective-permute-start | bytes 3272 | tf_op jit(solution)/shard_map/ppermute | solution.py:23
  369.7 5.8 %collective-permute-start.56 = (f32[1,8,1,128]{3,2,1,0:T(1,128)S(1)}, f32[1,8,1,128]{3,2,1,0:T(1,128)S(1)}, u32[]{:S(2)}, u32[]{:S(2)}) collective-permute-start(f32[1,8,1,128]{3,2,1,0:T(1,128)S(1)} %get-tuple-element.321), channel_id=1, source_target_pairs={{0,4},{4,8},{8,12},{12,16},{16,20},{20,24},{24,28},{1,5},{5,9},{9,... | collective-permute-start | bytes 12296 | tf_op jit(solution)/shard_map/ppermute | solution.py:23
  377.6 7.2 %collective-permute-start.58 = (f32[1,8,34,1]{3,2,1,0:T(8,128)S(1)}, f32[1,8,34,1]{3,2,1,0:T(8,128)S(1)}, u32[]{:S(2)}, u32[]{:S(2)}) collective-permute-start(f32[1,8,34,1]{3,2,1,0:T(8,128)S(1)} %get-tuple-element.293), channel_id=1, source_target_pairs={{0,1},{1,2},{2,3},{4,5},{5,6},{6,7},{8,9},{9,10},{10,11},{12,13},{... | collective-permute-start | bytes 3272 | tf_op jit(solution)/shard_map/ppermute | solution.py:23
  402.8 6.2 %collective-permute-start.62 = (f32[1,8,18,1]{3,1,2,0:T(8,128)S(1)}, f32[1,8,18,1]{3,1,2,0:T(8,128)S(1)}, u32[]{:S(2)}, u32[]{:S(2)}) collective-permute-start(f32[1,8,18,1]{3,1,2,0:T(8,128)S(1)} %get-tuple-element.359), channel_id=1, source_target_pairs={{0,1},{1,2},{2,3},{4,5},{5,6},{6,7},{8,9},{9,10},{10,11},{12,13},{... | collective-permute-start | bytes 1736 | tf_op jit(solution)/shard_map/ppermute | solution.py:23
  419.3 6.2 %collective-permute-start.66 = (f32[1,8,18,1]{3,1,2,0:T(8,128)S(1)}, f32[1,8,18,1]{3,1,2,0:T(8,128)S(1)}, u32[]{:S(2)}, u32[]{:S(2)}) collective-permute-start(f32[1,8,18,1]{3,1,2,0:T(8,128)S(1)} %get-tuple-element.357), channel_id=1, source_target_pairs={{0,1},{1,2},{2,3},{4,5},{5,6},{6,7},{8,9},{9,10},{10,11},{12,13},{... | collective-permute-start | bytes 1736 | tf_op jit(solution)/shard_map/ppermute | solution.py:23
  459.2 9.8 %all-to-all-start.4 = ((f32[4,1,10752]{2,1,0:T(1,128)}), f32[4,1,10752]{2,1,0:T(1,128)S(1)}, u32[]{:S(2)}, u32[]{:S(2)}) async-start(f32[4,1,10752]{2,1,0:T(1,128)} %reshape.151), calls=%async_computation.4 | async-start | bytes 344064 | tf_op jit(solution)/shard_map/all_to_all | solution.py:122
  495.0 6.2 %collective-permute-start.70 = (f32[1,8,18,1]{3,1,2,0:T(8,128)S(1)}, f32[1,8,18,1]{3,1,2,0:T(8,128)S(1)}, u32[]{:S(2)}, u32[]{:S(2)}) collective-permute-start(f32[1,8,18,1]{3,1,2,0:T(8,128)S(1)} %get-tuple-element.355), channel_id=1, source_target_pairs={{0,1},{1,2},{2,3},{4,5},{5,6},{6,7},{8,9},{9,10},{10,11},{12,13},{... | collective-permute-start | bytes 1736 | tf_op jit(solution)/shard_map/ppermute | solution.py:23
  513.4 6.2 %collective-permute-start.74 = (f32[1,8,18,1]{3,1,2,0:T(8,128)S(1)}, f32[1,8,18,1]{3,1,2,0:T(8,128)S(1)}, u32[]{:S(2)}, u32[]{:S(2)}) collective-permute-start(f32[1,8,18,1]{3,1,2,0:T(8,128)S(1)} %get-tuple-element.353), channel_id=1, source_target_pairs={{0,1},{1,2},{2,3},{4,5},{5,6},{6,7},{8,9},{9,10},{10,11},{12,13},{... | collective-permute-start | bytes 1736 | tf_op jit(solution)/shard_map/ppermute | solution.py:23
  531.3 7.2 %collective-permute-start.78 = (f32[1,8,34,1]{3,2,1,0:T(8,128)S(1)}, f32[1,8,34,1]{3,2,1,0:T(8,128)S(1)}, u32[]{:S(2)}, u32[]{:S(2)}) collective-permute-start(f32[1,8,34,1]{3,2,1,0:T(8,128)S(1)} %get-tuple-element.291), channel_id=1, source_target_pairs={{0,1},{1,2},{2,3},{4,5},{5,6},{6,7},{8,9},{9,10},{10,11},{12,13},{... | collective-permute-start | bytes 3272 | tf_op jit(solution)/shard_map/ppermute | solution.py:23
  549.3 7.2 %collective-permute-start.82 = (f32[1,8,34,1]{3,2,1,0:T(8,128)S(1)}, f32[1,8,34,1]{3,2,1,0:T(8,128)S(1)}, u32[]{:S(2)}, u32[]{:S(2)}) collective-permute-start(f32[1,8,34,1]{3,2,1,0:T(8,128)S(1)} %get-tuple-element.289), channel_id=1, source_target_pairs={{0,1},{1,2},{2,3},{4,5},{5,6},{6,7},{8,9},{9,10},{10,11},{12,13},{... | collective-permute-start | bytes 3272 | tf_op jit(solution)/shard_map/ppermute | solution.py:23
  (79 other events, 1907.0 us)
where the time goes:
time: 565 us; the launch traced here: 558 us
  starting transfers between devices  200 us (35%)
  waiting for transfers between devices  167 us (30%)
  local copies, waits for them, and re-layouts  76.3 us (14%)
  other arithmetic  47.8 us (8%)
  blocking collectives  46.6 us (8%)
  loops' own time  15.1 us (3%)
    ppermute x42, waiting for transfers between devices, extended(): before = lax.ppermute(last, axis, up)  138 us
    ppermute x42, starting transfers between devices, extended(): after = lax.ppermute(initial, axis, down)  103 us
    ppermute x42, starting transfers between devices, extended(): before = lax.ppermute(last, axis, up)  75.4 us
    all_gather x3, blocking collectives, to_strips(): gathered = lax.all_gather(level_values, 'px', axis=1, tiled=True)  36.4 us
    ppermute x42, waiting for transfers between devices, extended(): after = lax.ppermute(initial, axis, down)  20.2 us
    unnamed x90, local copies, waits for them, and re-layouts  17.2 us
    another operation x2, loops' own time, from_strips(): canvas = lax.fori_loop(0, pieces_count, place_strip, canvas)  15.1 us
  transfers between devices with their start and end apart: 88, of which 57 were waited for; matrix products, arithmetic and copies ran while one was open for 5% of the time, Pallas kernels for 0%

commit v1 on v0

v1 whole, which is shorter than its diff:
```python
import functools

import jax
import jax.numpy as jnp
from jax import lax
from jax.experimental import pallas as pl
from jax.experimental.pallas import tpu as pltpu
from jax.sharding import PartitionSpec as P

CYCLES = 2
COARSE_SWEEPS = 6
relaxation = 0.8
z_coupling = 0.25

HALO = 24
SIDE = 32
PAD = 8
LANES = 128
VMEM = pl.BlockSpec(memory_space=pltpu.VMEM)
SMEM = pl.BlockSpec(memory_space=pltpu.SMEM)
F32 = jnp.float32


def shifted(values, amount, axis):
    return pltpu.roll(values, amount % values.shape[axis], axis)


def lane_of(values):
    return lax.broadcasted_iota(jnp.int32, values.shape, values.ndim - 1)


def rows_loop(low, high, chunk, body):
    chunk = min(chunk, high - low)
    count = -(-(high - low) // chunk)

    def step(index, carry):
        body(jnp.minimum(low + index * chunk, high - chunk), chunk)
        return carry

    lax.fori_loop(0, count, step, 0)


def pair_sum_lanes(values, step):
    first = (lane_of(values) // step) % 2 == 0
    return values + jnp.where(first, shifted(values, -step, 2), shifted(values, step, 2))


def pair_sum_rows(values):
    count = values.shape[0] // 2
    pairs = values.reshape((count, 2) + values.shape[1:])
    return pairs[:, 0] + pairs[:, 1]


W, E, S, N, D, U, BACK, INV = range(8)


def make_coefficients(k_ref, co, low, high, z_factor, step, chunk):
    def body(at, size):
        k = k_ref[pl.ds(at, size)]
        layer = lax.broadcasted_iota(jnp.int32, k.shape, 1)
        west = 0.5 * (k + k_ref[pl.ds(at - 1, size)])
        east = 0.5 * (k + k_ref[pl.ds(at + 1, size)])
        south = 0.5 * (k + shifted(k, step, 2))
        north = 0.5 * (k + shifted(k, -step, 2))
        half = 0.5 * z_factor
        down = jnp.where(layer == 0, 0.0, half * (k + shifted(k, 1, 1)))
        up = jnp.where(layer == k.shape[1] - 1, 0.0, half * (k + shifted(k, -1, 1)))
        diagonal = west + east + south + north + down + up
        inside = k > 0.0
        inverse = jnp.where(inside, relaxation / jnp.where(inside, diagonal, 1.0), 0.0)
        for which, face in zip((W, E, S, N, D, U), (west, east, south, north, down, up)):
            co[which, pl.ds(at, size)] = inverse * face
        co[BACK, pl.ds(at, size)] = (1.0 / relaxation) * diagonal
        co[INV, pl.ds(at, size)] = inverse

    rows_loop(low, high, chunk, body)


def swept(v_ref, co, g_ref, at, size, step):
    here = pl.ds(at, size)
    v = v_ref[here]
    total = g_ref[here] + (1.0 - relaxation) * v
    total = total + co[W, here] * v_ref[pl.ds(at - 1, size)]
    total = total + co[E, here] * v_ref[pl.ds(at + 1, size)]
    total = total + co[S, here] * shifted(v, step, 2)
    total = total + co[N, here] * shifted(v, -step, 2)
    total = total + co[D, here] * shifted(v, 1, 1)
    total = total + co[U, here] * shifted(v, -1, 1)
    return v, total


def sweep(v_ref, out_ref, co, g_ref, low, high, step, chunk):
    def body(at, size):
        out_ref[pl.ds(at, size)] = swept(v_ref, co, g_ref, at, size, step)[1]

    rows_loop(low, high, chunk, body)


def restricted(v_ref, co, g_ref, at, size, step):
    v, new = swept(v_ref, co, g_ref, 2 * at, 2 * size, step)
    left_over = co[BACK, pl.ds(2 * at, 2 * size)] * (new - v)
    return pair_sum_lanes(pair_sum_rows(left_over), step)


def coarse_rows(values):
    own = values[:, :, :LANES]
    left = jnp.concatenate(
        [jnp.concatenate([own[4 * p + g] for g in range(4)], axis=1) for p in range(2)], axis=0
    )
    row = lax.broadcasted_iota(jnp.int32, (4 * LANES, LANES), 0)
    col = lax.broadcasted_iota(jnp.int32, (4 * LANES, LANES), 1)
    place = (row // LANES) * (LANES // 4) + (row % LANES) // 4
    pick = jnp.where((row % 4 == 0) & (col == place), 1.0, 0.0).astype(F32)
    packed = lax.dot_general(
        left, pick, (((1,), (0,)), ((), ())), precision=lax.Precision.HIGHEST, preferred_element_type=F32
    )
    layers = own.shape[1]
    return packed[:layers], packed[layers:]


def assemble_kernel(rows, even_ref, source, coefficient, recv_a, recv_b, ext_s, ext_k, send_a, send_b):
    even_x, even_y = even_ref[0] == 0, even_ref[1] == 0
    layers = ext_s.shape[1]
    for which, (own, ext) in enumerate(((source, ext_s), (coefficient, ext_k))):
        for r in range(HALO):
            pick = pl.ds(which * layers * HALO + r, layers, stride=HALO)
            a, b = recv_a[pick, :], recv_b[pick, :]
            ext[r] = jnp.where(even_x, b, a)
            ext[HALO + rows + r] = jnp.where(even_x, a, b)
        for r in range(rows):
            ext[HALO + r] = own[pl.ds(r, layers, stride=rows), :]
    half = send_a.shape[0]

    def body(at, size):
        parts = [e[pl.ds(at + h * half, size)] for e in (ext_s, ext_k) for h in range(2)]
        group = lane_of(parts[0]) // SIDE
        first, last = parts[0], shifted(parts[0], SIDE, 2)
        for g in range(1, 4):
            first = jnp.where(group == g, shifted(parts[g], g * SIDE, 2), first)
            last = jnp.where(group == g, shifted(parts[g], (g + 1) * SIDE, 2), last)
        send_a[pl.ds(at, size)] = jnp.where(even_y, last, first)
        send_b[pl.ds(at, size)] = jnp.where(even_y, first, last)

    rows_loop(0, half, 8, body)


def descend_kernel(
    rows, even_ref, ext_s, ext_k, recv_a, recv_b, fine_u, fine_g, fine_co, mid_v, mid_g, mid_co, packed, s, k, k1
):
    even_y = even_ref[1] == 0
    total = rows + 2 * HALO
    half = total // 2

    def widen(at, size):
        a, b = recv_a[pl.ds(at, size)], recv_b[pl.ds(at, size)]
        right, left = jnp.where(even_y, a, b), jnp.where(even_y, b, a)
        lane = lane_of(right)
        for which, (ext, wide) in enumerate(((ext_s, s), (ext_k, k))):
            for h in range(2):
                group = 2 * which + h
                beside = jnp.where(
                    lane < SIDE,
                    shifted(right, -group * SIDE, 2),
                    jnp.where(lane >= LANES - SIDE, shifted(left, -(group + 1) * SIDE, 2), 0.0),
                )
                wide[pl.ds(at + h * half, size), :, pl.ds(0, LANES)] = ext[pl.ds(at + h * half, size)]
                wide[pl.ds(at + h * half, size), :, pl.ds(LANES, LANES)] = beside

    rows_loop(0, half, 4, widen)

    def coarser(at, size):
        k1[pl.ds(at, size)] = 0.25 * pair_sum_lanes(pair_sum_rows(k[pl.ds(2 * at, 2 * size)]), 1)

    rows_loop(0, half, 4, coarser)
    h0, h1 = HALO, HALO // 2
    m = rows // 2
    make_coefficients(k, fine_co, h0 - 22, h0 + rows + 22, z_coupling, 1, 2)
    make_coefficients(k1, mid_co, h1 - 10, h1 + m + 10, 4.0 * z_coupling, 2, 2)

    def scale(at, size):
        fine_g[pl.ds(at, size)] = fine_co[INV, pl.ds(at, size)] * s[pl.ds(at, size)]

    rows_loop(h0 - 22, h0 + rows + 22, 8, scale)
    descend(rows, fine_g, fine_u, fine_g, fine_co, mid_v, mid_g, mid_co, 10, packed)
    k2 = 0.25 * pair_sum_lanes(pair_sum_rows(k1[pl.ds(h1, m)]), 2)
    packed[2], packed[3] = coarse_rows(k2)


def descend(rows, fine_first, fine_u, fine_g, fine_co, mid_v, mid_g, mid_co, reach, packed):
    h0, h1 = HALO, HALO // 2
    m = rows // 2
    sweep(fine_first, fine_u, fine_co, fine_g, h0 - 2 * reach - 1, h0 + rows + 2 * reach + 1, 1, 8)

    def down(at, size):
        total = restricted(fine_u, fine_co, fine_g, at, size, 1)
        mid_g[pl.ds(at, size)] = mid_co[INV, pl.ds(at, size)] * total

    rows_loop(h1 - reach, h1 + m + reach, 4, down)
    sweep(mid_g, mid_v, mid_co, mid_g, h1 - reach + 1, h1 + m + reach - 1, 2, 8)
    low = restricted(mid_v, mid_co, mid_g, h1 // 2, m // 2, 2)
    packed[0], packed[1] = coarse_rows(low)


def unpack(gathered, base, target, first, npx, npy, block):
    per = 4
    width = LANES // per

    def body(ix, carry):
        for p in range(block // per):
            for q in range(npy // per):
                parts = [gathered[ix * npy + per * q + j, base + p] for j in range(per)]
                group = lane_of(parts[0]) // width
                for g in range(per):
                    row = shifted(parts[0], -g * width, 1)
                    for j in range(1, per):
                        row = jnp.where(group == j, shifted(parts[j], (j - g) * width, 1), row)
                    target[first + ix * block + per * p + g, :, pl.ds(q * LANES, LANES)] = row
        return carry

    lax.fori_loop(0, npx, body, 0)


def coarse_coefficients(rows2, strips_ref, k2, co, count):
    layers, width = k2.shape[1], k2.shape[2]

    def body(index, start):
        end = start + strips_ref[index]

        def row(r, carry):
            k = k2[r]
            layer = lax.broadcasted_iota(jnp.int32, k.shape, 0)
            lane = lax.broadcasted_iota(jnp.int32, k.shape, 1)
            west = 0.5 * (k + k2[r - 1])
            east = 0.5 * (k + k2[r + 1])
            open_s, open_n = lane > 0, lane < width - 1
            south = 0.5 * (k + jnp.where(open_s, shifted(k, 1, 1), 0.0))
            north = 0.5 * (k + jnp.where(open_n, shifted(k, -1, 1), 0.0))
            half = 0.5 * 16.0 * z_coupling
            down = jnp.where(layer == 0, 0.0, half * (k + shifted(k, 1, 0)))
            up = jnp.where(layer == layers - 1, 0.0, half * (k + shifted(k, -1, 0)))
            diagonal = west + east + south + north + down + up
            inverse = relaxation / diagonal
            co[W, r] = jnp.where(r > start, inverse * west, 0.0)
            co[E, r] = jnp.where(r < end - 1, inverse * east, 0.0)
            co[S, r] = jnp.where(open_s, inverse * south, 0.0)
            co[N, r] = jnp.where(open_n, inverse * north, 0.0)
            co[D, r] = inverse * down
            co[U, r] = inverse * up
            co[BACK, r] = (1.0 / relaxation) * diagonal
            co[INV, r] = inverse
            return carry

        lax.fori_loop(start, end, row, 0)
        return end

    lax.fori_loop(0, count, body, PAD)


def coarse_solve(rows2, strips_ref, count, co, g, a, b):
    zero = jnp.zeros(g.shape[1:], F32)
    for ref in (g, a, b):
        ref[PAD - 1] = zero
        ref[PAD + rows2] = zero
    for r in range(PAD - 1):
        b[r] = zero
        b[PAD + rows2 + 1 + r] = zero
    at = g
    for index in range(COARSE_SWEEPS - 1):
        to = b if index % 2 == 0 else a
        sweep(at, to, co, g, PAD, PAD + rows2, 1, 8)
        at = to

    def left(first, size):
        v, new = swept(b, co, g, first, size, 1)
        a[pl.ds(first, size)] = co[BACK, pl.ds(first, size)] * (new - v)

    rows_loop(PAD, PAD + rows2, 8, left)

    def strip(index, start):
        end = start + strips_ref[index]

        def add(r, sums):
            return sums[0] + a[r], sums[1] + co[BACK, r]

        over, diagonal = lax.fori_loop(start, end, add, (zero, zero))
        over = jnp.sum(jnp.sum(over, axis=1, keepdims=True), axis=0, keepdims=True)
        diagonal = jnp.sum(jnp.sum(diagonal, axis=1, keepdims=True), axis=0, keepdims=True)
        shift = jnp.broadcast_to(over / (relaxation * diagonal), zero.shape)

        def apply(r, carry):
            b[r] = b[r] + shift
            return carry

        lax.fori_loop(start, end, apply, 0)
        return end

    lax.fori_loop(0, count, strip, PAD)


def correct(rows, place_ref, e2, mid_v, target, reach):
    h1, m = HALO // 2, rows // 2
    low = -(-reach // 2)
    block = rows // 4
    width = e2.shape[2]
    span = block + 2 * low
    x_at, y_at = place_ref[2], place_ref[3]
    window = e2[pl.ds(x_at * block + PAD - low, span)]
    row = lax.broadcasted_iota(jnp.int32, (width, 2 * LANES), 0)
    col = lax.broadcasted_iota(jnp.int32, (width, 2 * LANES), 1)
    offset = jnp.where(col >= 2 * LANES - SIDE, col - 2 * LANES, col)
    cell = (offset + LANES) // 4 - LANES // 4 + y_at * (LANES // 4)
    pick = jnp.where((row == cell) & ((col < LANES + SIDE) | (col >= 2 * LANES - SIDE)), 1.0, 0.0).astype(F32)
    spread = lax.dot_general(
        window.reshape(span * window.shape[1], width),
        pick,
        (((1,), (0,)), ((), ())),
        precision=lax.Precision.HIGHEST,
        preferred_element_type=F32,
    ).reshape(span, window.shape[1], 2 * LANES)
    for at in range(h1 - reach, h1 + m + reach):
        target[at] = mid_v[at] + spread[at // 2 - h1 // 2 + low]


def ascend(rows, reach, mid_a, mid_b, mid_co, mid_g, fine_u, fine_t, fine_co, fine_g, last_ref):
    h0, h1 = HALO, HALO // 2
    m = rows // 2
    sweep(mid_a, mid_b, mid_co, mid_g, h1 - reach + 1, h1 + m + reach - 1, 2, 8)
    sweep(mid_b, mid_a, mid_co, mid_g, h1 - reach + 2, h1 + m + reach - 2, 2, 8)
    edge = 2 * (reach - 2) - 1

    def add(at, size):
        fine = fine_u[pl.ds(2 * at, 2 * size)]
        both = fine.reshape((size, 2) + fine.shape[1:]) + mid_a[pl.ds(at, size)][:, None]
        fine_u[pl.ds(2 * at, 2 * size)] = both.reshape(fine.shape)

    for at in range(h1 - reach + 2, h1 + m + reach - 2):
        add(at, 1)
    sweep(fine_u, fine_t, fine_co, fine_g, h0 - edge + 0, h0 + rows + edge, 1, 8)
    sweep(fine_t, last_ref, fine_co, fine_g, h0 - edge + 1, h0 + rows + edge - 1, 1, 8)


def middle_kernel(
    rows, npx, npy, place_ref, strips_ref, gathered, fine_u, fine_g, fine_co, mid_v, mid_g, mid_co,
    fine_out, mid_v_out, mid_g_out, packed, low_co,
    k2, g2, a2, b2, va, vb, fa, fb,
):
    block = rows // 4
    rows2 = npx * block
    count = strips_ref.shape[0]
    k2[PAD - 1] = jnp.zeros(k2.shape[1:], F32)
    k2[PAD + rows2] = jnp.zeros(k2.shape[1:], F32)
    unpack(gathered, 2, k2, PAD, npx, npy, block)
    coarse_coefficients(rows2, strips_ref, k2, low_co, count)
    solve(rows2, strips_ref, count, gathered, g2, a2, b2, low_co, npx, npy, block)
    correct(rows, place_ref, b2, mid_v, va, 9)

    def copy(at, size):
        fa[pl.ds(at, size)] = fine_u[pl.ds(at, size)]

    rows_loop(HALO - 14, HALO + rows + 14, 8, copy)
    ascend(rows, 9, va, vb, mid_co, mid_g, fa, fb, fine_co, fine_g, fa)
    sweep(fa, fb, fine_co, fine_g, HALO - 10, HALO + rows + 10, 1, 8)
    descend(rows, fb, fine_out, fine_g, fine_co, mid_v_out, mid_g_out, mid_co, 4, packed)


def solve(rows2, strips_ref, count, gathered, g2, a2, b2, low_co, npx, npy, block):
    unpack(gathered, 0, g2, PAD, npx, npy, block)

    def scale(at, size):
        g2[pl.ds(at, size)] = g2[pl.ds(at, size)] * low_co[INV, pl.ds(at, size)]

    rows_loop(PAD, PAD + rows2, 8, scale)
    coarse_solve(rows2, strips_ref, count, low_co, g2, a2, b2)


def last_kernel(
    rows, npx, npy, place_ref, strips_ref, gathered, fine_u, fine_g, fine_co, mid_v, mid_g, mid_co, low_co,
    out, g2, a2, b2, va, vb, fa, fb,
):
    block = rows // 4
    rows2 = npx * block
    count = strips_ref.shape[0]
    solve(rows2, strips_ref, count, gathered, g2, a2, b2, low_co, npx, npy, block)
    correct(rows, place_ref, b2, mid_v, va, 3)

    def copy(at, size):
        fa[pl.ds(at, size)] = fine_u[pl.ds(at, size)]

    rows_loop(HALO - 2, HALO + rows + 2, 8, copy)
    ascend(rows, 3, va, vb, mid_co, mid_g, fa, fb, fine_co, fine_g, fa)
    layers = fa.shape[1]
    for r in range(rows):
        out[pl.ds(r, layers, stride=rows), :] = fa[HALO + r, :, pl.ds(0, LANES)]


def neighbour_swaps(axis, send_a, send_b):
    count = lax.axis_size(axis)
    a = [(i, i ^ 1) for i in range(count)]
    b = [(i, ((i + 1) ^ 1) - 1) for i in range(1, count - 1)]
    return lax.ppermute(send_a, axis, a), lax.ppermute(send_b, axis, b)


def arr(*shape):
    return jax.ShapeDtypeStruct(shape, F32)


def shards(source, coefficient, strip_rows):
    npx, npy = lax.axis_size("px"), lax.axis_size("py")
    layers, rows, _ = source.shape
    total, mids = rows + 2 * HALO, (rows + 2 * HALO) // 2
    rows2, width2 = npx * rows // 4, npy * LANES // 4
    px, py = lax.axis_index("px"), lax.axis_index("py")
    place = jnp.stack([px % 2, py % 2, px, py]).astype(jnp.int32)
    even = px % 2 == 0

    def cut(first):
        return jnp.stack(
            [lax.dynamic_slice_in_dim(array, first, HALO, 1) for array in (source, coefficient)]
        )

    send_a = cut(jnp.where(even, rows - HALO, 0))
    send_b = cut(jnp.where(even, 0, rows - HALO))
    recv_a, recv_b = neighbour_swaps("px", send_a, send_b)
    params = pltpu.CompilerParams(vmem_limit_bytes=44 * 1024 * 1024)
    ext_s, ext_k, send_a, send_b = pl.pallas_call(
        functools.partial(assemble_kernel, rows),
        out_shape=(arr(total, layers, LANES),) * 2 + (arr(mids, layers, LANES),) * 2,
        in_specs=[SMEM] + [VMEM] * 4,
        out_specs=(VMEM,) * 4,
        compiler_params=params,
        name="assemble",
    )(
        place,
        source.reshape(layers * rows, LANES),
        coefficient.reshape(layers * rows, LANES),
        recv_a.reshape(2 * layers * HALO, LANES),
        recv_b.reshape(2 * layers * HALO, LANES),
    )
    recv_a, recv_b = neighbour_swaps("py", send_a, send_b)
    fine, mid = arr(total, layers, 2 * LANES), arr(mids, layers, 2 * LANES)
    fine_cos, mid_cos = arr(8, *fine.shape), arr(8, *mid.shape)

    def scratch(*like):
        return [pltpu.VMEM(item.shape, F32) for item in like]

    fine_u, fine_g, fine_co, mid_v, mid_g, mid_co, packed = pl.pallas_call(
        functools.partial(descend_kernel, rows),
        out_shape=(fine, fine, fine_cos, mid, mid, mid_cos, arr(4, layers, LANES)),
        in_specs=[SMEM] + [VMEM] * 4,
        out_specs=(VMEM,) * 7,
        scratch_shapes=scratch(fine, fine, mid),
        compiler_params=params,
        name="descend",
    )(place, ext_s, ext_k, recv_a, recv_b)

    def gather(block):
        every = jnp.broadcast_to(block[None], (npx * npy,) + block.shape)
        return lax.all_to_all(every, ("px", "py"), 0, 0, tiled=True)

    low = arr(rows2 + 2 * PAD, layers, width2)
    low_cos = arr(8, *low.shape)
    fine_u, mid_v, mid_g, packed, low_co = pl.pallas_call(
        functools.partial(middle_kernel, rows, npx, npy),
        out_shape=(fine, mid, mid, arr(2, layers, LANES), low_cos),
        in_specs=[SMEM] * 2 + [VMEM] * 7,
        out_specs=(VMEM,) * 5,
        scratch_shapes=scratch(low, low, low, low, mid, mid, fine, fine),
        compiler_params=params,
        name="middle",
    )(place, strip_rows, gather(packed), fine_u, fine_g, fine_co, mid_v, mid_g, mid_co)
    out = pl.pallas_call(
        functools.partial(last_kernel, rows, npx, npy),
        out_shape=arr(layers * rows, LANES),
        in_specs=[SMEM] * 2 + [VMEM] * 8,
        out_specs=VMEM,
        scratch_shapes=scratch(low, low, low, mid, mid, fine, fine),
        compiler_params=params,
        name="last",
    )(place, strip_rows, gather(packed), fine_u, fine_g, fine_co, mid_v, mid_g, mid_co, low_co)
    return out.reshape(source.shape)


def solution(mesh):
    placed = (P(None, "px", "py"), P(None, "px", "py"), P())
    return jax.shard_map(
        shards, mesh=mesh, in_specs=placed, out_specs=P(None, "px", "py"), check_vma=False
    )
```

time: 565 us -> 104 us (0.18)
  the two profiles are of different devices: /device:TPU:28 before, /device:TPU:0 now
where the time goes in v1:
time: 104 us; the launch traced here: 103 us
  Pallas kernels  48.2 us (46%)
  blocking collectives  44.4 us (43%)
  starting transfers between devices  4.86 us (5%)
  local copies, waits for them, and re-layouts  2.97 us (3%)
  waiting for transfers between devices  2.92 us (3%)
    all_to_all x2, blocking collectives, gather(): return lax.all_to_all(every, ('px', 'py'), 0, 0, tiled=True)  44.4 us
    pallas_call x1, Pallas kernels, shards(): pl.pallas_call(functools.partial(middle_kernel, rows, npx, npy), out_shap...  21.6 us
    pallas_call x1, Pallas kernels, shards(): pl.pallas_call(functools.partial(descend_kernel, rows), out_shape=(fine,...  13.8 us
    pallas_call x1, Pallas kernels, shards(): pl.pallas_call(functools.partial(last_kernel, rows, npx, npy), out_shape=...  11.4 us
    ppermute x4, starting transfers between devices, neighbour_swaps(): return (lax.ppermute(send_a, axis, a), lax.ppermute(send_b, axis, b))  4.86 us
    ppermute x4, waiting for transfers between devices, neighbour_swaps(): return (lax.ppermute(send_a, axis, a), lax.ppermute(send_b, axis, b))  2.92 us
  transfers between devices with their start and end apart: 4, of which 2 were waited for; matrix products, arithmetic and copies ran while one was open for 0% of the time, Pallas kernels for 0%

profile of v1, /device:TPU:0, one launch (start us, length us, event | category | flops | bytes accessed | tf_op | source)
XLA Modules:
  0.0 103.5 jit_solution(4090274067940580533)
XLA Ops:
  0.0 0.0 copy-start.2
  0.0 1.1 %dynamic-slice_bitcast_fusion = (f32[1,8,24,128]{3,2,1,0:T(8,128)S(1)}, f32[1,8,24,128]{3,2,1,0:T(8,128)S(1)}, f32[1,8,24,128]{3,2,1,0:T(8,128)S(1)}, f32[1,8,24,128]{3,2,1,0:T(8,128)S(1)}) fusion(f32[8,32,128]{2,1,0:T(8,128)} %param.4, s32[]{:T(128)S(6)} %select_n.27, s32[]{:T(128)S(6)} %select_n.26, f32[8,32,128]{2,1,0:T(8,128)} %param.3), kind=kLoop, calls=%fused_computation.2 | loop fusion | bytes 786440 | tf_op jit(solution)/shard_map/stack | solution.py:417
  1.1 0.5 collective-permute-start
  1.6 0.7 collective-permute-start.1
  2.3 0.1 pad_add_fusion.even_ref.place_ref
  2.4 0.3 collective-permute-done
  2.7 0.0 collective-permute-done.1
  2.7 0.0 copy-start
  2.7 0.9 copy-done
  3.6 0.0 copy-start.1
  3.6 0.9 copy-done.1
  4.5 1.4 %assemble.1 = (f32[80,8,128]{2,1,0:T(8,128)S(1)}, f32[80,8,128]{2,1,0:T(8,128)S(1)}, f32[40,8,128]{2,1,0:T(8,128)S(1)}, f32[40,8,128]{2,1,0:T(8,128)S(1)}) custom-call(s32[4]{0:T(128)S(1)} %pad_add_fusion.even_ref.place_ref, f32[256,128]{1,0:T(8,128)S(1)} %bitcast.17, f32[256,128]{1,0:T(8,128)S(1)} %bitcast.18, f32[384,128]{1,0:T(8,128)S(1)} %bitcast.19, ...), custom_call_target="tpu_custom_call" | custom-call | tf_op jit(solution)/shard_map/assemble/pallas_call | solution.py:425
  5.9 3.0 %collective-permute-start.2 = (f32[40,8,128]{2,1,0:T(8,128)S(1)}, f32[40,8,128]{2,1,0:T(8,128)S(1)}, u32[]{:S(2)}, u32[]{:S(2)}) collective-permute-start(f32[40,8,128]{2,1,0:T(8,128)S(1)} %get-tuple-element.23), channel_id=1, source_target_pairs={{0,1},{1,0},{2,3},{3,2},{4,5},{5,4},{6,7},{7,6},{8,9},{9,8},{10,11... | collective-permute-start | bytes 491528 | tf_op jit(solution)/shard_map/ppermute | solution.py:400
  8.9 0.7 collective-permute-start.3
  9.6 2.6 %collective-permute-done.2.recv_a = f32[40,8,128]{2,1,0:T(8,128)S(1)} collective-permute-done((f32[40,8,128]{2,1,0:T(8,128)S(1)}, f32[40,8,128]{2,1,0:T(8,128)S(1)}, u32[]{:S(2)}, u32[]{:S(2)}) %collective-permute-start.2) | collective-permute-done | bytes 163872 | tf_op jit(solution)/shard_map/ppermute | solution.py:400
  12.2 0.0 collective-permute-done.3.recv_b
  12.2 13.8 %descend.1 = (f32[80,8,256]{2,1,0:T(8,128)S(1)}, f32[80,8,256]{2,1,0:T(8,128)S(1)}, f32[8,80,8,256]{3,2,1,0:T(8,128)}, f32[40,8,256]{2,1,0:T(8,128)S(1)}, f32[40...) custom-call(s32[4]{0:T(128)S(1)} %pad_add_fusion.even_ref.place_ref, ...), custom_call_target="tpu_custom_call" | custom-call | tf_op jit(solution)/shard_map/descend/pallas_call | solution.py:446
  26.0 30.3 %all_to_all.10.gathered = f32[32,4,8,128]{3,2,1,0:T(8,128)S(1)} all-to-all(f32[32,4,8,128]{3,2,1,0:T(8,128)S(1)} %broadcast_in_dim.4), channel_id=1, replica_groups=mesh['px'=8,'py'=4] {'px','py'}, dimensions={0} | all-to-all | bytes 1048576 | tf_op jit(solution)/shard_map/all_to_all | solution.py:458
  56.3 0.0 copy-done.2
  56.3 21.6 %middle.1 = (f32[80,8,256]{2,1,0:T(8,128)S(1)}, f32[40,8,256]{2,1,0:T(8,128)S(1)}, f32[40,8,256]{2,1,0:T(8,128)S(1)}, f32[2,8,128]{2,1,0:T(8,128)S(1)}, f32[8,80,8,128]{3,2,1,0:T(8,128)S(1)}) custom-call(s32[4]{0:T(128)S(1)} %pad_add_fusion.even_ref.place_ref, s32[4]{0:T(128)S(1)} %copy-done.2, f32[32,4,8,128]{3,2,1,0:T(8,128)S(1)} %all_to_all.10.gathered, ...), custom_call_target="tpu_custom_call" | custom-call | tf_op jit(solution)/shard_map/middle/pallas_call | solution.py:462
  78.0 14.1 %all_to_all.11.gathered = f32[32,2,8,128]{3,2,1,0:T(8,128)S(1)} all-to-all(f32[32,2,8,128]{3,2,1,0:T(8,128)S(1)} %broadcast_in_dim.5), channel_id=1, replica_groups=mesh['px'=8,'py'=4] {'px','py'}, dimensions={0} | all-to-all | bytes 524288 | tf_op jit(solution)/shard_map/all_to_all | solution.py:458
  92.1 11.4 %last.1 = f32[256,128]{1,0:T(8,128)} custom-call(s32[4]{0:T(128)S(1)} %pad_add_fusion.even_ref.place_ref, s32[4]{0:T(128)S(1)} %copy-done.2, f32[32,2,8,128]{3,2,1,0:T(8,128)S(1)} %all_to_all.11.gathered, f32[80,8,256]{2,1,0:T(8,128)S(1)} %get-tuple-element.33.fine_u, f32[80,8,256]{2,1,0:T(8,128)S(1)} %get-tuple-element.27.fine_g, ...), custom_call_target="tpu_custom_call" | custom-call | tf_op jit(solution)/shard_map/last/pallas_call | solution.py:471
  (4 shorter events, 0.1 us)
Async XLA Ops:
  0.0 56.3 %copy-start.2 = (s32[4]{0:T(128)S(1)}, s32[4]{0:T(128)}, u32[]{:S(2)}) copy-start(s32[4]{0:T(128)} %strips_ref.3) | copy-start | bytes 52
  1.1 1.6 %collective-permute-start = (f32[2,8,24,128]{3,2,1,0:T(8,128)S(1)}, f32[2,8,24,128]{3,2,1,0:T(8,128)S(1)}, u32[]{:S(2)}, u32[]{:S(2)}) collective-permute-start(f32[2,8,24,128]{3,2,1,0:T(8,128)S(1)} %pad_maximum_fusion), channel_id=1, source_target_pairs={{0,4},{4,0},{8,12},{12,8},{16,20},{20,16},{24,28},{28,24},{1,5},{5... | collective-permute-start | bytes 589832 | tf_op jit(solution)/shard_map/ppermute | solution.py:400
  1.6 1.1 %collective-permute-start.1 = (f32[2,8,24,128]{3,2,1,0:T(8,128)S(1)}, f32[2,8,24,128]{3,2,1,0:T(8,128)S(1)}, u32[]{:S(2)}, u32[]{:S(2)}) collective-permute-start(f32[2,8,24,128]{3,2,1,0:T(8,128)S(1)} %pad_maximum_fusion.1), channel_id=1, source_target_pairs={{4,8},{8,4},{12,16},{16,12},{20,24},{24,20},{5,9},{9,5},{13,17},{1... | collective-permute-start | bytes 589832 | tf_op jit(solution)/shard_map/ppermute | solution.py:400
  2.7 0.9 copy-start
  3.6 0.9 copy-start.1
  5.9 6.3 %collective-permute-start.2 = (f32[40,8,128]{2,1,0:T(8,128)S(1)}, f32[40,8,128]{2,1,0:T(8,128)S(1)}, u32[]{:S(2)}, u32[]{:S(2)}) collective-permute-start(f32[40,8,128]{2,1,0:T(8,128)S(1)} %get-tuple-element.23), channel_id=1, source_target_pairs={{0,1},{1,0},{2,3},{3,2},{4,5},{5,4},{6,7},{7,6},{8,9},{9,8},{10,11... | collective-permute-start | bytes 491528 | tf_op jit(solution)/shard_map/ppermute | solution.py:400
  8.9 3.3 %collective-permute-start.3 = (f32[40,8,128]{2,1,0:T(8,128)S(1)}, f32[40,8,128]{2,1,0:T(8,128)S(1)}, u32[]{:S(2)}, u32[]{:S(2)}) collective-permute-start(f32[40,8,128]{2,1,0:T(8,128)S(1)} %get-tuple-element.24), channel_id=1, source_target_pairs={{1,2},{2,1},{5,6},{6,5},{9,10},{10,9},{13,14},{14,13},{17,18},{18,... | collective-permute-start | bytes 491528 | tf_op jit(solution)/shard_map/ppermute | solution.py:400

commit v2 on v0

v2 whole, which is shorter than its diff:
```python
import functools

import jax
import jax.numpy as jnp
from jax import lax
from jax.experimental import pallas as pl
from jax.experimental.pallas import tpu as pltpu
from jax.sharding import PartitionSpec as P

COARSE_SWEEPS = 6
relaxation = 0.8
z_coupling = 0.25

HALO = 24
SIDE = 32
PAD = 8
LANES = 128
HALF = LANES // 2
SLOT = SIDE // 2
VMEM = pl.BlockSpec(memory_space=pltpu.VMEM)
SMEM = pl.BlockSpec(memory_space=pltpu.SMEM)
F32 = jnp.float32


def shifted(values, amount, axis):
    return pltpu.roll(values, amount % values.shape[axis], axis)


def iota_of(values, axis):
    return lax.broadcasted_iota(jnp.int32, values.shape, axis % values.ndim)


def rows_loop(low, high, chunk, body):
    chunk = min(chunk, high - low)
    count = -(-(high - low) // chunk)
    chunk = -(-(high - low) // count)

    def step(index, carry):
        body(jnp.minimum(low + index * chunk, high - chunk), chunk)
        return carry

    if count == 1:
        body(low, chunk)
    else:
        lax.fori_loop(0, count, step, 0)


def pair_sum_rows(values):
    count = values.shape[0] // 2
    pairs = values.reshape((count, 2) + values.shape[1:])
    return pairs[:, 0] + pairs[:, 1]


def pair_sum_lanes(values):
    return values + jnp.where(iota_of(values, -1) % 2 == 0, shifted(values, -1, 2), shifted(values, 1, 2))


def exact_dot(left, right):
    return lax.dot_general(
        left, right, (((1,), (0,)), ((), ())), precision=lax.Precision.HIGHEST, preferred_element_type=F32
    )


def one_hot(shape, place):
    row = lax.broadcasted_iota(jnp.int32, shape, 0)
    col = lax.broadcasted_iota(jnp.int32, shape, 1)
    return jnp.where(place(row, col), 1.0, 0.0).astype(F32)


W, E, S, N, D, U, BACK, INV = range(8)


def weights(k, west, east, south, north, z_factor):
    layer = iota_of(k, -2)
    west, east, south, north = (0.5 * (k + other) for other in (west, east, south, north))
    half = 0.5 * z_factor
    axis = k.ndim - 2
    down = jnp.where(layer == 0, 0.0, half * (k + shifted(k, 1, axis)))
    up = jnp.where(layer == k.shape[axis] - 1, 0.0, half * (k + shifted(k, -1, axis)))
    diagonal = west + east + south + north + down + up
    inside = k > 0.0
    inverse = jnp.where(inside, relaxation / jnp.where(inside, diagonal, 1.0), 0.0)
    scaled = [inverse * face for face in (west, east, south, north, down, up)]
    return scaled + [(1.0 / relaxation) * diagonal, inverse]


def fine_coefficients(k_ref, s_ref, co, g_ref, low, high, chunk):
    def body(at, size):
        here, before, after = pl.ds(at, size), pl.ds(at - 1, size), pl.ds(at + 1, size)
        k = [k_ref[here, s] for s in range(2)]
        sides = ((shifted(k[1], 1, 2), k[1]), (k[0], shifted(k[0], -1, 2)))
        for s in range(2):
            found = weights(k[s], k_ref[before, s], k_ref[after, s], *sides[s], z_coupling)
            for which in range(INV):
                co[which, here, s] = found[which]
            g_ref[here, s] = found[INV] * s_ref[here, s]

    rows_loop(low, high, chunk, body)


def mid_coefficients(k_ref, co, low, high, chunk):
    def body(at, size):
        here = pl.ds(at, size)
        k = k_ref[here]
        found = weights(
            k, k_ref[pl.ds(at - 1, size)], k_ref[pl.ds(at + 1, size)], shifted(k, 1, 2), shifted(k, -1, 2),
            4.0 * z_coupling,
        )
        for which in range(INV + 1):
            co[which, here] = found[which]

    rows_loop(low, high, chunk, body)


def swept_fine(v_ref, co, g_ref, at, size):
    here, before, after = pl.ds(at, size), pl.ds(at - 1, size), pl.ds(at + 1, size)
    v = [v_ref[here, s] for s in range(2)]
    sides = ((shifted(v[1], 1, 2), v[1]), (v[0], shifted(v[0], -1, 2)))
    new = []
    for s in range(2):
        total = g_ref[here, s] + (1.0 - relaxation) * v[s]
        total = total + co[W, here, s] * v_ref[before, s]
        total = total + co[E, here, s] * v_ref[after, s]
        total = total + co[D, here, s] * shifted(v[s], 1, 1)
        total = total + co[U, here, s] * shifted(v[s], -1, 1)
        total = total + co[S, here, s] * sides[s][0]
        total = total + co[N, here, s] * sides[s][1]
        new.append(total)
    return v, new


def swept(v_ref, co, g_ref, at, size):
    here = pl.ds(at, size)
    v = v_ref[here]
    total = g_ref[here] + (1.0 - relaxation) * v
    total = total + co[W, here] * v_ref[pl.ds(at - 1, size)]
    total = total + co[E, here] * v_ref[pl.ds(at + 1, size)]
    total = total + co[D, here] * shifted(v, 1, 1)
    total = total + co[U, here] * shifted(v, -1, 1)
    total = total + co[S, here] * shifted(v, 1, 2)
    total = total + co[N, here] * shifted(v, -1, 2)
    return v, total


def sweep_fine(v_ref, out_ref, co, g_ref, low, high):
    def body(at, size):
        new = swept_fine(v_ref, co, g_ref, at, size)[1]
        for s in range(2):
            out_ref[pl.ds(at, size), s] = new[s]

    rows_loop(low, high, FINE_CHUNK, body)


def sweep(v_ref, out_ref, co, g_ref, low, high):
    def body(at, size):
        out_ref[pl.ds(at, size)] = swept(v_ref, co, g_ref, at, size)[1]

    rows_loop(low, high, CHUNK, body)


FINE_CHUNK = 16
CHUNK = 32


def coarse_rows(values):
    per = LANES // (HALF // 2)
    count = values.shape[0] // per
    left = jnp.concatenate(
        [jnp.concatenate([values[per * p + g] for g in range(per)], axis=1) for p in range(count)], axis=0
    )

    def place(row, col):
        lane = row % LANES
        return (lane < HALF) & (lane % 2 == 0) & (col == (row // LANES) * (HALF // 2) + lane // 2)

    packed = exact_dot(left, one_hot((per * LANES, LANES), place))
    layers = values.shape[1]
    return [packed[p * layers : (p + 1) * layers] for p in range(count)]


def cut_kernel(rows, place_ref, source, coefficient, own, send_a, send_b):
    layers = own.shape[2]
    pick = [pl.ds(r, layers, stride=rows) for r in range(rows)]
    left = jnp.concatenate(
        [jnp.concatenate([source[at, :], coefficient[at, :]], axis=1) for at in pick], axis=0
    )

    def place(row, col):
        y = row % LANES
        return col == (row // LANES) * LANES + (y % 2) * HALF + y // 2

    sorted_y = exact_dot(left, one_hot((2 * LANES, 2 * LANES), place))
    for which in range(2):
        part = sorted_y[:, which * LANES : (which + 1) * LANES]
        own[:, which] = part.reshape(rows, layers, LANES)
    even_x = place_ref[0] == 0
    send_a[...] = own[pl.ds(jnp.where(even_x, rows - HALO, 0), HALO)]
    send_b[...] = own[pl.ds(jnp.where(even_x, 0, rows - HALO), HALO)]


RIGHT_SLOT = (0, 2, 1, 3)
LEFT_SLOT = (3, 5, 4, 6)


def pack_kernel(rows, place_ref, own, recv_a, recv_b, ext, send_a, send_b):
    even_x, even_y = place_ref[0] == 0, place_ref[1] == 0
    half = send_a.shape[0]
    ext[pl.ds(HALO, rows)] = own[...]
    a, b = recv_a[...], recv_b[...]
    ext[pl.ds(0, HALO)] = jnp.where(even_x, b, a)
    ext[pl.ds(HALO + rows, HALO)] = jnp.where(even_x, a, b)

    def body(at, size):
        parts = [ext[pl.ds(at + h * half, size), which] for which in range(2) for h in range(2)]
        slot = (iota_of(parts[0], 2) // SLOT) % 4
        first = last = None
        for g in range(4):
            right = shifted(parts[g], RIGHT_SLOT[g] * SLOT, 2)
            left = shifted(parts[g], (LEFT_SLOT[g] - 3) * SLOT, 2)
            first = right if g == 0 else jnp.where(slot == RIGHT_SLOT[g] % 4, right, first)
            last = left if g == 0 else jnp.where(slot == LEFT_SLOT[g] % 4, left, last)
        send_a[pl.ds(at, size)] = jnp.where(even_y, last, first)
        send_b[pl.ds(at, size)] = jnp.where(even_y, first, last)

    rows_loop(0, half, 8, body)


def descend_kernel(
    rows, place_ref, ext, recv_a, recv_b, fine_u, fine_g, fine_co, mid_v, mid_g, mid_co, packed, s_ref, k_ref, k1
):
    even_y = place_ref[1] == 0
    half = recv_a.shape[0]
    h0, h1, m = HALO, HALO // 2, rows // 2

    def widen(at, size):
        a, b = recv_a[pl.ds(at, size)], recv_b[pl.ds(at, size)]
        right, left = jnp.where(even_y, a, b), jnp.where(even_y, b, a)
        lane = iota_of(right, 2)
        odd_slot = (lane // SLOT) % 2 == 1
        merged = (jnp.where(odd_slot, left, right), jnp.where(odd_slot, right, left))
        for which, wide in enumerate((s_ref, k_ref)):
            for h in range(2):
                here = pl.ds(at + h * half, size)
                slot = RIGHT_SLOT[2 * which + h]
                inner = ext[here, which]
                wide[here, 0] = jnp.where(lane < HALF, inner, shifted(merged[which], HALF - slot * SLOT, 2))
                wide[here, 1] = jnp.where(lane < HALF, shifted(inner, HALF, 2), shifted(merged[which], -slot * SLOT, 2))

    rows_loop(0, half, 8, widen)

    def coarser(at, size):
        here = pl.ds(2 * at, 2 * size)
        k1[pl.ds(at, size)] = 0.25 * pair_sum_rows(k_ref[here, 0] + k_ref[here, 1])

    rows_loop(0, half, 20, coarser)
    fine_coefficients(k_ref, s_ref, fine_co, fine_g, h0 - 22, h0 + rows + 22, 8)
    mid_coefficients(k1, mid_co, h1 - 10, h1 + m + 10, 12)
    descend(rows, fine_g, fine_u, fine_g, fine_co, mid_v, mid_g, mid_co, 10, packed)
    k2 = 0.25 * pair_sum_lanes(pair_sum_rows(k1[pl.ds(h1, m)]))
    packed[2], packed[3] = coarse_rows(k2)


def descend(rows, fine_first, fine_u, fine_g, fine_co, mid_v, mid_g, mid_co, reach, packed):
    h0, h1, m = HALO, HALO // 2, rows // 2
    sweep_fine(fine_first, fine_u, fine_co, fine_g, h0 - 2 * reach - 1, h0 + rows + 2 * reach + 1)

    def down(at, size):
        v, new = swept_fine(fine_u, fine_co, fine_g, 2 * at, 2 * size)
        here = pl.ds(2 * at, 2 * size)
        left = fine_co[BACK, here, 0] * (new[0] - v[0]) + fine_co[BACK, here, 1] * (new[1] - v[1])
        mid_g[pl.ds(at, size)] = mid_co[INV, pl.ds(at, size)] * pair_sum_rows(left)

    rows_loop(h1 - reach, h1 + m + reach, FINE_CHUNK // 2, down)
    sweep(mid_g, mid_v, mid_co, mid_g, h1 - reach + 1, h1 + m + reach - 1)
    v, new = swept(mid_v, mid_co, mid_g, h1, m)
    left = mid_co[BACK, pl.ds(h1, m)] * (new - v)
    packed[0], packed[1] = coarse_rows(pair_sum_lanes(pair_sum_rows(left)))


def unpack(gathered, base, target, scale, npx, npy, block):
    per = 4
    width = LANES // per
    group_of = 4 if npx % 4 == 0 else 1

    def body(step, carry):
        for i in range(group_of):
            ix = step * group_of + i
            for p in range(block // per):
                for q in range(npy // per):
                    parts = [gathered[ix * npy + per * q + j, base + p] for j in range(per)]
                    group = iota_of(parts[0], 1) // width
                    for g in range(per):
                        row = shifted(parts[0], -g * width, 1)
                        for j in range(1, per):
                            row = jnp.where(group == j, shifted(parts[j], (j - g) * width, 1), row)
                        at = PAD + ix * block + per * p + g
                        lanes = pl.ds(q * LANES, LANES)
                        if scale is not None:
                            row = row * scale[INV, at, :, lanes]
                        target[at, :, lanes] = row
        return carry

    lax.fori_loop(0, npx // group_of, body, 0)


def coarse_coefficients(rows2, strips_ref, k2, co, sums):
    width = k2.shape[2]

    def body(at, size):
        k = k2[pl.ds(at, size)]
        lane = iota_of(k, 2)
        open_s, open_n = lane > 0, lane < width - 1
        found = weights(
            k, k2[pl.ds(at - 1, size)], k2[pl.ds(at + 1, size)],
            jnp.where(open_s, shifted(k, 1, 2), 0.0), jnp.where(open_n, shifted(k, -1, 2), 0.0), 16.0 * z_coupling,
        )
        found[S] = jnp.where(open_s, found[S], 0.0)
        found[N] = jnp.where(open_n, found[N], 0.0)
        for which in range(INV + 1):
            co[which, pl.ds(at, size)] = found[which]

    rows_loop(PAD, PAD + rows2, 16, body)
    zero = jnp.zeros(k2.shape[1:], F32)

    def strip(index, start):
        end = start + strips_ref[index]
        co[W, start] = zero
        co[E, end - 1] = zero
        sums[index] = lax.fori_loop(start, end, lambda r, total: total + co[BACK, r], zero)
        return end

    lax.fori_loop(0, strips_ref.shape[0], strip, PAD)
    total = jnp.sum(jnp.sum(sums[...], axis=2, keepdims=True), axis=1, keepdims=True)
    sums[...] = jnp.broadcast_to(relaxation * total, sums.shape)


def coarse_solve(rows, rows2, place_ref, strips_ref, co, sums, g, a, b, over, reach):
    zero = jnp.zeros(g.shape[1:], F32)
    for ref in (g, a, b):
        ref[PAD - 1] = zero
        ref[PAD + rows2] = zero
    for r in range(PAD - 1):
        b[r] = zero
        b[PAD + rows2 + 1 + r] = zero
    at = g
    for index in range(COARSE_SWEEPS - 1):
        to = b if index % 2 == 0 else a
        sweep(at, to, co, g, PAD, PAD + rows2)
        at = to

    def left(first, size):
        v, new = swept(b, co, g, first, size)
        a[pl.ds(first, size)] = co[BACK, pl.ds(first, size)] * (new - v)

    rows_loop(PAD, PAD + rows2, CHUNK, left)
    count = strips_ref.shape[0]

    def strip(index, start):
        end = start + strips_ref[index]
        over[index] = lax.fori_loop(start, end, lambda r, total: total + a[r], zero)
        return end

    lax.fori_loop(0, count, strip, PAD)
    total = jnp.sum(jnp.sum(over[...], axis=2, keepdims=True), axis=1, keepdims=True)
    over[...] = total / sums[...]
    block = rows // 4
    first = PAD + place_ref[2] * block - reach
    final = first + block + 2 * reach

    def shift(index, start):
        end = start + strips_ref[index]
        amount = over[index]

        def row(r, carry):
            b[r] = b[r] + amount
            return carry

        lax.fori_loop(jnp.maximum(start, first), jnp.minimum(end, final), row, 0)
        return end

    lax.fori_loop(0, count, shift, PAD)


def correct(rows, place_ref, e2, mid_v, target, reach):
    h1, m = HALO // 2, rows // 2
    low = -(-reach // 2)
    block = rows // 4
    layers, width = e2.shape[1:]
    span = block + 2 * low
    window = e2[pl.ds(place_ref[2] * block + PAD - low, span)]
    first = place_ref[3] * (HALF // 2)

    def place(row, col):
        from_own = jnp.where(col >= LANES - SLOT, col - LANES, col)
        used = (col < HALF + SLOT) | (col >= LANES - SLOT)
        return used & (row == (from_own + LANES) // 2 - HALF + first)

    spread = exact_dot(window.reshape(span * layers, width), one_hot((width, LANES), place))
    spread = spread.reshape(span, layers, LANES)
    wide = jnp.broadcast_to(spread[:, None], (span, 2, layers, LANES)).reshape(2 * span, layers, LANES)
    start = (h1 - reach) - 2 * (h1 // 2 - low)
    here = pl.ds(h1 - reach, m + 2 * reach)
    target[here] = mid_v[here] + wide[start : start + m + 2 * reach]


def ascend(rows, reach, fine_reach, mid_a, mid_b, mid_co, mid_g, fine_u, fine_a, fine_b, fine_co, fine_g):
    h0, h1, m = HALO, HALO // 2, rows // 2
    sweep(mid_a, mid_b, mid_co, mid_g, h1 - reach + 1, h1 + m + reach - 1)
    sweep(mid_b, mid_a, mid_co, mid_g, h1 - reach + 2, h1 + m + reach - 2)

    def add(at, size):
        fine = fine_u[pl.ds(2 * at, 2 * size)]
        both = fine.reshape((size, 2) + fine.shape[1:]) + mid_a[pl.ds(at, size)][:, None, None]
        fine_a[pl.ds(2 * at, 2 * size)] = both.reshape(fine.shape)

    rows_loop(h1 - reach + 2, h1 + m + reach - 2, 10, add)
    sweep_fine(fine_a, fine_b, fine_co, fine_g, h0 - fine_reach - 1, h0 + rows + fine_reach + 1)
    sweep_fine(fine_b, fine_a, fine_co, fine_g, h0 - fine_reach, h0 + rows + fine_reach)


def middle_kernel(
    rows, npx, npy, place_ref, strips_ref, gathered, fine_u, fine_g, fine_co, mid_v, mid_g, mid_co,
    fine_out, mid_v_out, mid_g_out, packed, low_co, sums,
    k2, g2, a2, b2, over, va, vb, fa, fb,
):
    block = rows // 4
    rows2 = npx * block
    zero = jnp.zeros(k2.shape[1:], F32)
    k2[PAD - 1] = zero
    k2[PAD + rows2] = zero
    unpack(gathered, 2, k2, None, npx, npy, block)
    coarse_coefficients(rows2, strips_ref, k2, low_co, sums)
    unpack(gathered, 0, g2, low_co, npx, npy, block)
    coarse_solve(rows, rows2, place_ref, strips_ref, low_co, sums, g2, a2, b2, over, 5)
    correct(rows, place_ref, b2, mid_v, va, 9)
    ascend(rows, 9, 11, va, vb, mid_co, mid_g, fine_u, fa, fb, fine_co, fine_g)
    sweep_fine(fa, fb, fine_co, fine_g, HALO - 10, HALO + rows + 10)
    descend(rows, fb, fine_out, fine_g, fine_co, mid_v_out, mid_g_out, mid_co, 4, packed)


def last_kernel(
    rows, npx, npy, place_ref, strips_ref, gathered, fine_u, fine_g, fine_co, mid_v, mid_g, mid_co, low_co, sums,
    out, g2, a2, b2, over, va, vb, fa, fb,
):
    block = rows // 4
    rows2 = npx * block
    unpack(gathered, 0, g2, low_co, npx, npy, block)
    coarse_solve(rows, rows2, place_ref, strips_ref, low_co, sums, g2, a2, b2, over, 2)
    correct(rows, place_ref, b2, mid_v, va, 3)
    ascend(rows, 3, 0, va, vb, mid_co, mid_g, fine_u, fa, fb, fine_co, fine_g)
    layers = fa.shape[2]
    here = pl.ds(HALO, rows)
    even, odd = fa[here, 0], fa[here, 1]
    both = jnp.where(iota_of(even, 2) < HALF, even, shifted(odd, HALF, 2))

    def place(row, col):
        return col == 2 * (row % HALF) + row // HALF

    natural = exact_dot(both.reshape(rows * layers, LANES), one_hot((LANES, LANES), place))
    for r in range(rows):
        out[pl.ds(r, layers, stride=rows), :] = natural[r * layers : (r + 1) * layers]


def neighbour_swaps(axis, send_a, send_b):
    count = lax.axis_size(axis)
    a = [(i, i ^ 1) for i in range(count)]
    b = [(i, ((i + 1) ^ 1) - 1) for i in range(1, count - 1)]
    return lax.ppermute(send_a, axis, a), lax.ppermute(send_b, axis, b)


def arr(*shape):
    return jax.ShapeDtypeStruct(shape, F32)


def shards(source, coefficient, strip_rows):
    npx, npy = lax.axis_size("px"), lax.axis_size("py")
    layers, rows, _ = source.shape
    total, mids = rows + 2 * HALO, (rows + 2 * HALO) // 2
    rows2, width2 = npx * rows // 4, npy * LANES // 4
    px, py = lax.axis_index("px"), lax.axis_index("py")
    place = jnp.stack([px % 2, py % 2, px, py]).astype(jnp.int32)
    fine, mid = arr(total, 2, layers, LANES), arr(mids, layers, LANES)
    low, strip_sums = arr(rows2 + 2 * PAD, layers, width2), arr(strip_rows.shape[0], layers, width2)
    fine_cos, mid_cos, low_cos = (arr(n, *item.shape) for n, item in ((7, fine), (8, mid), (8, low)))
    halo = arr(HALO, 2, layers, LANES)
    columns = arr(mids, layers, LANES)
    room = min(48, 12 + 24 * rows2 * layers * width2 * 4 // 2**20)

    def call(body, name, smem, vmem, out_shape, scratch):
        return pl.pallas_call(
            functools.partial(body, rows),
            out_shape=out_shape,
            in_specs=[SMEM] * smem + [VMEM] * vmem,
            out_specs=jax.tree.map(lambda _: VMEM, out_shape),
            scratch_shapes=[pltpu.VMEM(item.shape, F32) for item in scratch],
            compiler_params=pltpu.CompilerParams(vmem_limit_bytes=room * 2**20),
            name=name,
        )

    own, send_a, send_b = call(cut_kernel, "cut", 1, 2, (arr(rows, 2, layers, LANES), halo, halo), ())(
        place, source.reshape(layers * rows, LANES), coefficient.reshape(layers * rows, LANES)
    )
    recv_a, recv_b = neighbour_swaps("px", send_a, send_b)
    ext, send_a, send_b = call(pack_kernel, "pack", 1, 3, (arr(total, 2, layers, LANES), columns, columns), ())(
        place, own, recv_a, recv_b
    )
    recv_a, recv_b = neighbour_swaps("py", send_a, send_b)
    fine_u, fine_g, fine_co, mid_v, mid_g, mid_co, packed = call(
        descend_kernel, "descend", 1, 3, (fine, fine, fine_cos, mid, mid, mid_cos, arr(4, layers, LANES)),
        (fine, fine, mid),
    )(place, ext, recv_a, recv_b)

    def gather(block):
        every = jnp.broadcast_to(block[None], (npx * npy,) + block.shape)
        return lax.all_to_all(every, ("px", "py"), 0, 0, tiled=True)

    def sized(body):
        return lambda rows, *refs: body(rows, npx, npy, *refs)

    fine_u, mid_v, mid_g, packed, low_co, sums = call(
        sized(middle_kernel), "middle", 2, 7, (fine, mid, mid, arr(2, layers, LANES), low_cos, strip_sums),
        (low, low, low, low, strip_sums, mid, mid, fine, fine),
    )(place, strip_rows, gather(packed), fine_u, fine_g, fine_co, mid_v, mid_g, mid_co)
    out = call(
        sized(last_kernel), "last", 2, 9, arr(layers * rows, LANES),
        (low, low, low, strip_sums, mid, mid, fine, fine),
    )(place, strip_rows, gather(packed), fine_u, fine_g, fine_co, mid_v, mid_g, mid_co, low_co, sums)
    return out.reshape(source.shape)


def solution(mesh):
    placed = (P(None, "px", "py"), P(None, "px", "py"), P())
    return jax.shard_map(
        shards, mesh=mesh, in_specs=placed, out_specs=P(None, "px", "py"), check_vma=False
    )
```

time: 565 us -> 74.7 us (0.13)
  the two profiles are of different devices: /device:TPU:28 before, /device:TPU:0 now
where the time goes in v2:
time: 74.7 us; the launch traced here: 74.5 us
  blocking collectives  44.4 us (59%)
  Pallas kernels  20.2 us (27%)
  starting transfers between devices  4.85 us (6%)
  waiting for transfers between devices  3.04 us (4%)
  local copies, waits for them, and re-layouts  1.9 us (3%)
    all_to_all x2, blocking collectives, gather(): return lax.all_to_all(every, ('px', 'py'), 0, 0, tiled=True)  44.4 us
    pallas_call x1, Pallas kernels, shards(): call(sized(middle_kernel), 'middle', 2, 7, (fine, mid, mid, arr(2, layers...  7.81 us
    pallas_call x1, Pallas kernels, shards(): call(sized(last_kernel), 'last', 2, 9, arr(layers * rows, LANES), (low, l...  5.17 us
    pallas_call x1, Pallas kernels, shards(): call(descend_kernel, 'descend', 1, 3, (fine, fine, fine_cos, mid, mid, mi...  5.04 us
    ppermute x4, starting transfers between devices, neighbour_swaps(): return (lax.ppermute(send_a, axis, a), lax.ppermute(send_b, axis, b))  4.85 us
    ppermute x4, waiting for transfers between devices, neighbour_swaps(): return (lax.ppermute(send_a, axis, a), lax.ppermute(send_b, axis, b))  3.04 us
    unnamed x6, local copies, waits for them, and re-layouts  1.81 us
  transfers between devices with their start and end apart: 4, of which 2 were waited for; matrix products, arithmetic and copies ran while one was open for 0% of the time, Pallas kernels for 0%

profile of v2, /device:TPU:0, one launch (start us, length us, event | category | flops | bytes accessed | tf_op | source)
XLA Modules:
  0.0 74.5 jit_solution(11652238636948948957)
XLA Ops:
  0.0 0.0 copy-start.2
  0.0 0.1 pad_add_fusion.place_ref.refs_0_
  0.1 0.0 copy-start
  0.1 0.9 %copy-done = f32[8,32,128]{2,1,0:T(8,128)S(1)} copy-done((f32[8,32,128]{2,1,0:T(8,128)S(1)}, f32[8,32,128]{2,1,0:T(8,128)}, u32[]{:S(2)}) %copy-start) | copy-done | bytes 131096
  1.0 0.0 copy-start.1
  1.0 0.9 %copy-done.1 = f32[8,32,128]{2,1,0:T(8,128)S(1)} copy-done((f32[8,32,128]{2,1,0:T(8,128)S(1)}, f32[8,32,128]{2,1,0:T(8,128)}, u32[]{:S(2)}) %copy-start.1) | copy-done | bytes 131096
  1.9 1.1 %cut.1 = (f32[32,2,8,128]{3,2,1,0:T(8,128)S(1)}, f32[24,2,8,128]{3,2,1,0:T(8,128)S(1)}, f32[24,2,8,128]{3,2,1,0:T(8,128)S(1)}) custom-call(s32[4]{0:T(128)S(1)} %pad_add_fusion.place_ref.refs_0_, f32[256,128]{1,0:T(8,128)S(1)} %bitcast.7, f32[256,128]{1,0:T(8,128)S(1)} %bitcast.8), custom_call_target="tpu_custom_call" | custom-call | tf_op jit(solution)/shard_map/cut/pallas_call | solution.py:500
  3.0 0.5 collective-permute-start
  3.5 0.7 collective-permute-start.1
  4.2 0.4 collective-permute-done.recv_a
  4.6 0.0 collective-permute-done.1.recv_b
  4.6 1.1 %pack.1 = (f32[80,2,8,128]{3,2,1,0:T(8,128)S(1)}, f32[40,8,128]{2,1,0:T(8,128)S(1)}, f32[40,8,128]{2,1,0:T(8,128)S(1)}) custom-call(s32[4]{0:T(128)S(1)} %pad_add_fusion.place_ref.refs_0_, f32[32,2,8,128]{3,2,1,0:T(8,128)S(1)} %get-tuple-element.24.own, f32[24,2,8,128]{3,2,1,0:T(8,128)S(1)} %collective-permute-done.recv_a, ...), custom_call_target="tpu_custom_call" | custom-call | tf_op jit(solution)/shard_map/pack/pallas_call | solution.py:504
  5.7 3.0 %collective-permute-start.2 = (f32[40,8,128]{2,1,0:T(8,128)S(1)}, f32[40,8,128]{2,1,0:T(8,128)S(1)}, u32[]{:S(2)}, u32[]{:S(2)}) collective-permute-start(f32[40,8,128]{2,1,0:T(8,128)S(1)} %get-tuple-element.28), channel_id=1, source_target_pairs={{0,1},{1,0},{2,3},{3,2},{4,5},{5,4},{6,7},{7,6},{8,9},{9,8},{10,11... | collective-permute-start | bytes 491528 | tf_op jit(solution)/shard_map/ppermute | solution.py:468
  8.7 0.7 collective-permute-start.3
  9.4 2.6 %collective-permute-done.2.recv_a = f32[40,8,128]{2,1,0:T(8,128)S(1)} collective-permute-done((f32[40,8,128]{2,1,0:T(8,128)S(1)}, f32[40,8,128]{2,1,0:T(8,128)S(1)}, u32[]{:S(2)}, u32[]{:S(2)}) %collective-permute-start.2) | collective-permute-done | bytes 163872 | tf_op jit(solution)/shard_map/ppermute | solution.py:468
  12.0 0.0 collective-permute-done.3.recv_b
  12.0 5.0 %descend.1 = (f32[80,2,8,128]{3,2,1,0:T(8,128)S(1)}, f32[80,2,8,128]{3,2,1,0:T(8,128)S(1)}, f32[7,80,2,8,128]{4,3,2,1,0:T(8,128)S(1)}, f32[40,8,128]{2,1,0:T(8,1...) custom-call(s32[4]{0:T(128)S(1)} %pad_add_fusion.place_ref.refs_0_, ...), custom_call_target="tpu_custom_call" | custom-call | tf_op jit(solution)/shard_map/descend/pallas_call | solution.py:508
  17.0 0.1 broadcast_in_dim.4
  17.1 30.3 %all_to_all.10.refs_2_ = f32[32,4,8,128]{3,2,1,0:T(8,128)S(1)} all-to-all(f32[32,4,8,128]{3,2,1,0:T(8,128)S(1)} %broadcast_in_dim.4), channel_id=1, replica_groups=mesh['px'=8,'py'=4] {'px','py'}, dimensions={0} | all-to-all | bytes 1048576 | tf_op jit(solution)/shard_map/all_to_all | solution.py:515
  47.4 0.0 copy-done.2
  47.4 7.8 %middle.1 = (f32[80,2,8,128]{3,2,1,0:T(8,128)S(1)}, f32[40,8,128]{2,1,0:T(8,128)S(1)}, f32[40,8,128]{2,1,0:T(8,128)S(1)}, f32[2,8,128]{2,1,0:T(8,128)S(1)}, f32[...) custom-call(s32[4]{0:T(128)S(1)} %pad_add_fusion.place_ref.refs_0_, s32[4]{0:T(128)S(1)} %copy-done.2, ...), custom_call_target="tpu_custom_call" | custom-call | tf_op jit(solution)/shard_map/middle/pallas_call | solution.py:520
  55.2 14.1 %all_to_all.11.refs_2_ = f32[32,2,8,128]{3,2,1,0:T(8,128)S(1)} all-to-all(f32[32,2,8,128]{3,2,1,0:T(8,128)S(1)} %broadcast_in_dim.5), channel_id=1, replica_groups=mesh['px'=8,'py'=4] {'px','py'}, dimensions={0} | all-to-all | bytes 524288 | tf_op jit(solution)/shard_map/all_to_all | solution.py:515
  69.3 5.2 %last.1 = f32[256,128]{1,0:T(8,128)} custom-call(s32[4]{0:T(128)S(1)} %pad_add_fusion.place_ref.refs_0_, s32[4]{0:T(128)S(1)} %copy-done.2, f32[32,2,8,128]{3,2,1,0:T(8,128)S(1)} %all_to_all.11.refs_2_, f32[80,2,8,128]{3,2,1,0:T(8,128)S(1)} %get-tuple-element.38.refs_3_, f32[80,2,8,128]{3,2,1,0:T(8,128)S(1)} %get-tuple-element.32.refs_4_, ...), custom_call_target="tpu_custom_call" | custom-call | tf_op jit(solution)/shard_map/last/pallas_call | solution.py:524
  (1 shorter events, 0.0 us)
Async XLA Ops:
  0.0 47.4 %copy-start.2 = (s32[4]{0:T(128)S(1)}, s32[4]{0:T(128)}, u32[]{:S(2)}) copy-start(s32[4]{0:T(128)} %refs_1_.3) | copy-start | bytes 52
  0.1 0.9 %copy-start = (f32[8,32,128]{2,1,0:T(8,128)S(1)}, f32[8,32,128]{2,1,0:T(8,128)}, u32[]{:S(2)}) copy-start(f32[8,32,128]{2,1,0:T(8,128)} %param.3) | copy-start | bytes 393220
  1.0 0.9 %copy-start.1 = (f32[8,32,128]{2,1,0:T(8,128)S(1)}, f32[8,32,128]{2,1,0:T(8,128)}, u32[]{:S(2)}) copy-start(f32[8,32,128]{2,1,0:T(8,128)} %param.4) | copy-start | bytes 393220
  3.0 1.6 %collective-permute-start = (f32[24,2,8,128]{3,2,1,0:T(8,128)S(1)}, f32[24,2,8,128]{3,2,1,0:T(8,128)S(1)}, u32[]{:S(2)}, u32[]{:S(2)}) collective-permute-start(f32[24,2,8,128]{3,2,1,0:T(8,128)S(1)} %get-tuple-element.25), channel_id=1, source_target_pairs={{0,4},{4,0},{8,12},{12,8},{16,20},{20,16},{24,28},{28,24},{1,5},{5... | collective-permute-start | bytes 589832 | tf_op jit(solution)/shard_map/ppermute | solution.py:468
  3.5 1.1 %collective-permute-start.1 = (f32[24,2,8,128]{3,2,1,0:T(8,128)S(1)}, f32[24,2,8,128]{3,2,1,0:T(8,128)S(1)}, u32[]{:S(2)}, u32[]{:S(2)}) collective-permute-start(f32[24,2,8,128]{3,2,1,0:T(8,128)S(1)} %get-tuple-element.26), channel_id=1, source_target_pairs={{4,8},{8,4},{12,16},{16,12},{20,24},{24,20},{5,9},{9,5},{13,17},{1... | collective-permute-start | bytes 589832 | tf_op jit(solution)/shard_map/ppermute | solution.py:468
  5.7 6.3 %collective-permute-start.2 = (f32[40,8,128]{2,1,0:T(8,128)S(1)}, f32[40,8,128]{2,1,0:T(8,128)S(1)}, u32[]{:S(2)}, u32[]{:S(2)}) collective-permute-start(f32[40,8,128]{2,1,0:T(8,128)S(1)} %get-tuple-element.28), channel_id=1, source_target_pairs={{0,1},{1,0},{2,3},{3,2},{4,5},{5,4},{6,7},{7,6},{8,9},{9,8},{10,11... | collective-permute-start | bytes 491528 | tf_op jit(solution)/shard_map/ppermute | solution.py:468
  8.7 3.3 %collective-permute-start.3 = (f32[40,8,128]{2,1,0:T(8,128)S(1)}, f32[40,8,128]{2,1,0:T(8,128)S(1)}, u32[]{:S(2)}, u32[]{:S(2)}) collective-permute-start(f32[40,8,128]{2,1,0:T(8,128)S(1)} %get-tuple-element.29), channel_id=1, source_target_pairs={{1,2},{2,1},{5,6},{6,5},{9,10},{10,9},{13,14},{14,13},{17,18},{18,... | collective-permute-start | bytes 491528 | tf_op jit(solution)/shard_map/ppermute | solution.py:468

commit v3 on v2

--- a/solution.py
+++ b/solution.py
@@ -178,8 +178,16 @@
     return [packed[p * layers : (p + 1) * layers] for p in range(count)]
 
 
-def cut_kernel(rows, place_ref, source, coefficient, own, send_a, send_b):
+def cut_kernel(rows, place_ref, source_far, coefficient_far, own, send_a, send_b, source, coefficient, arrived):
     layers = own.shape[2]
+    copies = [
+        pltpu.make_async_copy(far, near, arrived.at[i])
+        for i, (far, near) in enumerate(((source_far, source), (coefficient_far, coefficient)))
+    ]
+    for copy in copies:
+        copy.start()
+    for copy in copies:
+        copy.wait()
     pick = [pl.ds(r, layers, stride=rows) for r in range(rows)]
     left = jnp.concatenate(
         [jnp.concatenate([source[at, :], coefficient[at, :]], axis=1) for at in pick], axis=0
@@ -257,7 +265,8 @@
     mid_coefficients(k1, mid_co, h1 - 10, h1 + m + 10, 12)
     descend(rows, fine_g, fine_u, fine_g, fine_co, mid_v, mid_g, mid_co, 10, packed)
     k2 = 0.25 * pair_sum_lanes(pair_sum_rows(k1[pl.ds(h1, m)]))
-    packed[2], packed[3] = coarse_rows(k2)
+    for p, part in enumerate(coarse_rows(k2)):
+        packed[p, 1] = part
 
 
 def descend(rows, fine_first, fine_u, fine_g, fine_co, mid_v, mid_g, mid_co, reach, packed):
@@ -274,10 +283,12 @@
     sweep(mid_g, mid_v, mid_co, mid_g, h1 - reach + 1, h1 + m + reach - 1)
     v, new = swept(mid_v, mid_co, mid_g, h1, m)
     left = mid_co[BACK, pl.ds(h1, m)] * (new - v)
-    packed[0], packed[1] = coarse_rows(pair_sum_lanes(pair_sum_rows(left)))
-
-
-def unpack(gathered, base, target, scale, npx, npy, block):
+    for p, part in enumerate(coarse_rows(pair_sum_lanes(pair_sum_rows(left)))):
+        packed[p, 0] = part
+
+
+def unpack(place_ref, mine, other, which, target, scale, npx, npy, block):
+    even_x = place_ref[0] == 0
     per = 4
     width = LANES // per
     group_of = 4 if npx % 4 == 0 else 1
@@ -287,7 +298,9 @@
             ix = step * group_of + i
             for p in range(block // per):
                 for q in range(npy // per):
-                    parts = [gathered[ix * npy + per * q + j, base + p] for j in range(per)]
+                    devices = [ix * npy + per * q + j for j in range(per)]
+                    here = even_x if p == 0 else jnp.logical_not(even_x)
+                    parts = [jnp.where(here, mine[i, which], other[i, which]) for i in devices]
                     group = iota_of(parts[0], 1) // width
                     for g in range(per):
                         row = shifted(parts[0], -g * width, 1)
@@ -419,7 +432,7 @@
 
 
 def middle_kernel(
-    rows, npx, npy, place_ref, strips_ref, gathered, fine_u, fine_g, fine_co, mid_v, mid_g, mid_co,
+    rows, npx, npy, place_ref, strips_ref, mine, other, fine_u, fine_g, fine_co, mid_v, mid_g, mid_co,
     fine_out, mid_v_out, mid_g_out, packed, low_co, sums,
     k2, g2, a2, b2, over, va, vb, fa, fb,
 ):
@@ -428,9 +441,9 @@
     zero = jnp.zeros(k2.shape[1:], F32)
     k2[PAD - 1] = zero
     k2[PAD + rows2] = zero
-    unpack(gathered, 2, k2, None, npx, npy, block)
+    unpack(place_ref, mine, other, 1, k2, None, npx, npy, block)
     coarse_coefficients(rows2, strips_ref, k2, low_co, sums)
-    unpack(gathered, 0, g2, low_co, npx, npy, block)
+    unpack(place_ref, mine, other, 0, g2, low_co, npx, npy, block)
     coarse_solve(rows, rows2, place_ref, strips_ref, low_co, sums, g2, a2, b2, over, 5)
     correct(rows, place_ref, b2, mid_v, va, 9)
     ascend(rows, 9, 11, va, vb, mid_co, mid_g, fine_u, fa, fb, fine_co, fine_g)
@@ -439,12 +452,12 @@
 
 
 def last_kernel(
-    rows, npx, npy, place_ref, strips_ref, gathered, fine_u, fine_g, fine_co, mid_v, mid_g, mid_co, low_co, sums,
+    rows, npx, npy, place_ref, strips_ref, mine, other, fine_u, fine_g, fine_co, mid_v, mid_g, mid_co, low_co, sums,
     out, g2, a2, b2, over, va, vb, fa, fb,
 ):
     block = rows // 4
     rows2 = npx * block
-    unpack(gathered, 0, g2, low_co, npx, npy, block)
+    unpack(place_ref, mine, other, 0, g2, low_co, npx, npy, block)
     coarse_solve(rows, rows2, place_ref, strips_ref, low_co, sums, g2, a2, b2, over, 2)
     correct(rows, place_ref, b2, mid_v, va, 3)
     ascend(rows, 3, 0, va, vb, mid_co, mid_g, fine_u, fa, fb, fine_co, fine_g)
@@ -486,45 +499,49 @@
     columns = arr(mids, layers, LANES)
     room = min(48, 12 + 24 * rows2 * layers * width2 * 4 // 2**20)
 
-    def call(body, name, smem, vmem, out_shape, scratch):
+    def call(body, name, smem, vmem, out_shape, scratch, where=VMEM, semaphores=()):
         return pl.pallas_call(
             functools.partial(body, rows),
             out_shape=out_shape,
-            in_specs=[SMEM] * smem + [VMEM] * vmem,
+            in_specs=[SMEM] * smem + [where] * vmem,
             out_specs=jax.tree.map(lambda _: VMEM, out_shape),
-            scratch_shapes=[pltpu.VMEM(item.shape, F32) for item in scratch],
+            scratch_shapes=[pltpu.VMEM(item.shape, F32) for item in scratch] + list(semaphores),
             compiler_params=pltpu.CompilerParams(vmem_limit_bytes=room * 2**20),
             name=name,
         )
 
-    own, send_a, send_b = call(cut_kernel, "cut", 1, 2, (arr(rows, 2, layers, LANES), halo, halo), ())(
-        place, source.reshape(layers * rows, LANES), coefficient.reshape(layers * rows, LANES)
-    )
+    flat = arr(layers * rows, LANES)
+    own, send_a, send_b = call(
+        cut_kernel, "cut", 1, 2, (arr(rows, 2, layers, LANES), halo, halo), (flat, flat),
+        pl.BlockSpec(memory_space=pl.ANY), (pltpu.SemaphoreType.DMA((2,)),),
+    )(place, source.reshape(flat.shape), coefficient.reshape(flat.shape))
     recv_a, recv_b = neighbour_swaps("px", send_a, send_b)
     ext, send_a, send_b = call(pack_kernel, "pack", 1, 3, (arr(total, 2, layers, LANES), columns, columns), ())(
         place, own, recv_a, recv_b
     )
     recv_a, recv_b = neighbour_swaps("py", send_a, send_b)
     fine_u, fine_g, fine_co, mid_v, mid_g, mid_co, packed = call(
-        descend_kernel, "descend", 1, 3, (fine, fine, fine_cos, mid, mid, mid_cos, arr(4, layers, LANES)),
+        descend_kernel, "descend", 1, 3, (fine, fine, fine_cos, mid, mid, mid_cos, arr(2, 2, layers, LANES)),
         (fine, fine, mid),
     )(place, ext, recv_a, recv_b)
 
     def gather(block):
-        every = jnp.broadcast_to(block[None], (npx * npy,) + block.shape)
-        return lax.all_to_all(every, ("px", "py"), 0, 0, tiled=True)
+        shape = (npx // 2, 2, npy) + block.shape[1:]
+        every = jnp.broadcast_to(block[None, :, None], shape).reshape((npx * npy,) + block.shape[1:])
+        half = lax.all_to_all(every, ("px", "py"), 0, 0, tiled=True)
+        return half, lax.ppermute(half, "px", [(i, i ^ 1) for i in range(npx)])
 
     def sized(body):
         return lambda rows, *refs: body(rows, npx, npy, *refs)
 
     fine_u, mid_v, mid_g, packed, low_co, sums = call(
-        sized(middle_kernel), "middle", 2, 7, (fine, mid, mid, arr(2, layers, LANES), low_cos, strip_sums),
+        sized(middle_kernel), "middle", 2, 8, (fine, mid, mid, arr(2, 1, layers, LANES), low_cos, strip_sums),
         (low, low, low, low, strip_sums, mid, mid, fine, fine),
-    )(place, strip_rows, gather(packed), fine_u, fine_g, fine_co, mid_v, mid_g, mid_co)
+    )(place, strip_rows, *gather(packed), fine_u, fine_g, fine_co, mid_v, mid_g, mid_co)
     out = call(
-        sized(last_kernel), "last", 2, 9, arr(layers * rows, LANES),
+        sized(last_kernel), "last", 2, 10, arr(layers * rows, LANES),
         (low, low, low, strip_sums, mid, mid, fine, fine),
-    )(place, strip_rows, gather(packed), fine_u, fine_g, fine_co, mid_v, mid_g, mid_co, low_co, sums)
+    )(place, strip_rows, *gather(packed), fine_u, fine_g, fine_co, mid_v, mid_g, mid_co, low_co, sums)
     return out.reshape(source.shape)
 
 

time: 74.7 us -> 70.5 us (0.944)
  blocking collectives: 44.4 us -> 37 us
  waiting for transfers between devices: 3.04 us -> 5.55 us
    all_to_all x2, blocking collectives: 44.4 us -> 37 us  [gather(): half = lax.all_to_all(every, ('px', 'py'), 0, 0, tiled=True)]
    ppermute x0 -> x2, waiting for transfers between devices: none -> 2.51 us  [gather(): return (half, lax.ppermute(half, 'px', [(i, i ^ 1) for i in range(npx)]))]
  transfers between devices with their start and end apart: 4 -> 6, of which waited for: 2 -> 4; matrix products, arithmetic and copies ran while one was open for 0% -> 0% of each run, Pallas kernels for 0% -> 0%
where the time goes in v3:
time: 70.5 us; the launch traced here: 70.3 us
  blocking collectives  37 us (52%)
  Pallas kernels  20.5 us (29%)
  waiting for transfers between devices  5.55 us (8%)
  starting transfers between devices  5.24 us (7%)
  local copies, waits for them, and re-layouts  1.86 us (3%)
    all_to_all x2, blocking collectives, gather(): half = lax.all_to_all(every, ('px', 'py'), 0, 0, tiled=True)  37 us
    pallas_call x1, Pallas kernels, shards(): call(sized(middle_kernel), 'middle', 2, 8, (fine, mid, mid, arr(2, 1, lay...  7.75 us
    pallas_call x1, Pallas kernels, shards(): call(sized(last_kernel), 'last', 2, 10, arr(layers * rows, LANES), (low,...  5.17 us
    pallas_call x1, Pallas kernels, shards(): call(descend_kernel, 'descend', 1, 3, (fine, fine, fine_cos, mid, mid, mi...  5.04 us
    ppermute x4, starting transfers between devices, neighbour_swaps(): return (lax.ppermute(send_a, axis, a), lax.ppermute(send_b, axis, b))  4.85 us
    ppermute x4, waiting for transfers between devices, neighbour_swaps(): return (lax.ppermute(send_a, axis, a), lax.ppermute(send_b, axis, b))  3.04 us
    ppermute x2, waiting for transfers between devices, gather(): return (half, lax.ppermute(half, 'px', [(i, i ^ 1) for i in range(npx)]))  2.51 us
    unnamed x6, local copies, waits for them, and re-layouts  1.81 us
  transfers between devices with their start and end apart: 6, of which 4 were waited for; matrix products, arithmetic and copies ran while one was open for 0% of the time, Pallas kernels for 0%

profile of v3, /device:TPU:0, one launch (start us, length us, event | category | flops | bytes accessed | tf_op | source)
XLA Modules:
  0.0 70.3 jit_solution(1687330632524454129)
XLA Ops:
  0.0 0.0 copy-start.2
  0.0 0.1 pad_add_fusion.place_ref.refs_0_
  0.1 0.0 copy-start
  0.1 0.9 %copy-done = f32[8,32,128]{2,1,0:T(8,128)S(1)} copy-done((f32[8,32,128]{2,1,0:T(8,128)S(1)}, f32[8,32,128]{2,1,0:T(8,128)}, u32[]{:S(2)}) %copy-start) | copy-done | bytes 131096
  1.0 0.0 copy-start.1
  1.0 0.9 %copy-done.1 = f32[8,32,128]{2,1,0:T(8,128)S(1)} copy-done((f32[8,32,128]{2,1,0:T(8,128)S(1)}, f32[8,32,128]{2,1,0:T(8,128)}, u32[]{:S(2)}) %copy-start.1) | copy-done | bytes 131096
  1.9 1.5 %cut.1 = (f32[32,2,8,128]{3,2,1,0:T(8,128)S(1)}, f32[24,2,8,128]{3,2,1,0:T(8,128)S(1)}, f32[24,2,8,128]{3,2,1,0:T(8,128)S(1)}) custom-call(s32[4]{0:T(128)S(1)} %pad_add_fusion.place_ref.refs_0_, f32[256,128]{1,0:T(8,128)S(1)} %bitcast.10, f32[256,128]{1,0:T(8,128)S(1)} %bitcast.11), custom_call_target="tpu_custom_call" | custom-call | tf_op jit(solution)/shard_map/cut/pallas_call | solution.py:514
  3.4 0.5 collective-permute-start
  3.9 0.7 collective-permute-start.1
  4.6 0.4 collective-permute-done.recv_a
  5.0 0.0 collective-permute-done.1.recv_b
  5.0 1.1 %pack.1 = (f32[80,2,8,128]{3,2,1,0:T(8,128)S(1)}, f32[40,8,128]{2,1,0:T(8,128)S(1)}, f32[40,8,128]{2,1,0:T(8,128)S(1)}) custom-call(s32[4]{0:T(128)S(1)} %pad_add_fusion.place_ref.refs_0_, f32[32,2,8,128]{3,2,1,0:T(8,128)S(1)} %get-tuple-element.24.own, f32[24,2,8,128]{3,2,1,0:T(8,128)S(1)} %collective-permute-done.recv_a, ...), custom_call_target="tpu_custom_call" | custom-call | tf_op jit(solution)/shard_map/pack/pallas_call | solution.py:519
  6.0 3.0 %collective-permute-start.2 = (f32[40,8,128]{2,1,0:T(8,128)S(1)}, f32[40,8,128]{2,1,0:T(8,128)S(1)}, u32[]{:S(2)}, u32[]{:S(2)}) collective-permute-start(f32[40,8,128]{2,1,0:T(8,128)S(1)} %get-tuple-element.28), channel_id=1, source_target_pairs={{0,1},{1,0},{2,3},{3,2},{4,5},{5,4},{6,7},{7,6},{8,9},{9,8},{10,11... | collective-permute-start | bytes 491528 | tf_op jit(solution)/shard_map/ppermute | solution.py:481
  9.0 0.7 collective-permute-start.3
  9.7 2.6 %collective-permute-done.2.recv_a = f32[40,8,128]{2,1,0:T(8,128)S(1)} collective-permute-done((f32[40,8,128]{2,1,0:T(8,128)S(1)}, f32[40,8,128]{2,1,0:T(8,128)S(1)}, u32[]{:S(2)}, u32[]{:S(2)}) %collective-permute-start.2) | collective-permute-done | bytes 163872 | tf_op jit(solution)/shard_map/ppermute | solution.py:481
  12.3 0.0 collective-permute-done.3.recv_b
  12.3 5.0 %descend.1 = (f32[80,2,8,128]{3,2,1,0:T(8,128)S(1)}, f32[80,2,8,128]{3,2,1,0:T(8,128)S(1)}, f32[7,80,2,8,128]{4,3,2,1,0:T(8,128)S(1)}, f32[40,8,128]{2,1,0:T(8,1...) custom-call(s32[4]{0:T(128)S(1)} %pad_add_fusion.place_ref.refs_0_, ...), custom_call_target="tpu_custom_call" | custom-call | tf_op jit(solution)/shard_map/descend/pallas_call | solution.py:523
  17.4 26.1 %all_to_all.10.refs_2_ = f32[32,2,8,128]{3,2,1,0:T(8,128)S(1)} all-to-all(f32[32,2,8,128]{3,2,1,0:T(8,128)S(1)} %bitcast.13), channel_id=1, replica_groups=mesh['px'=8,'py'=4] {'px','py'}, dimensions={0} | all-to-all | bytes 524288 | tf_op jit(solution)/shard_map/all_to_all | solution.py:531
  43.5 0.4 collective-permute-start.4
  43.9 1.2 %collective-permute-done.4.refs_3_ = f32[32,2,8,128]{3,2,1,0:T(8,128)S(1)} collective-permute-done((f32[32,2,8,128]{3,2,1,0:T(8,128)S(1)}, f32[32,2,8,128]{3,2,1,0:T(8,128)S(1)}, u32[]{:S(2)}, u32[]{:S(2)}) %collective-permute-start.4) | collective-permute-done | bytes 262176 | tf_op jit(solution)/shard_map/ppermute | solution.py:532
  45.1 0.0 copy-done.2
  45.1 7.8 %middle.1 = (f32[80,2,8,128]{3,2,1,0:T(8,128)S(1)}, f32[40,8,128]{2,1,0:T(8,128)S(1)}, f32[40,8,128]{2,1,0:T(8,128)S(1)}, f32[2,1,8,128]{3,2,1,0:T(8,128)S(1)}, ...) custom-call(s32[4]{0:T(128)S(1)} %pad_add_fusion.place_ref.refs_0_, s32[4]{0:T(128)S(1)} %copy-done.2, ...), custom_call_target="tpu_custom_call" | custom-call | tf_op jit(solution)/shard_map/middle/pallas_call | solution.py:537
  52.8 10.9 %all_to_all.11.refs_2_ = f32[32,1,8,128]{3,2,1,0:T(8,128)S(1)} all-to-all(f32[32,1,8,128]{3,2,1,0:T(8,128)S(1)} %bitcast.14), channel_id=1, replica_groups=mesh['px'=8,'py'=4] {'px','py'}, dimensions={0} | all-to-all | bytes 262144 | tf_op jit(solution)/shard_map/all_to_all | solution.py:531
  63.8 0.0 collective-permute-start.5
  63.8 1.3 %collective-permute-done.5.refs_3_ = f32[32,1,8,128]{3,2,1,0:T(8,128)S(1)} collective-permute-done((f32[32,1,8,128]{3,2,1,0:T(8,128)S(1)}, f32[32,1,8,128]{3,2,1,0:T(8,128)S(1)}, u32[]{:S(2)}, u32[]{:S(2)}) %collective-permute-start.5) | collective-permute-done | bytes 131104 | tf_op jit(solution)/shard_map/ppermute | solution.py:532
  65.1 5.2 %last.1 = f32[256,128]{1,0:T(8,128)} custom-call(s32[4]{0:T(128)S(1)} %pad_add_fusion.place_ref.refs_0_, s32[4]{0:T(128)S(1)} %copy-done.2, f32[32,1,8,128]{3,2,1,0:T(8,128)S(1)} %all_to_all.11.refs_2_, f32[32,1,8,128]{3,2,1,0:T(8,128)S(1)} %collective-permute-done.5.refs_3_, f32[80,2,8,128]{3,2,1,0:T(8,128)S(1)} %get-tuple-element.38.refs_4_, ...), custom_call_target="tpu_custom_call" | custom-call | tf_op jit(solution)/shard_map/last/pallas_call | solution.py:541
  (2 shorter events, 0.0 us)
Async XLA Ops:
  0.0 45.1 %copy-start.2 = (s32[4]{0:T(128)S(1)}, s32[4]{0:T(128)}, u32[]{:S(2)}) copy-start(s32[4]{0:T(128)} %refs_1_.3) | copy-start | bytes 52
  0.1 0.9 %copy-start = (f32[8,32,128]{2,1,0:T(8,128)S(1)}, f32[8,32,128]{2,1,0:T(8,128)}, u32[]{:S(2)}) copy-start(f32[8,32,128]{2,1,0:T(8,128)} %param.3) | copy-start | bytes 393220
  1.0 0.9 %copy-start.1 = (f32[8,32,128]{2,1,0:T(8,128)S(1)}, f32[8,32,128]{2,1,0:T(8,128)}, u32[]{:S(2)}) copy-start(f32[8,32,128]{2,1,0:T(8,128)} %param.4) | copy-start | bytes 393220
  3.4 1.6 %collective-permute-start = (f32[24,2,8,128]{3,2,1,0:T(8,128)S(1)}, f32[24,2,8,128]{3,2,1,0:T(8,128)S(1)}, u32[]{:S(2)}, u32[]{:S(2)}) collective-permute-start(f32[24,2,8,128]{3,2,1,0:T(8,128)S(1)} %get-tuple-element.25), channel_id=1, source_target_pairs={{0,4},{4,0},{8,12},{12,8},{16,20},{20,16},{24,28},{28,24},{1,5},{5... | collective-permute-start | bytes 589832 | tf_op jit(solution)/shard_map/ppermute | solution.py:481
  3.9 1.1 %collective-permute-start.1 = (f32[24,2,8,128]{3,2,1,0:T(8,128)S(1)}, f32[24,2,8,128]{3,2,1,0:T(8,128)S(1)}, u32[]{:S(2)}, u32[]{:S(2)}) collective-permute-start(f32[24,2,8,128]{3,2,1,0:T(8,128)S(1)} %get-tuple-element.26), channel_id=1, source_target_pairs={{4,8},{8,4},{12,16},{16,12},{20,24},{24,20},{5,9},{9,5},{13,17},{1... | collective-permute-start | bytes 589832 | tf_op jit(solution)/shard_map/ppermute | solution.py:481
  6.0 6.3 %collective-permute-start.2 = (f32[40,8,128]{2,1,0:T(8,128)S(1)}, f32[40,8,128]{2,1,0:T(8,128)S(1)}, u32[]{:S(2)}, u32[]{:S(2)}) collective-permute-start(f32[40,8,128]{2,1,0:T(8,128)S(1)} %get-tuple-element.28), channel_id=1, source_target_pairs={{0,1},{1,0},{2,3},{3,2},{4,5},{5,4},{6,7},{7,6},{8,9},{9,8},{10,11... | collective-permute-start | bytes 491528 | tf_op jit(solution)/shard_map/ppermute | solution.py:481
  9.0 3.3 %collective-permute-start.3 = (f32[40,8,128]{2,1,0:T(8,128)S(1)}, f32[40,8,128]{2,1,0:T(8,128)S(1)}, u32[]{:S(2)}, u32[]{:S(2)}) collective-permute-start(f32[40,8,128]{2,1,0:T(8,128)S(1)} %get-tuple-element.29), channel_id=1, source_target_pairs={{1,2},{2,1},{5,6},{6,5},{9,10},{10,9},{13,14},{14,13},{17,18},{18,... | collective-permute-start | bytes 491528 | tf_op jit(solution)/shard_map/ppermute | solution.py:481
  43.5 1.6 %collective-permute-start.4 = (f32[32,2,8,128]{3,2,1,0:T(8,128)S(1)}, f32[32,2,8,128]{3,2,1,0:T(8,128)S(1)}, u32[]{:S(2)}, u32[]{:S(2)}) collective-permute-start(f32[32,2,8,128]{3,2,1,0:T(8,128)S(1)} %all_to_all.10.refs_2_), channel_id=1, source_target_pairs={{0,4},{4,0},{8,12},{12,8},{16,20},{20,16},{24,28},{28,24},{1,5},{5... | collective-permute-start | bytes 786440 | tf_op jit(solution)/shard_map/ppermute | solution.py:532
  63.8 1.3 %collective-permute-start.5 = (f32[32,1,8,128]{3,2,1,0:T(8,128)S(1)}, f32[32,1,8,128]{3,2,1,0:T(8,128)S(1)}, u32[]{:S(2)}, u32[]{:S(2)}) collective-permute-start(f32[32,1,8,128]{3,2,1,0:T(8,128)S(1)} %all_to_all.11.refs_2_), channel_id=1, source_target_pairs={{0,4},{4,0},{8,12},{12,8},{16,20},{20,16},{24,28},{28,24},{1,5},{5... | collective-permute-start | bytes 393224 | tf_op jit(solution)/shard_map/ppermute | solution.py:532

commit v4 on v3

--- a/solution.py
+++ b/solution.py
@@ -158,8 +158,8 @@
     rows_loop(low, high, CHUNK, body)
 
 
-FINE_CHUNK = 16
-CHUNK = 32
+FINE_CHUNK = 20
+CHUNK = 64
 
 
 def coarse_rows(values):
@@ -214,7 +214,7 @@
     even_x, even_y = place_ref[0] == 0, place_ref[1] == 0
     half = send_a.shape[0]
     ext[pl.ds(HALO, rows)] = own[...]
-    a, b = recv_a[...], recv_b[...]
+    a, b = recv_a[...], jnp.where(place_ref[4] != 0, recv_b[...], 0.0)
     ext[pl.ds(0, HALO)] = jnp.where(even_x, b, a)
     ext[pl.ds(HALO + rows, HALO)] = jnp.where(even_x, a, b)
 
@@ -241,7 +241,7 @@
     h0, h1, m = HALO, HALO // 2, rows // 2
 
     def widen(at, size):
-        a, b = recv_a[pl.ds(at, size)], recv_b[pl.ds(at, size)]
+        a, b = recv_a[pl.ds(at, size)], jnp.where(place_ref[5] != 0, recv_b[pl.ds(at, size)], 0.0)
         right, left = jnp.where(even_y, a, b), jnp.where(even_y, b, a)
         lane = iota_of(right, 2)
         odd_slot = (lane // SLOT) % 2 == 1
@@ -474,11 +474,24 @@
         out[pl.ds(r, layers, stride=rows), :] = natural[r * layers : (r + 1) * layers]
 
 
-def neighbour_swaps(axis, send_a, send_b):
-    count = lax.axis_size(axis)
-    a = [(i, i ^ 1) for i in range(count)]
-    b = [(i, ((i + 1) ^ 1) - 1) for i in range(1, count - 1)]
-    return lax.ppermute(send_a, axis, a), lax.ppermute(send_b, axis, b)
+def neighbour_swaps(along_x, send_a, send_b):
+    npx, npy = lax.axis_size("px"), lax.axis_size("py")
+
+    def swap_with(partner):
+        pairs = [(x * npy + y, partner(x, y)) for x in range(npx) for y in range(npy)]
+        return [(here, x * npy + y) for here, (x, y) in pairs]
+
+    def beside(i):
+        return ((i + 1) ^ 1) - 1
+
+    if along_x:
+        a = swap_with(lambda x, y: (x ^ 1, y))
+        b = swap_with(lambda x, y: (beside(x), y) if 0 < x < npx - 1 else (x, y ^ 1))
+    else:
+        a = swap_with(lambda x, y: (x, y ^ 1))
+        b = swap_with(lambda x, y: (x, beside(y)) if 0 < y < npy - 1 else (x ^ 1, y))
+    recv_b = lax.ppermute(send_b, ("px", "py"), b)
+    return lax.ppermute(send_a, ("px", "py"), a), recv_b
 
 
 def arr(*shape):
@@ -491,7 +504,8 @@
     total, mids = rows + 2 * HALO, (rows + 2 * HALO) // 2
     rows2, width2 = npx * rows // 4, npy * LANES // 4
     px, py = lax.axis_index("px"), lax.axis_index("py")
-    place = jnp.stack([px % 2, py % 2, px, py]).astype(jnp.int32)
+    inner_x, inner_y = ((i > 0) & (i < n - 1) for i, n in ((px, npx), (py, npy)))
+    place = jnp.stack([px % 2, py % 2, px, py, inner_x, inner_y]).astype(jnp.int32)
     fine, mid = arr(total, 2, layers, LANES), arr(mids, layers, LANES)
     low, strip_sums = arr(rows2 + 2 * PAD, layers, width2), arr(strip_rows.shape[0], layers, width2)
     fine_cos, mid_cos, low_cos = (arr(n, *item.shape) for n, item in ((7, fine), (8, mid), (8, low)))
@@ -513,13 +527,13 @@
     flat = arr(layers * rows, LANES)
     own, send_a, send_b = call(
         cut_kernel, "cut", 1, 2, (arr(rows, 2, layers, LANES), halo, halo), (flat, flat),
-        pl.BlockSpec(memory_space=pl.ANY), (pltpu.SemaphoreType.DMA((2,)),),
+        pl.BlockSpec(memory_space=pltpu.HBM), (pltpu.SemaphoreType.DMA((2,)),),
     )(place, source.reshape(flat.shape), coefficient.reshape(flat.shape))
-    recv_a, recv_b = neighbour_swaps("px", send_a, send_b)
+    recv_a, recv_b = neighbour_swaps(True, send_a, send_b)
     ext, send_a, send_b = call(pack_kernel, "pack", 1, 3, (arr(total, 2, layers, LANES), columns, columns), ())(
         place, own, recv_a, recv_b
     )
-    recv_a, recv_b = neighbour_swaps("py", send_a, send_b)
+    recv_a, recv_b = neighbour_swaps(False, send_a, send_b)
     fine_u, fine_g, fine_co, mid_v, mid_g, mid_co, packed = call(
         descend_kernel, "descend", 1, 3, (fine, fine, fine_cos, mid, mid, mid_cos, arr(2, 2, layers, LANES)),
         (fine, fine, mid),

time: 70.5 us -> 64.6 us (0.916)
  blocking collectives: 37 us -> 28.1 us
  waiting for transfers between devices: 5.55 us -> 8.95 us
  Pallas kernels: 20.5 us -> 18.4 us
  starting transfers between devices: 5.24 us -> 6.99 us
    all_to_all x2, blocking collectives: 37 us -> 28.1 us  [gather(): half = lax.all_to_all(every, ('px', 'py'), 0, 0, tiled=True)]
    ppermute x4, waiting for transfers between devices: 3.04 us -> 6.44 us  [the longest x2 3.65 us: neighbour_swaps(): recv_b = lax.ppermute(send_b, ('px', 'py'), b)]
    ppermute x4, starting transfers between devices: 4.85 us -> 6.59 us  [the longest x2 3.99 us: neighbour_swaps(): recv_b = lax.ppermute(send_b, ('px', 'py'), b)]
    pallas_call x1, Pallas kernels: 7.75 us -> 6.68 us  [shards(): call(sized(middle_kernel), 'middle', 2, 8, (fine, mid, mid, arr(2, 1, lay...]
    pallas_call x1, Pallas kernels: 5.17 us -> 4.36 us  [shards(): call(sized(last_kernel), 'last', 2, 10, arr(layers * rows, LANES), (low,...]
where the time goes in v4:
time: 64.6 us; the launch traced here: 64.4 us
  blocking collectives  28.1 us (43%)
  Pallas kernels  18.4 us (28%)
  waiting for transfers between devices  8.95 us (14%)
  starting transfers between devices  6.99 us (11%)
  local copies, waits for them, and re-layouts  1.93 us (3%)
    all_to_all x2, blocking collectives, gather(): half = lax.all_to_all(every, ('px', 'py'), 0, 0, tiled=True)  28.1 us
    pallas_call x1, Pallas kernels, shards(): call(sized(middle_kernel), 'middle', 2, 8, (fine, mid, mid, arr(2, 1, lay...  6.68 us
    pallas_call x1, Pallas kernels, shards(): call(descend_kernel, 'descend', 1, 3, (fine, fine, fine_cos, mid, mid, mi...  4.81 us
    pallas_call x1, Pallas kernels, shards(): call(sized(last_kernel), 'last', 2, 10, arr(layers * rows, LANES), (low,...  4.36 us
    ppermute x2, starting transfers between devices, neighbour_swaps(): recv_b = lax.ppermute(send_b, ('px', 'py'), b)  3.99 us
    ppermute x2, waiting for transfers between devices, neighbour_swaps(): recv_b = lax.ppermute(send_b, ('px', 'py'), b)  3.65 us
    ppermute x2, waiting for transfers between devices, neighbour_swaps(): return (lax.ppermute(send_a, ('px', 'py'), a), recv_b)  2.8 us
    ppermute x2, starting transfers between devices, neighbour_swaps(): return (lax.ppermute(send_a, ('px', 'py'), a), recv_b)  2.6 us
  transfers between devices with their start and end apart: 6, of which 4 were waited for; matrix products, arithmetic and copies ran while one was open for 0% of the time, Pallas kernels for 0%

profile of v4, /device:TPU:0, one launch (start us, length us, event | category | flops | bytes accessed | tf_op | source)
XLA Modules:
  0.0 64.4 jit_solution(9026875979678079150)
XLA Ops:
  0.0 0.0 copy-start.2
  0.0 0.1 stack.35.place_ref.refs_0_
  0.1 0.0 copy-start
  0.1 0.9 %copy-done = f32[8,32,128]{2,1,0:T(8,128)S(1)} copy-done((f32[8,32,128]{2,1,0:T(8,128)S(1)}, f32[8,32,128]{2,1,0:T(8,128)}, u32[]{:S(2)}) %copy-start) | copy-done | bytes 131096
  1.0 0.0 copy-start.1
  1.0 0.9 %copy-done.1 = f32[8,32,128]{2,1,0:T(8,128)S(1)} copy-done((f32[8,32,128]{2,1,0:T(8,128)S(1)}, f32[8,32,128]{2,1,0:T(8,128)}, u32[]{:S(2)}) %copy-start.1) | copy-done | bytes 131096
  1.9 1.5 %cut.1 = (f32[32,2,8,128]{3,2,1,0:T(8,128)S(1)}, f32[24,2,8,128]{3,2,1,0:T(8,128)S(1)}, f32[24,2,8,128]{3,2,1,0:T(8,128)S(1)}) custom-call(s32[6]{0:T(128)S(1)} %stack.35.place_ref.refs_0_, f32[256,128]{1,0:T(8,128)S(1)} %bitcast.12, f32[256,128]{1,0:T(8,128)S(1)} %bitcast.13), custom_call_target="tpu_custom_call" | custom-call | tf_op jit(solution)/shard_map/cut/pallas_call | solution.py:528
  3.4 0.5 collective-permute-start
  3.9 2.7 %collective-permute-start.1 = (f32[24,2,8,128]{3,2,1,0:T(8,128)S(1)}, f32[24,2,8,128]{3,2,1,0:T(8,128)S(1)}, u32[]{:S(2)}, u32[]{:S(2)}) collective-permute-start(f32[24,2,8,128]{3,2,1,0:T(8,128)S(1)} %get-tuple-element.26), channel_id=1, source_target_pairs={{0,1},{1,0},{2,3},{3,2},{4,8},{5,9},{6,10},{7,11},{8,4},{9,5},{10,... | collective-permute-start | bytes 589832 | tf_op jit(solution)/shard_map/ppermute | solution.py:493
  6.5 0.0 collective-permute-done.recv_a
  6.5 3.6 %collective-permute-done.1.recv_b = f32[24,2,8,128]{3,2,1,0:T(8,128)S(1)} collective-permute-done((f32[24,2,8,128]{3,2,1,0:T(8,128)S(1)}, f32[24,2,8,128]{3,2,1,0:T(8,128)S(1)}, u32[]{:S(2)}, u32[]{:S(2)}) %collective-permute-start.1) | collective-permute-done | bytes 196640 | tf_op jit(solution)/shard_map/ppermute | solution.py:493
  10.2 1.1 %pack.1 = (f32[80,2,8,128]{3,2,1,0:T(8,128)S(1)}, f32[40,8,128]{2,1,0:T(8,128)S(1)}, f32[40,8,128]{2,1,0:T(8,128)S(1)}) custom-call(s32[6]{0:T(128)S(1)} %stack.35.place_ref.refs_0_, f32[32,2,8,128]{3,2,1,0:T(8,128)S(1)} %get-tuple-element.24.own, f32[24,2,8,128]{3,2,1,0:T(8,128)S(1)} %collective-permute-done.recv_a, ...), custom_call_target="tpu_custom_call" | custom-call | tf_op jit(solution)/shard_map/pack/pallas_call | solution.py:533
  11.3 2.1 %collective-permute-start.2 = (f32[40,8,128]{2,1,0:T(8,128)S(1)}, f32[40,8,128]{2,1,0:T(8,128)S(1)}, u32[]{:S(2)}, u32[]{:S(2)}) collective-permute-start(f32[40,8,128]{2,1,0:T(8,128)S(1)} %get-tuple-element.28), channel_id=1, source_target_pairs={{0,1},{1,0},{2,3},{3,2},{4,5},{5,4},{6,7},{7,6},{8,9},{9,8},{10,11... | collective-permute-start | bytes 491528 | tf_op jit(solution)/shard_map/ppermute | solution.py:494
  13.4 1.3 %collective-permute-start.3 = (f32[40,8,128]{2,1,0:T(8,128)S(1)}, f32[40,8,128]{2,1,0:T(8,128)S(1)}, u32[]{:S(2)}, u32[]{:S(2)}) collective-permute-start(f32[40,8,128]{2,1,0:T(8,128)S(1)} %get-tuple-element.29), channel_id=1, source_target_pairs={{0,4},{1,2},{2,1},{3,7},{4,0},{5,6},{6,5},{7,3},{8,12},{9,10},{10,... | collective-permute-start | bytes 491528 | tf_op jit(solution)/shard_map/ppermute | solution.py:493
  14.7 2.8 %collective-permute-done.2.recv_a = f32[40,8,128]{2,1,0:T(8,128)S(1)} collective-permute-done((f32[40,8,128]{2,1,0:T(8,128)S(1)}, f32[40,8,128]{2,1,0:T(8,128)S(1)}, u32[]{:S(2)}, u32[]{:S(2)}) %collective-permute-start.2) | collective-permute-done | bytes 163872 | tf_op jit(solution)/shard_map/ppermute | solution.py:494
  17.5 0.0 collective-permute-done.3.recv_b
  17.5 4.8 %descend.1 = (f32[80,2,8,128]{3,2,1,0:T(8,128)S(1)}, f32[80,2,8,128]{3,2,1,0:T(8,128)S(1)}, f32[7,80,2,8,128]{4,3,2,1,0:T(8,128)S(1)}, f32[40,8,128]{2,1,0:T(8,1...) custom-call(s32[6]{0:T(128)S(1)} %stack.35.place_ref.refs_0_, ...), custom_call_target="tpu_custom_call" | custom-call | tf_op jit(solution)/shard_map/descend/pallas_call | solution.py:537
  22.3 17.2 %all_to_all.10.refs_2_ = f32[32,2,8,128]{3,2,1,0:T(8,128)S(1)} all-to-all(f32[32,2,8,128]{3,2,1,0:T(8,128)S(1)} %bitcast.15), channel_id=1, replica_groups=mesh['px'=8,'py'=4] {'px','py'}, dimensions={0} | all-to-all | bytes 524288 | tf_op jit(solution)/shard_map/all_to_all | solution.py:545
  39.5 0.4 collective-permute-start.4
  39.9 1.2 %collective-permute-done.4.refs_3_ = f32[32,2,8,128]{3,2,1,0:T(8,128)S(1)} collective-permute-done((f32[32,2,8,128]{3,2,1,0:T(8,128)S(1)}, f32[32,2,8,128]{3,2,1,0:T(8,128)S(1)}, u32[]{:S(2)}, u32[]{:S(2)}) %collective-permute-start.4) | collective-permute-done | bytes 262176 | tf_op jit(solution)/shard_map/ppermute | solution.py:546
  41.1 0.0 copy-done.2
  41.1 6.7 %middle.1 = (f32[80,2,8,128]{3,2,1,0:T(8,128)S(1)}, f32[40,8,128]{2,1,0:T(8,128)S(1)}, f32[40,8,128]{2,1,0:T(8,128)S(1)}, f32[2,1,8,128]{3,2,1,0:T(8,128)S(1)}, ...) custom-call(s32[6]{0:T(128)S(1)} %stack.35.place_ref.refs_0_, s32[4]{0:T(128)S(1)} %copy-done.2, ...), custom_call_target="tpu_custom_call" | custom-call | tf_op jit(solution)/shard_map/middle/pallas_call | solution.py:551
  47.8 10.9 %all_to_all.11.refs_2_ = f32[32,1,8,128]{3,2,1,0:T(8,128)S(1)} all-to-all(f32[32,1,8,128]{3,2,1,0:T(8,128)S(1)} %bitcast.16), channel_id=1, replica_groups=mesh['px'=8,'py'=4] {'px','py'}, dimensions={0} | all-to-all | bytes 262144 | tf_op jit(solution)/shard_map/all_to_all | solution.py:545
  58.7 0.0 collective-permute-start.5
  58.7 1.3 %collective-permute-done.5.refs_3_ = f32[32,1,8,128]{3,2,1,0:T(8,128)S(1)} collective-permute-done((f32[32,1,8,128]{3,2,1,0:T(8,128)S(1)}, f32[32,1,8,128]{3,2,1,0:T(8,128)S(1)}, u32[]{:S(2)}, u32[]{:S(2)}) %collective-permute-start.5) | collective-permute-done | bytes 131104 | tf_op jit(solution)/shard_map/ppermute | solution.py:546
  60.0 4.4 %last.1 = f32[256,128]{1,0:T(8,128)} custom-call(s32[6]{0:T(128)S(1)} %stack.35.place_ref.refs_0_, s32[4]{0:T(128)S(1)} %copy-done.2, f32[32,1,8,128]{3,2,1,0:T(8,128)S(1)} %all_to_all.11.refs_2_, f32[32,1,8,128]{3,2,1,0:T(8,128)S(1)} %collective-permute-done.5.refs_3_, f32[80,2,8,128]{3,2,1,0:T(8,128)S(1)} %get-tuple-element.38.refs_4_, ...), custom_call_target="tpu_custom_call" | custom-call | tf_op jit(solution)/shard_map/last/pallas_call | solution.py:555
  (2 shorter events, 0.0 us)
Async XLA Ops:
  0.0 41.1 %copy-start.2 = (s32[4]{0:T(128)S(1)}, s32[4]{0:T(128)}, u32[]{:S(2)}) copy-start(s32[4]{0:T(128)} %refs_1_.3) | copy-start | bytes 52
  0.1 0.9 %copy-start = (f32[8,32,128]{2,1,0:T(8,128)S(1)}, f32[8,32,128]{2,1,0:T(8,128)}, u32[]{:S(2)}) copy-start(f32[8,32,128]{2,1,0:T(8,128)} %param.3) | copy-start | bytes 393220
  1.0 0.9 %copy-start.1 = (f32[8,32,128]{2,1,0:T(8,128)S(1)}, f32[8,32,128]{2,1,0:T(8,128)}, u32[]{:S(2)}) copy-start(f32[8,32,128]{2,1,0:T(8,128)} %param.4) | copy-start | bytes 393220
  3.4 3.2 %collective-permute-start = (f32[24,2,8,128]{3,2,1,0:T(8,128)S(1)}, f32[24,2,8,128]{3,2,1,0:T(8,128)S(1)}, u32[]{:S(2)}, u32[]{:S(2)}) collective-permute-start(f32[24,2,8,128]{3,2,1,0:T(8,128)S(1)} %get-tuple-element.25), channel_id=1, source_target_pairs={{0,4},{1,5},{2,6},{3,7},{4,0},{5,1},{6,2},{7,3},{8,12},{9,13},{10,... | collective-permute-start | bytes 589832 | tf_op jit(solution)/shard_map/ppermute | solution.py:494
  3.9 6.3 %collective-permute-start.1 = (f32[24,2,8,128]{3,2,1,0:T(8,128)S(1)}, f32[24,2,8,128]{3,2,1,0:T(8,128)S(1)}, u32[]{:S(2)}, u32[]{:S(2)}) collective-permute-start(f32[24,2,8,128]{3,2,1,0:T(8,128)S(1)} %get-tuple-element.26), channel_id=1, source_target_pairs={{0,1},{1,0},{2,3},{3,2},{4,8},{5,9},{6,10},{7,11},{8,4},{9,5},{10,... | collective-permute-start | bytes 589832 | tf_op jit(solution)/shard_map/ppermute | solution.py:493
  11.3 6.2 %collective-permute-start.2 = (f32[40,8,128]{2,1,0:T(8,128)S(1)}, f32[40,8,128]{2,1,0:T(8,128)S(1)}, u32[]{:S(2)}, u32[]{:S(2)}) collective-permute-start(f32[40,8,128]{2,1,0:T(8,128)S(1)} %get-tuple-element.28), channel_id=1, source_target_pairs={{0,1},{1,0},{2,3},{3,2},{4,5},{5,4},{6,7},{7,6},{8,9},{9,8},{10,11... | collective-permute-start | bytes 491528 | tf_op jit(solution)/shard_map/ppermute | solution.py:494
  13.4 4.1 %collective-permute-start.3 = (f32[40,8,128]{2,1,0:T(8,128)S(1)}, f32[40,8,128]{2,1,0:T(8,128)S(1)}, u32[]{:S(2)}, u32[]{:S(2)}) collective-permute-start(f32[40,8,128]{2,1,0:T(8,128)S(1)} %get-tuple-element.29), channel_id=1, source_target_pairs={{0,4},{1,2},{2,1},{3,7},{4,0},{5,6},{6,5},{7,3},{8,12},{9,10},{10,... | collective-permute-start | bytes 491528 | tf_op jit(solution)/shard_map/ppermute | solution.py:493
  39.5 1.6 %collective-permute-start.4 = (f32[32,2,8,128]{3,2,1,0:T(8,128)S(1)}, f32[32,2,8,128]{3,2,1,0:T(8,128)S(1)}, u32[]{:S(2)}, u32[]{:S(2)}) collective-permute-start(f32[32,2,8,128]{3,2,1,0:T(8,128)S(1)} %all_to_all.10.refs_2_), channel_id=1, source_target_pairs={{0,4},{4,0},{8,12},{12,8},{16,20},{20,16},{24,28},{28,24},{1,5},{5... | collective-permute-start | bytes 786440 | tf_op jit(solution)/shard_map/ppermute | solution.py:546
  58.7 1.3 %collective-permute-start.5 = (f32[32,1,8,128]{3,2,1,0:T(8,128)S(1)}, f32[32,1,8,128]{3,2,1,0:T(8,128)S(1)}, u32[]{:S(2)}, u32[]{:S(2)}) collective-permute-start(f32[32,1,8,128]{3,2,1,0:T(8,128)S(1)} %all_to_all.11.refs_2_), channel_id=1, source_target_pairs={{0,4},{4,0},{8,12},{12,8},{16,20},{20,16},{24,28},{28,24},{1,5},{5... | collective-permute-start | bytes 393224 | tf_op jit(solution)/shard_map/ppermute | solution.py:546

commit v5 on v4

--- a/solution.py
+++ b/solution.py
@@ -160,10 +160,18 @@
 
 FINE_CHUNK = 20
 CHUNK = 64
-
-
-def coarse_rows(values):
+DOWN_CHUNK = 10
+PACK_CHUNK = 40
+WIDEN_CHUNK = 40
+FINE_SET = 19
+MID_SET = 18
+LOW_SET = 32
+ADD_CHUNK = 15
+
+
+def coarse_rows(values, place_ref):
     per = LANES // (HALF // 2)
+    turn = place_ref[3] % per
     count = values.shape[0] // per
     left = jnp.concatenate(
         [jnp.concatenate([values[per * p + g] for g in range(per)], axis=1) for p in range(count)], axis=0
@@ -171,26 +179,19 @@
 
     def place(row, col):
         lane = row % LANES
-        return (lane < HALF) & (lane % 2 == 0) & (col == (row // LANES) * (HALF // 2) + lane // 2)
+        quarter = (row // LANES + turn) % per
+        return (lane < HALF) & (lane % 2 == 0) & (col == quarter * (HALF // 2) + lane // 2)
 
     packed = exact_dot(left, one_hot((per * LANES, LANES), place))
     layers = values.shape[1]
     return [packed[p * layers : (p + 1) * layers] for p in range(count)]
 
 
-def cut_kernel(rows, place_ref, source_far, coefficient_far, own, send_a, send_b, source, coefficient, arrived):
+def cut_kernel(rows, place_ref, both, own, send_a, send_b):
     layers = own.shape[2]
-    copies = [
-        pltpu.make_async_copy(far, near, arrived.at[i])
-        for i, (far, near) in enumerate(((source_far, source), (coefficient_far, coefficient)))
-    ]
-    for copy in copies:
-        copy.start()
-    for copy in copies:
-        copy.wait()
-    pick = [pl.ds(r, layers, stride=rows) for r in range(rows)]
+    pick = [[pl.ds(which * layers * rows + r, layers, stride=rows) for which in range(2)] for r in range(rows)]
     left = jnp.concatenate(
-        [jnp.concatenate([source[at, :], coefficient[at, :]], axis=1) for at in pick], axis=0
+        [jnp.concatenate([both[at, :] for at in pair], axis=1) for pair in pick], axis=0
     )
 
     def place(row, col):
@@ -230,7 +231,7 @@
         send_a[pl.ds(at, size)] = jnp.where(even_y, last, first)
         send_b[pl.ds(at, size)] = jnp.where(even_y, first, last)
 
-    rows_loop(0, half, 8, body)
+    rows_loop(0, half, PACK_CHUNK, body)
 
 
 def descend_kernel(
@@ -254,22 +255,22 @@
                 wide[here, 0] = jnp.where(lane < HALF, inner, shifted(merged[which], HALF - slot * SLOT, 2))
                 wide[here, 1] = jnp.where(lane < HALF, shifted(inner, HALF, 2), shifted(merged[which], -slot * SLOT, 2))
 
-    rows_loop(0, half, 8, widen)
+    rows_loop(0, half, WIDEN_CHUNK, widen)
 
     def coarser(at, size):
         here = pl.ds(2 * at, 2 * size)
         k1[pl.ds(at, size)] = 0.25 * pair_sum_rows(k_ref[here, 0] + k_ref[here, 1])
 
     rows_loop(0, half, 20, coarser)
-    fine_coefficients(k_ref, s_ref, fine_co, fine_g, h0 - 22, h0 + rows + 22, 8)
-    mid_coefficients(k1, mid_co, h1 - 10, h1 + m + 10, 12)
-    descend(rows, fine_g, fine_u, fine_g, fine_co, mid_v, mid_g, mid_co, 10, packed)
+    fine_coefficients(k_ref, s_ref, fine_co, fine_g, h0 - 22, h0 + rows + 22, FINE_SET)
+    mid_coefficients(k1, mid_co, h1 - 10, h1 + m + 10, MID_SET)
+    descend(rows, place_ref, fine_g, fine_u, fine_g, fine_co, mid_v, mid_g, mid_co, 10, packed)
     k2 = 0.25 * pair_sum_lanes(pair_sum_rows(k1[pl.ds(h1, m)]))
-    for p, part in enumerate(coarse_rows(k2)):
+    for p, part in enumerate(coarse_rows(k2, place_ref)):
         packed[p, 1] = part
 
 
-def descend(rows, fine_first, fine_u, fine_g, fine_co, mid_v, mid_g, mid_co, reach, packed):
+def descend(rows, place_ref, fine_first, fine_u, fine_g, fine_co, mid_v, mid_g, mid_co, reach, packed):
     h0, h1, m = HALO, HALO // 2, rows // 2
     sweep_fine(fine_first, fine_u, fine_co, fine_g, h0 - 2 * reach - 1, h0 + rows + 2 * reach + 1)
 
@@ -279,11 +280,11 @@
         left = fine_co[BACK, here, 0] * (new[0] - v[0]) + fine_co[BACK, here, 1] * (new[1] - v[1])
         mid_g[pl.ds(at, size)] = mid_co[INV, pl.ds(at, size)] * pair_sum_rows(left)
 
-    rows_loop(h1 - reach, h1 + m + reach, FINE_CHUNK // 2, down)
+    rows_loop(h1 - reach, h1 + m + reach, DOWN_CHUNK, down)
     sweep(mid_g, mid_v, mid_co, mid_g, h1 - reach + 1, h1 + m + reach - 1)
     v, new = swept(mid_v, mid_co, mid_g, h1, m)
     left = mid_co[BACK, pl.ds(h1, m)] * (new - v)
-    for p, part in enumerate(coarse_rows(pair_sum_lanes(pair_sum_rows(left)))):
+    for p, part in enumerate(coarse_rows(pair_sum_lanes(pair_sum_rows(left)), place_ref)):
         packed[p, 0] = part
 
 
@@ -303,9 +304,10 @@
                     parts = [jnp.where(here, mine[i, which], other[i, which]) for i in devices]
                     group = iota_of(parts[0], 1) // width
                     for g in range(per):
-                        row = shifted(parts[0], -g * width, 1)
-                        for j in range(1, per):
-                            row = jnp.where(group == j, shifted(parts[j], (j - g) * width, 1), row)
+                        row = parts[-g % per]
+                        for quarter in range(1, per):
+                            row = jnp.where(group == quarter, parts[(quarter - g) % per], row)
+                        row = shifted(row, -g * width, 1)
                         at = PAD + ix * block + per * p + g
                         lanes = pl.ds(q * LANES, LANES)
                         if scale is not None:
@@ -332,22 +334,31 @@
         for which in range(INV + 1):
             co[which, pl.ds(at, size)] = found[which]
 
-    rows_loop(PAD, PAD + rows2, 16, body)
+    rows_loop(PAD, PAD + rows2, LOW_SET, body)
     zero = jnp.zeros(k2.shape[1:], F32)
-
-    def strip(index, start):
-        end = start + strips_ref[index]
-        co[W, start] = zero
-        co[E, end - 1] = zero
-        sums[index] = lax.fori_loop(start, end, lambda r, total: total + co[BACK, r], zero)
-        return end
-
-    lax.fori_loop(0, strips_ref.shape[0], strip, PAD)
-    total = jnp.sum(jnp.sum(sums[...], axis=2, keepdims=True), axis=1, keepdims=True)
-    sums[...] = jnp.broadcast_to(relaxation * total, sums.shape)
-
-
-def coarse_solve(rows, rows2, place_ref, strips_ref, co, sums, g, a, b, over, reach):
+    for start, end in strips(strips_ref):
+        co[W, PAD + start] = zero
+        co[E, PAD + end - 1] = zero
+    sums[...] = 1.0 / (relaxation * strip_sums(co.at[BACK], strips_ref, rows2, sums))
+
+
+def strips(strips_ref):
+    ends = [0]
+    for index in range(strips_ref.shape[0]):
+        ends.append(ends[-1] + strips_ref[index])
+    return list(zip(ends[:-1], ends[1:]))
+
+
+def strip_sums(values, strips_ref, rows2, scratch):
+    whole = values[pl.ds(PAD, rows2)]
+    row = iota_of(whole, 0)
+    for index, (start, end) in enumerate(strips(strips_ref)):
+        scratch[index] = jnp.sum(jnp.where((row >= start) & (row < end), whole, 0.0), axis=0)
+    total = jnp.sum(jnp.sum(scratch[...], axis=2, keepdims=True), axis=1, keepdims=True)
+    return jnp.broadcast_to(total, scratch.shape)
+
+
+def coarse_solve(rows2, strips_ref, co, sums, g, a, b, over):
     zero = jnp.zeros(g.shape[1:], F32)
     for ref in (g, a, b):
         ref[PAD - 1] = zero
@@ -366,41 +377,20 @@
         a[pl.ds(first, size)] = co[BACK, pl.ds(first, size)] * (new - v)
 
     rows_loop(PAD, PAD + rows2, CHUNK, left)
-    count = strips_ref.shape[0]
-
-    def strip(index, start):
-        end = start + strips_ref[index]
-        over[index] = lax.fori_loop(start, end, lambda r, total: total + a[r], zero)
-        return end
-
-    lax.fori_loop(0, count, strip, PAD)
-    total = jnp.sum(jnp.sum(over[...], axis=2, keepdims=True), axis=1, keepdims=True)
-    over[...] = total / sums[...]
-    block = rows // 4
-    first = PAD + place_ref[2] * block - reach
-    final = first + block + 2 * reach
-
-    def shift(index, start):
-        end = start + strips_ref[index]
-        amount = over[index]
-
-        def row(r, carry):
-            b[r] = b[r] + amount
-            return carry
-
-        lax.fori_loop(jnp.maximum(start, first), jnp.minimum(end, final), row, 0)
-        return end
-
-    lax.fori_loop(0, count, shift, PAD)
-
-
-def correct(rows, place_ref, e2, mid_v, target, reach):
+    over[...] = sums[...] * strip_sums(a, strips_ref, rows2, over)
+
+
+def correct(rows, place_ref, strips_ref, e2, over, mid_v, target, reach):
     h1, m = HALO // 2, rows // 2
     low = -(-reach // 2)
     block = rows // 4
     layers, width = e2.shape[1:]
     span = block + 2 * low
-    window = e2[pl.ds(place_ref[2] * block + PAD - low, span)]
+    first_row = place_ref[2] * block - low
+    window = e2[pl.ds(first_row + PAD, span)]
+    row = iota_of(window, 0) + first_row
+    for index, (start, end) in enumerate(strips(strips_ref)):
+        window = window + jnp.where((row >= start) & (row < end), over[index][None], 0.0)
     first = place_ref[3] * (HALF // 2)
 
     def place(row, col):
@@ -426,7 +416,7 @@
         both = fine.reshape((size, 2) + fine.shape[1:]) + mid_a[pl.ds(at, size)][:, None, None]
         fine_a[pl.ds(2 * at, 2 * size)] = both.reshape(fine.shape)
 
-    rows_loop(h1 - reach + 2, h1 + m + reach - 2, 10, add)
+    rows_loop(h1 - reach + 2, h1 + m + reach - 2, ADD_CHUNK, add)
     sweep_fine(fine_a, fine_b, fine_co, fine_g, h0 - fine_reach - 1, h0 + rows + fine_reach + 1)
     sweep_fine(fine_b, fine_a, fine_co, fine_g, h0 - fine_reach, h0 + rows + fine_reach)
 
@@ -444,11 +434,11 @@
     unpack(place_ref, mine, other, 1, k2, None, npx, npy, block)
     coarse_coefficients(rows2, strips_ref, k2, low_co, sums)
     unpack(place_ref, mine, other, 0, g2, low_co, npx, npy, block)
-    coarse_solve(rows, rows2, place_ref, strips_ref, low_co, sums, g2, a2, b2, over, 5)
-    correct(rows, place_ref, b2, mid_v, va, 9)
+    coarse_solve(rows2, strips_ref, low_co, sums, g2, a2, b2, over)
+    correct(rows, place_ref, strips_ref, b2, over, mid_v, va, 9)
     ascend(rows, 9, 11, va, vb, mid_co, mid_g, fine_u, fa, fb, fine_co, fine_g)
     sweep_fine(fa, fb, fine_co, fine_g, HALO - 10, HALO + rows + 10)
-    descend(rows, fb, fine_out, fine_g, fine_co, mid_v_out, mid_g_out, mid_co, 4, packed)
+    descend(rows, place_ref, fb, fine_out, fine_g, fine_co, mid_v_out, mid_g_out, mid_co, 4, packed)
 
 
 def last_kernel(
@@ -458,8 +448,8 @@
     block = rows // 4
     rows2 = npx * block
     unpack(place_ref, mine, other, 0, g2, low_co, npx, npy, block)
-    coarse_solve(rows, rows2, place_ref, strips_ref, low_co, sums, g2, a2, b2, over, 2)
-    correct(rows, place_ref, b2, mid_v, va, 3)
+    coarse_solve(rows2, strips_ref, low_co, sums, g2, a2, b2, over)
+    correct(rows, place_ref, strips_ref, b2, over, mid_v, va, 3)
     ascend(rows, 3, 0, va, vb, mid_co, mid_g, fine_u, fa, fb, fine_co, fine_g)
     layers = fa.shape[2]
     here = pl.ds(HALO, rows)
@@ -513,22 +503,19 @@
     columns = arr(mids, layers, LANES)
     room = min(48, 12 + 24 * rows2 * layers * width2 * 4 // 2**20)
 
-    def call(body, name, smem, vmem, out_shape, scratch, where=VMEM, semaphores=()):
+    def call(body, name, smem, vmem, out_shape, scratch):
         return pl.pallas_call(
             functools.partial(body, rows),
             out_shape=out_shape,
-            in_specs=[SMEM] * smem + [where] * vmem,
+            in_specs=[SMEM] * smem + [VMEM] * vmem,
             out_specs=jax.tree.map(lambda _: VMEM, out_shape),
-            scratch_shapes=[pltpu.VMEM(item.shape, F32) for item in scratch] + list(semaphores),
+            scratch_shapes=[pltpu.VMEM(item.shape, F32) for item in scratch],
             compiler_params=pltpu.CompilerParams(vmem_limit_bytes=room * 2**20),
             name=name,
         )
 
-    flat = arr(layers * rows, LANES)
-    own, send_a, send_b = call(
-        cut_kernel, "cut", 1, 2, (arr(rows, 2, layers, LANES), halo, halo), (flat, flat),
-        pl.BlockSpec(memory_space=pltpu.HBM), (pltpu.SemaphoreType.DMA((2,)),),
-    )(place, source.reshape(flat.shape), coefficient.reshape(flat.shape))
+    both = jnp.stack([source, coefficient]).reshape(2 * layers * rows, LANES)
+    own, send_a, send_b = call(cut_kernel, "cut", 1, 1, (arr(rows, 2, layers, LANES), halo, halo), ())(place, both)
     recv_a, recv_b = neighbour_swaps(True, send_a, send_b)
     ext, send_a, send_b = call(pack_kernel, "pack", 1, 3, (arr(total, 2, layers, LANES), columns, columns), ())(
         place, own, recv_a, recv_b

time: 64.6 us -> 60.9 us (0.943)
  Pallas kernels: 18.4 us -> 15.5 us
  local copies, waits for them, and re-layouts: 1.93 us -> 0.13 us
  other arithmetic: 0 us -> 1 us
    unnamed x6 -> x2, local copies, waits for them, and re-layouts: 1.81 us -> 0.01 us
    another operation x0 -> x1, other arithmetic: none -> 1 us  [shards(): both = jnp.stack([source, coefficient]).reshape(2 * layers * rows, LANES)]
    pallas_call x1, Pallas kernels: 6.68 us -> 5.79 us  [shards(): call(sized(middle_kernel), 'middle', 2, 8, (fine, mid, mid, arr(2, 1, lay...]
    pallas_call x1, Pallas kernels: 4.81 us -> 3.98 us  [shards(): call(descend_kernel, 'descend', 1, 3, (fine, fine, fine_cos, mid, mid, mi...]
where the time goes in v5:
time: 60.9 us; the launch traced here: 60.7 us
  blocking collectives  28.1 us (46%)
  Pallas kernels  15.5 us (25%)
  waiting for transfers between devices  8.95 us (15%)
  starting transfers between devices  6.99 us (11%)
  other arithmetic  1 us (2%)
    all_to_all x2, blocking collectives, gather(): half = lax.all_to_all(every, ('px', 'py'), 0, 0, tiled=True)  28.1 us
    pallas_call x1, Pallas kernels, shards(): call(sized(middle_kernel), 'middle', 2, 8, (fine, mid, mid, arr(2, 1, lay...  5.79 us
    ppermute x2, starting transfers between devices, neighbour_swaps(): recv_b = lax.ppermute(send_b, ('px', 'py'), b)  3.99 us
    pallas_call x1, Pallas kernels, shards(): call(descend_kernel, 'descend', 1, 3, (fine, fine, fine_cos, mid, mid, mi...  3.98 us
    pallas_call x1, Pallas kernels, shards(): call(sized(last_kernel), 'last', 2, 10, arr(layers * rows, LANES), (low,...  3.87 us
    ppermute x2, waiting for transfers between devices, neighbour_swaps(): recv_b = lax.ppermute(send_b, ('px', 'py'), b)  3.65 us
    ppermute x2, waiting for transfers between devices, neighbour_swaps(): return (lax.ppermute(send_a, ('px', 'py'), a), recv_b)  2.8 us
    ppermute x2, starting transfers between devices, neighbour_swaps(): return (lax.ppermute(send_a, ('px', 'py'), a), recv_b)  2.6 us
  transfers between devices with their start and end apart: 6, of which 4 were waited for; matrix products, arithmetic and copies ran while one was open for 0% of the time, Pallas kernels for 0%

profile of v5, /device:TPU:0, one launch (start us, length us, event | category | flops | bytes accessed | tf_op | source)
XLA Modules:
  0.0 60.7 jit_solution(17694078578650971155)
XLA Ops:
  0.0 0.0 copy-start
  0.0 1.0 %pad_maximum_fusion = f32[2,8,32,128]{3,2,1,0:T(8,128)S(1)} fusion(f32[1,8,32,128]{3,2,1,0:T(8,128)} %bitcast.17, f32[1,8,32,128]{3,2,1,0:T(8,128)} %bitcast.18), kind=kLoop, calls=%fused_computation | loop fusion | flops 65536 | bytes 524288 | tf_op jit(solution)/shard_map/stack | solution.py:517
  1.0 0.1 stack.44.place_ref.refs_0_
  1.1 1.1 %cut.1 = (f32[32,2,8,128]{3,2,1,0:T(8,128)S(1)}, f32[24,2,8,128]{3,2,1,0:T(8,128)S(1)}, f32[24,2,8,128]{3,2,1,0:T(8,128)S(1)}) custom-call(s32[6]{0:T(128)S(1)} %stack.44.place_ref.refs_0_, f32[512,128]{1,0:T(8,128)S(1)} %bitcast.13), custom_call_target="tpu_custom_call" | custom-call | tf_op jit(solution)/shard_map/cut/pallas_call | solution.py:518
  2.2 0.5 collective-permute-start
  2.7 2.7 %collective-permute-start.1 = (f32[24,2,8,128]{3,2,1,0:T(8,128)S(1)}, f32[24,2,8,128]{3,2,1,0:T(8,128)S(1)}, u32[]{:S(2)}, u32[]{:S(2)}) collective-permute-start(f32[24,2,8,128]{3,2,1,0:T(8,128)S(1)} %get-tuple-element.26), channel_id=1, source_target_pairs={{0,1},{1,0},{2,3},{3,2},{4,8},{5,9},{6,10},{7,11},{8,4},{9,5},{10,... | collective-permute-start | bytes 589832 | tf_op jit(solution)/shard_map/ppermute | solution.py:483
  5.4 0.0 collective-permute-done.recv_a
  5.4 3.6 %collective-permute-done.1.recv_b = f32[24,2,8,128]{3,2,1,0:T(8,128)S(1)} collective-permute-done((f32[24,2,8,128]{3,2,1,0:T(8,128)S(1)}, f32[24,2,8,128]{3,2,1,0:T(8,128)S(1)}, u32[]{:S(2)}, u32[]{:S(2)}) %collective-permute-start.1) | collective-permute-done | bytes 196640 | tf_op jit(solution)/shard_map/ppermute | solution.py:483
  9.0 0.7 %pack.1 = (f32[80,2,8,128]{3,2,1,0:T(8,128)S(1)}, f32[40,8,128]{2,1,0:T(8,128)S(1)}, f32[40,8,128]{2,1,0:T(8,128)S(1)}) custom-call(s32[6]{0:T(128)S(1)} %stack.44.place_ref.refs_0_, f32[32,2,8,128]{3,2,1,0:T(8,128)S(1)} %get-tuple-element.24.own, f32[24,2,8,128]{3,2,1,0:T(8,128)S(1)} %collective-permute-done.recv_a, ...), custom_call_target="tpu_custom_call" | custom-call | tf_op jit(solution)/shard_map/pack/pallas_call | solution.py:520
  9.8 2.1 %collective-permute-start.2 = (f32[40,8,128]{2,1,0:T(8,128)S(1)}, f32[40,8,128]{2,1,0:T(8,128)S(1)}, u32[]{:S(2)}, u32[]{:S(2)}) collective-permute-start(f32[40,8,128]{2,1,0:T(8,128)S(1)} %get-tuple-element.28), channel_id=1, source_target_pairs={{0,1},{1,0},{2,3},{3,2},{4,5},{5,4},{6,7},{7,6},{8,9},{9,8},{10,11... | collective-permute-start | bytes 491528 | tf_op jit(solution)/shard_map/ppermute | solution.py:484
  11.9 1.3 %collective-permute-start.3 = (f32[40,8,128]{2,1,0:T(8,128)S(1)}, f32[40,8,128]{2,1,0:T(8,128)S(1)}, u32[]{:S(2)}, u32[]{:S(2)}) collective-permute-start(f32[40,8,128]{2,1,0:T(8,128)S(1)} %get-tuple-element.29), channel_id=1, source_target_pairs={{0,4},{1,2},{2,1},{3,7},{4,0},{5,6},{6,5},{7,3},{8,12},{9,10},{10,... | collective-permute-start | bytes 491528 | tf_op jit(solution)/shard_map/ppermute | solution.py:483
  13.2 2.8 %collective-permute-done.2.recv_a = f32[40,8,128]{2,1,0:T(8,128)S(1)} collective-permute-done((f32[40,8,128]{2,1,0:T(8,128)S(1)}, f32[40,8,128]{2,1,0:T(8,128)S(1)}, u32[]{:S(2)}, u32[]{:S(2)}) %collective-permute-start.2) | collective-permute-done | bytes 163872 | tf_op jit(solution)/shard_map/ppermute | solution.py:484
  16.0 0.0 collective-permute-done.3.recv_b
  16.0 4.0 %descend.1 = (f32[80,2,8,128]{3,2,1,0:T(8,128)S(1)}, f32[80,2,8,128]{3,2,1,0:T(8,128)S(1)}, f32[7,80,2,8,128]{4,3,2,1,0:T(8,128)S(1)}, f32[40,8,128]{2,1,0:T(8,1...) custom-call(s32[6]{0:T(128)S(1)} %stack.44.place_ref.refs_0_, ...), custom_call_target="tpu_custom_call" | custom-call | tf_op jit(solution)/shard_map/descend/pallas_call | solution.py:524
  20.0 17.2 %all_to_all.10.refs_2_ = f32[32,2,8,128]{3,2,1,0:T(8,128)S(1)} all-to-all(f32[32,2,8,128]{3,2,1,0:T(8,128)S(1)} %bitcast.15), channel_id=1, replica_groups=mesh['px'=8,'py'=4] {'px','py'}, dimensions={0} | all-to-all | bytes 524288 | tf_op jit(solution)/shard_map/all_to_all | solution.py:532
  37.2 0.4 collective-permute-start.4
  37.6 1.2 %collective-permute-done.4.refs_3_ = f32[32,2,8,128]{3,2,1,0:T(8,128)S(1)} collective-permute-done((f32[32,2,8,128]{3,2,1,0:T(8,128)S(1)}, f32[32,2,8,128]{3,2,1,0:T(8,128)S(1)}, u32[]{:S(2)}, u32[]{:S(2)}) %collective-permute-start.4) | collective-permute-done | bytes 262176 | tf_op jit(solution)/shard_map/ppermute | solution.py:533
  38.8 0.0 copy-done
  38.8 5.8 %middle.1 = (f32[80,2,8,128]{3,2,1,0:T(8,128)S(1)}, f32[40,8,128]{2,1,0:T(8,128)S(1)}, f32[40,8,128]{2,1,0:T(8,128)S(1)}, f32[2,1,8,128]{3,2,1,0:T(8,128)S(1)}, ...) custom-call(s32[6]{0:T(128)S(1)} %stack.44.place_ref.refs_0_, s32[4]{0:T(128)S(1)} %copy-done, ...), custom_call_target="tpu_custom_call" | custom-call | tf_op jit(solution)/shard_map/middle/pallas_call | solution.py:538
  44.6 10.9 %all_to_all.11.refs_2_ = f32[32,1,8,128]{3,2,1,0:T(8,128)S(1)} all-to-all(f32[32,1,8,128]{3,2,1,0:T(8,128)S(1)} %bitcast.16), channel_id=1, replica_groups=mesh['px'=8,'py'=4] {'px','py'}, dimensions={0} | all-to-all | bytes 262144 | tf_op jit(solution)/shard_map/all_to_all | solution.py:532
  55.5 0.0 collective-permute-start.5
  55.5 1.3 %collective-permute-done.5.refs_3_ = f32[32,1,8,128]{3,2,1,0:T(8,128)S(1)} collective-permute-done((f32[32,1,8,128]{3,2,1,0:T(8,128)S(1)}, f32[32,1,8,128]{3,2,1,0:T(8,128)S(1)}, u32[]{:S(2)}, u32[]{:S(2)}) %collective-permute-start.5) | collective-permute-done | bytes 131104 | tf_op jit(solution)/shard_map/ppermute | solution.py:533
  56.8 3.9 %last.1 = f32[256,128]{1,0:T(8,128)} custom-call(s32[6]{0:T(128)S(1)} %stack.44.place_ref.refs_0_, s32[4]{0:T(128)S(1)} %copy-done, f32[32,1,8,128]{3,2,1,0:T(8,128)S(1)} %all_to_all.11.refs_2_, f32[32,1,8,128]{3,2,1,0:T(8,128)S(1)} %collective-permute-done.5.refs_3_, f32[80,2,8,128]{3,2,1,0:T(8,128)S(1)} %get-tuple-element.38.refs_4_, ...), custom_call_target="tpu_custom_call" | custom-call | tf_op jit(solution)/shard_map/last/pallas_call | solution.py:542
  (2 shorter events, 0.0 us)
Async XLA Ops:
  0.0 38.8 %copy-start = (s32[4]{0:T(128)S(1)}, s32[4]{0:T(128)}, u32[]{:S(2)}) copy-start(s32[4]{0:T(128)} %refs_1_.3) | copy-start | bytes 52
  2.2 3.2 %collective-permute-start = (f32[24,2,8,128]{3,2,1,0:T(8,128)S(1)}, f32[24,2,8,128]{3,2,1,0:T(8,128)S(1)}, u32[]{:S(2)}, u32[]{:S(2)}) collective-permute-start(f32[24,2,8,128]{3,2,1,0:T(8,128)S(1)} %get-tuple-element.25), channel_id=1, source_target_pairs={{0,4},{1,5},{2,6},{3,7},{4,0},{5,1},{6,2},{7,3},{8,12},{9,13},{10,... | collective-permute-start | bytes 589832 | tf_op jit(solution)/shard_map/ppermute | solution.py:484
  2.7 6.3 %collective-permute-start.1 = (f32[24,2,8,128]{3,2,1,0:T(8,128)S(1)}, f32[24,2,8,128]{3,2,1,0:T(8,128)S(1)}, u32[]{:S(2)}, u32[]{:S(2)}) collective-permute-start(f32[24,2,8,128]{3,2,1,0:T(8,128)S(1)} %get-tuple-element.26), channel_id=1, source_target_pairs={{0,1},{1,0},{2,3},{3,2},{4,8},{5,9},{6,10},{7,11},{8,4},{9,5},{10,... | collective-permute-start | bytes 589832 | tf_op jit(solution)/shard_map/ppermute | solution.py:483
  9.8 6.2 %collective-permute-start.2 = (f32[40,8,128]{2,1,0:T(8,128)S(1)}, f32[40,8,128]{2,1,0:T(8,128)S(1)}, u32[]{:S(2)}, u32[]{:S(2)}) collective-permute-start(f32[40,8,128]{2,1,0:T(8,128)S(1)} %get-tuple-element.28), channel_id=1, source_target_pairs={{0,1},{1,0},{2,3},{3,2},{4,5},{5,4},{6,7},{7,6},{8,9},{9,8},{10,11... | collective-permute-start | bytes 491528 | tf_op jit(solution)/shard_map/ppermute | solution.py:484
  11.9 4.1 %collective-permute-start.3 = (f32[40,8,128]{2,1,0:T(8,128)S(1)}, f32[40,8,128]{2,1,0:T(8,128)S(1)}, u32[]{:S(2)}, u32[]{:S(2)}) collective-permute-start(f32[40,8,128]{2,1,0:T(8,128)S(1)} %get-tuple-element.29), channel_id=1, source_target_pairs={{0,4},{1,2},{2,1},{3,7},{4,0},{5,6},{6,5},{7,3},{8,12},{9,10},{10,... | collective-permute-start | bytes 491528 | tf_op jit(solution)/shard_map/ppermute | solution.py:483
  37.2 1.6 %collective-permute-start.4 = (f32[32,2,8,128]{3,2,1,0:T(8,128)S(1)}, f32[32,2,8,128]{3,2,1,0:T(8,128)S(1)}, u32[]{:S(2)}, u32[]{:S(2)}) collective-permute-start(f32[32,2,8,128]{3,2,1,0:T(8,128)S(1)} %all_to_all.10.refs_2_), channel_id=1, source_target_pairs={{0,4},{4,0},{8,12},{12,8},{16,20},{20,16},{24,28},{28,24},{1,5},{5... | collective-permute-start | bytes 786440 | tf_op jit(solution)/shard_map/ppermute | solution.py:533
  55.5 1.3 %collective-permute-start.5 = (f32[32,1,8,128]{3,2,1,0:T(8,128)S(1)}, f32[32,1,8,128]{3,2,1,0:T(8,128)S(1)}, u32[]{:S(2)}, u32[]{:S(2)}) collective-permute-start(f32[32,1,8,128]{3,2,1,0:T(8,128)S(1)} %all_to_all.11.refs_2_), channel_id=1, source_target_pairs={{0,4},{4,0},{8,12},{12,8},{16,20},{20,16},{24,28},{28,24},{1,5},{5... | collective-permute-start | bytes 393224 | tf_op jit(solution)/shard_map/ppermute | solution.py:533

commit v6 on v5

--- a/solution.py
+++ b/solution.py
@@ -56,15 +56,20 @@
 
 
 def exact_dot(left, right):
-    return lax.dot_general(
-        left, right, (((1,), (0,)), ((), ())), precision=lax.Precision.HIGHEST, preferred_element_type=F32
-    )
+    total = None
+    for last in (False, False, True):
+        part = left.astype(jnp.bfloat16)
+        term = lax.dot_general(part, right, (((1,), (0,)), ((), ())), preferred_element_type=F32)
+        total = term if total is None else total + term
+        if not last:
+            left = left - part.astype(F32)
+    return total
 
 
 def one_hot(shape, place):
     row = lax.broadcasted_iota(jnp.int32, shape, 0)
     col = lax.broadcasted_iota(jnp.int32, shape, 1)
-    return jnp.where(place(row, col), 1.0, 0.0).astype(F32)
+    return jnp.where(place(row, col), 1.0, 0.0).astype(jnp.bfloat16)
 
 
 W, E, S, N, D, U, BACK, INV = range(8)
@@ -161,8 +166,6 @@
 FINE_CHUNK = 20
 CHUNK = 64
 DOWN_CHUNK = 10
-PACK_CHUNK = 40
-WIDEN_CHUNK = 40
 FINE_SET = 19
 MID_SET = 18
 LOW_SET = 32
@@ -187,7 +190,12 @@
     return [packed[p * layers : (p + 1) * layers] for p in range(count)]
 
 
-def cut_kernel(rows, place_ref, both, own, send_a, send_b):
+RIGHT_SLOT = (0, 2, 1, 3)
+LEFT_SLOT = (3, 5, 4, 6)
+PAIRS = HALO // 2
+
+
+def cut_kernel(rows, place_ref, both, own, xa, xb, ya, yb, aa, ab, ba, bb):
     layers = own.shape[2]
     pick = [[pl.ds(which * layers * rows + r, layers, stride=rows) for which in range(2)] for r in range(rows)]
     left = jnp.concatenate(
@@ -199,63 +207,71 @@
         return col == (row // LANES) * LANES + (y % 2) * HALF + y // 2
 
     sorted_y = exact_dot(left, one_hot((2 * LANES, 2 * LANES), place))
+    parts = []
     for which in range(2):
-        part = sorted_y[:, which * LANES : (which + 1) * LANES]
-        own[:, which] = part.reshape(rows, layers, LANES)
-    even_x = place_ref[0] == 0
-    send_a[...] = own[pl.ds(jnp.where(even_x, rows - HALO, 0), HALO)]
-    send_b[...] = own[pl.ds(jnp.where(even_x, 0, rows - HALO), HALO)]
-
-
-RIGHT_SLOT = (0, 2, 1, 3)
-LEFT_SLOT = (3, 5, 4, 6)
-
-
-def pack_kernel(rows, place_ref, own, recv_a, recv_b, ext, send_a, send_b):
+        part = sorted_y[:, which * LANES : (which + 1) * LANES].reshape(rows, layers, LANES)
+        own[:, which] = part
+        pairs = part.reshape(rows // 2, 2, layers, LANES)
+        parts += [pairs[:, 0], pairs[:, 1]]
     even_x, even_y = place_ref[0] == 0, place_ref[1] == 0
-    half = send_a.shape[0]
-    ext[pl.ds(HALO, rows)] = own[...]
-    a, b = recv_a[...], jnp.where(place_ref[4] != 0, recv_b[...], 0.0)
-    ext[pl.ds(0, HALO)] = jnp.where(even_x, b, a)
-    ext[pl.ds(HALO + rows, HALO)] = jnp.where(even_x, a, b)
-
-    def body(at, size):
-        parts = [ext[pl.ds(at + h * half, size), which] for which in range(2) for h in range(2)]
-        slot = (iota_of(parts[0], 2) // SLOT) % 4
-        first = last = None
-        for g in range(4):
-            right = shifted(parts[g], RIGHT_SLOT[g] * SLOT, 2)
-            left = shifted(parts[g], (LEFT_SLOT[g] - 3) * SLOT, 2)
-            first = right if g == 0 else jnp.where(slot == RIGHT_SLOT[g] % 4, right, first)
-            last = left if g == 0 else jnp.where(slot == LEFT_SLOT[g] % 4, left, last)
-        send_a[pl.ds(at, size)] = jnp.where(even_y, last, first)
-        send_b[pl.ds(at, size)] = jnp.where(even_y, first, last)
-
-    rows_loop(0, half, PACK_CHUNK, body)
-
-
-def descend_kernel(
-    rows, place_ref, ext, recv_a, recv_b, fine_u, fine_g, fine_co, mid_v, mid_g, mid_co, packed, s_ref, k_ref, k1
-):
-    even_y = place_ref[1] == 0
-    half = recv_a.shape[0]
-    h0, h1, m = HALO, HALO // 2, rows // 2
-
-    def widen(at, size):
-        a, b = recv_a[pl.ds(at, size)], jnp.where(place_ref[5] != 0, recv_b[pl.ds(at, size)], 0.0)
+    low, high = jnp.where(even_x, rows - HALO, 0), jnp.where(even_x, 0, rows - HALO)
+    xa[...] = own[pl.ds(low, HALO)]
+    xb[...] = own[pl.ds(high, HALO)]
+    slot = (iota_of(parts[0], 2) // SLOT) % 4
+    for g in range(4):
+        right = shifted(parts[g], RIGHT_SLOT[g] * SLOT, 2)
+        left = shifted(parts[g], (LEFT_SLOT[g] - 3) * SLOT, 2)
+        first = right if g == 0 else jnp.where(slot == RIGHT_SLOT[g] % 4, right, first)
+        last = left if g == 0 else jnp.where(slot == LEFT_SLOT[g] % 4, left, last)
+    ya[...] = jnp.where(even_y, last, first)
+    yb[...] = jnp.where(even_y, first, last)
+    for columns, with_a, with_b in ((ya, aa, ba), (yb, ab, bb)):
+        with_a[...] = columns[pl.ds(low // 2, PAIRS)]
+        with_b[...] = columns[pl.ds(high // 2, PAIRS)]
+
+
+def widen(rows, place_ref, own, xa, xb, ya, yb, aa, ab, ba, bb, s_ref, k_ref):
+    even_x, even_y = place_ref[0] == 0, place_ref[1] == 0
+    inner_x, inner_y = place_ref[4] != 0, place_ref[5] != 0
+    inner_both = jnp.logical_and(inner_x, inner_y)
+    xa, ya, aa = xa[...], ya[...], aa[...]
+    xb, ba = (jnp.where(inner_x, ref[...], 0.0) for ref in (xb, ba))
+    yb, ab = (jnp.where(inner_y, ref[...], 0.0) for ref in (yb, ab))
+    bb = jnp.where(inner_both, bb[...], 0.0)
+    before = [jnp.where(even_x, b, a) for a, b in ((aa, ba), (ab, bb))]
+    after = [jnp.where(even_x, a, b) for a, b in ((aa, ba), (ab, bb))]
+    for start, inner, (a, b) in (
+        (0, jnp.where(even_x, xb, xa), before),
+        (HALO, own[...], (ya, yb)),
+        (HALO + rows, jnp.where(even_x, xa, xb), after),
+    ):
         right, left = jnp.where(even_y, a, b), jnp.where(even_y, b, a)
         lane = iota_of(right, 2)
         odd_slot = (lane // SLOT) % 2 == 1
         merged = (jnp.where(odd_slot, left, right), jnp.where(odd_slot, right, left))
+        count, layers = right.shape[:2]
+        pairs = inner.reshape(count, 2, 2, layers, LANES)
         for which, wide in enumerate((s_ref, k_ref)):
+            found = []
             for h in range(2):
-                here = pl.ds(at + h * half, size)
                 slot = RIGHT_SLOT[2 * which + h]
-                inner = ext[here, which]
-                wide[here, 0] = jnp.where(lane < HALF, inner, shifted(merged[which], HALF - slot * SLOT, 2))
-                wide[here, 1] = jnp.where(lane < HALF, shifted(inner, HALF, 2), shifted(merged[which], -slot * SLOT, 2))
-
-    rows_loop(0, half, WIDEN_CHUNK, widen)
+                block = pairs[:, h, which]
+                found.append((
+                    jnp.where(lane < HALF, block, shifted(merged[which], HALF - slot * SLOT, 2)),
+                    jnp.where(lane < HALF, shifted(block, HALF, 2), shifted(merged[which], -slot * SLOT, 2)),
+                ))
+            for s in range(2):
+                both = jnp.stack([found[0][s], found[1][s]], axis=1)
+                wide[pl.ds(start, 2 * count), s] = both.reshape(2 * count, layers, LANES)
+
+
+def descend_kernel(
+    rows, place_ref, own, xa, xb, ya, yb, aa, ab, ba, bb,
+    fine_u, fine_g, fine_co, mid_v, mid_g, mid_co, packed, s_ref, k_ref, k1,
+):
+    h0, h1, m = HALO, HALO // 2, rows // 2
+    half = h0 + m
+    widen(rows, place_ref, own, xa, xb, ya, yb, aa, ab, ba, bb, s_ref, k_ref)
 
     def coarser(at, size):
         here = pl.ds(2 * at, 2 * size)
@@ -464,24 +480,34 @@
         out[pl.ds(r, layers, stride=rows), :] = natural[r * layers : (r + 1) * layers]
 
 
-def neighbour_swaps(along_x, send_a, send_b):
+def neighbour_swaps(xa, xb, ya, yb, aa, ab, ba, bb):
     npx, npy = lax.axis_size("px"), lax.axis_size("py")
 
-    def swap_with(partner):
-        pairs = [(x * npy + y, partner(x, y)) for x in range(npx) for y in range(npy)]
-        return [(here, x * npy + y) for here, (x, y) in pairs]
-
-    def beside(i):
+    def swap(block, partner):
+        pairs = []
+        for x in range(npx):
+            for y in range(npy):
+                to_x, to_y = partner(x, y, 0 < x < npx - 1, 0 < y < npy - 1)
+                pairs.append((x * npy + y, to_x * npy + to_y))
+        return lax.ppermute(block, ("px", "py"), pairs)
+
+    def far(i):
         return ((i + 1) ^ 1) - 1
 
-    if along_x:
-        a = swap_with(lambda x, y: (x ^ 1, y))
-        b = swap_with(lambda x, y: (beside(x), y) if 0 < x < npx - 1 else (x, y ^ 1))
-    else:
-        a = swap_with(lambda x, y: (x, y ^ 1))
-        b = swap_with(lambda x, y: (x, beside(y)) if 0 < y < npy - 1 else (x ^ 1, y))
-    recv_b = lax.ppermute(send_b, ("px", "py"), b)
-    return lax.ppermute(send_a, ("px", "py"), a), recv_b
+    def corner(x, y, inner_x, inner_y):
+        if not inner_y:
+            return x ^ 1, y
+        return far(x) if inner_x else x, far(y)
+
+    ya = swap(ya, lambda x, y, inner_x, inner_y: (x, y ^ 1))
+    xa = swap(xa, lambda x, y, inner_x, inner_y: (x ^ 1, y))
+    aa = swap(aa, lambda x, y, inner_x, inner_y: (x ^ 1, y ^ 1))
+    yb = swap(yb, lambda x, y, inner_x, inner_y: (x, far(y)) if inner_y else (x ^ 1, y))
+    ab = swap(ab, lambda x, y, inner_x, inner_y: (x ^ 1, far(y) if inner_y else y))
+    ba = swap(ba, lambda x, y, inner_x, inner_y: (far(x) if inner_x else x, y ^ 1))
+    xb = swap(xb, lambda x, y, inner_x, inner_y: (far(x), y) if inner_x else (x, y ^ 1))
+    bb = swap(bb, corner)
+    return xa, xb, ya, yb, aa, ab, ba, bb
 
 
 def arr(*shape):
@@ -499,8 +525,7 @@
     fine, mid = arr(total, 2, layers, LANES), arr(mids, layers, LANES)
     low, strip_sums = arr(rows2 + 2 * PAD, layers, width2), arr(strip_rows.shape[0], layers, width2)
     fine_cos, mid_cos, low_cos = (arr(n, *item.shape) for n, item in ((7, fine), (8, mid), (8, low)))
-    halo = arr(HALO, 2, layers, LANES)
-    columns = arr(mids, layers, LANES)
+    halo, columns, corner = (arr(*n, layers, LANES) for n in ((HALO, 2), (rows // 2,), (PAIRS,)))
     room = min(48, 12 + 24 * rows2 * layers * width2 * 4 // 2**20)
 
     def call(body, name, smem, vmem, out_shape, scratch):
@@ -515,16 +540,13 @@
         )
 
     both = jnp.stack([source, coefficient]).reshape(2 * layers * rows, LANES)
-    own, send_a, send_b = call(cut_kernel, "cut", 1, 1, (arr(rows, 2, layers, LANES), halo, halo), ())(place, both)
-    recv_a, recv_b = neighbour_swaps(True, send_a, send_b)
-    ext, send_a, send_b = call(pack_kernel, "pack", 1, 3, (arr(total, 2, layers, LANES), columns, columns), ())(
-        place, own, recv_a, recv_b
-    )
-    recv_a, recv_b = neighbour_swaps(False, send_a, send_b)
+    own, *sent = call(
+        cut_kernel, "cut", 1, 1, (arr(rows, 2, layers, LANES),) + (halo,) * 2 + (columns,) * 2 + (corner,) * 4, ()
+    )(place, both)
     fine_u, fine_g, fine_co, mid_v, mid_g, mid_co, packed = call(
-        descend_kernel, "descend", 1, 3, (fine, fine, fine_cos, mid, mid, mid_cos, arr(2, 2, layers, LANES)),
+        descend_kernel, "descend", 1, 9, (fine, fine, fine_cos, mid, mid, mid_cos, arr(2, 2, layers, LANES)),
         (fine, fine, mid),
-    )(place, ext, recv_a, recv_b)
+    )(place, own, *neighbour_swaps(*sent))
 
     def gather(block):
         shape = (npx // 2, 2, npy) + block.shape[1:]

time: 60.9 us -> 59.4 us (0.975)
  waiting for transfers between devices: 8.95 us -> 5.49 us
  starting transfers between devices: 6.99 us -> 9.12 us
  Pallas kernels: 15.5 us -> 14.3 us
  blocking collectives: 28.1 us -> 29.2 us
    ppermute x4 -> x8, waiting for transfers between devices: 6.44 us -> 2.99 us  [swap(): return lax.ppermute(block, ('px', 'py'), pairs)]
    ppermute x4 -> x8, starting transfers between devices: 6.59 us -> 8.72 us  [swap(): return lax.ppermute(block, ('px', 'py'), pairs)]
    all_to_all x2, blocking collectives: 28.1 us -> 29.2 us  [gather(): half = lax.all_to_all(every, ('px', 'py'), 0, 0, tiled=True)]
    pallas_call x3 -> x2, Pallas kernels: 5.84 us -> 4.88 us  [the longest x1 3.86 us: shards(): call(descend_kernel, 'descend', 1, 9, (fine, fine, fine_cos, mid, mid, mi...]
  transfers between devices with their start and end apart: 6 -> 10, of which waited for: 4 -> 5; matrix products, arithmetic and copies ran while one was open for 0% -> 0% of each run, Pallas kernels for 0% -> 0%
where the time goes in v6:
time: 59.4 us; the launch traced here: 59.2 us
  blocking collectives  29.2 us (49%)
  Pallas kernels  14.3 us (24%)
  starting transfers between devices  9.12 us (15%)
  waiting for transfers between devices  5.49 us (9%)
  other arithmetic  1 us (2%)
    all_to_all x2, blocking collectives, gather(): half = lax.all_to_all(every, ('px', 'py'), 0, 0, tiled=True)  29.2 us
    ppermute x8, starting transfers between devices, swap(): return lax.ppermute(block, ('px', 'py'), pairs)  8.72 us
    pallas_call x1, Pallas kernels, shards(): call(sized(middle_kernel), 'middle', 2, 8, (fine, mid, mid, arr(2, 1, lay...  5.68 us
    pallas_call x1, Pallas kernels, shards(): call(descend_kernel, 'descend', 1, 9, (fine, fine, fine_cos, mid, mid, mi...  3.86 us
    pallas_call x1, Pallas kernels, shards(): call(sized(last_kernel), 'last', 2, 10, arr(layers * rows, LANES), (low,...  3.75 us
    ppermute x8, waiting for transfers between devices, swap(): return lax.ppermute(block, ('px', 'py'), pairs)  2.99 us
    ppermute x2, waiting for transfers between devices, gather(): return (half, lax.ppermute(half, 'px', [(i, i ^ 1) for i in range(npx)]))  2.51 us
  transfers between devices with their start and end apart: 10, of which 5 were waited for; matrix products, arithmetic and copies ran while one was open for 0% of the time, Pallas kernels for 0%

profile of v6, /device:TPU:0, one launch (start us, length us, event | category | flops | bytes accessed | tf_op | source)
XLA Modules:
  0.0 59.2 jit_solution(3552744381000175593)
XLA Ops:
  0.0 0.0 copy-start
  0.0 1.0 %pad_maximum_fusion = f32[2,8,32,128]{3,2,1,0:T(8,128)S(1)} fusion(f32[1,8,32,128]{3,2,1,0:T(8,128)} %bitcast.17, f32[1,8,32,128]{3,2,1,0:T(8,128)} %bitcast.18), kind=kLoop, calls=%fused_computation | loop fusion | flops 65536 | bytes 524288 | tf_op jit(solution)/shard_map/stack | solution.py:542
  1.0 0.1 stack.44.place_ref.refs_0_
  1.1 1.0 %cut.1 = (f32[32,2,8,128]{3,2,1,0:T(8,128)S(1)}, f32[24,2,8,128]{3,2,1,0:T(8,128)S(1)}, f32[24,2,8,128]{3,2,1,0:T(8,128)S(1)}, f32[16,8,128]{2,1,0:T(8,128)S(1)}...) custom-call(s32[6]{0:T(128)S(1)} %stack.44.place_ref.refs_0_, ...), custom_call_target="tpu_custom_call" | custom-call | tf_op jit(solution)/shard_map/cut/pallas_call | solution.py:543
  2.1 0.5 collective-permute-start
  2.6 2.7 %collective-permute-start.1 = (f32[24,2,8,128]{3,2,1,0:T(8,128)S(1)}, f32[24,2,8,128]{3,2,1,0:T(8,128)S(1)}, u32[]{:S(2)}, u32[]{:S(2)}) collective-permute-start(f32[24,2,8,128]{3,2,1,0:T(8,128)S(1)} %get-tuple-element.29), channel_id=1, source_target_pairs={{0,1},{1,0},{2,3},{3,2},{4,8},{5,9},{6,10},{7,11},{8,4},{9,5},{10,... | collective-permute-start | bytes 589832 | tf_op jit(solution)/shard_map/ppermute | solution.py:492
  5.3 1.2 %collective-permute-start.4 = (f32[12,8,128]{2,1,0:T(8,128)S(1)}, f32[12,8,128]{2,1,0:T(8,128)S(1)}, u32[]{:S(2)}, u32[]{:S(2)}) collective-permute-start(f32[12,8,128]{2,1,0:T(8,128)S(1)} %get-tuple-element.32), channel_id=1, source_target_pairs={{0,5},{1,4},{2,7},{3,6},{4,1},{5,0},{6,3},{7,2},{8,13},{9,12},{10,... | collective-permute-start | bytes 147464 | tf_op jit(solution)/shard_map/ppermute | solution.py:492
  6.5 0.0 collective-permute-start.5
  6.5 2.1 %collective-permute-start.6 = (f32[12,8,128]{2,1,0:T(8,128)S(1)}, f32[12,8,128]{2,1,0:T(8,128)S(1)}, u32[]{:S(2)}, u32[]{:S(2)}) collective-permute-start(f32[12,8,128]{2,1,0:T(8,128)S(1)} %get-tuple-element.34), channel_id=1, source_target_pairs={{0,1},{1,0},{2,3},{3,2},{4,9},{5,8},{6,11},{7,10},{8,5},{9,4},{10,... | collective-permute-start | bytes 147464 | tf_op jit(solution)/shard_map/ppermute | solution.py:492
  8.6 0.8 %collective-permute-done.4.aa = f32[12,8,128]{2,1,0:T(8,128)S(1)} collective-permute-done((f32[12,8,128]{2,1,0:T(8,128)S(1)}, f32[12,8,128]{2,1,0:T(8,128)S(1)}, u32[]{:S(2)}, u32[]{:S(2)}) %collective-permute-start.4) | collective-permute-done | bytes 49184 | tf_op jit(solution)/shard_map/ppermute | solution.py:492
  9.4 0.1 collective-permute-start.2
  9.5 0.0 collective-permute-done.5.ab
  9.5 1.5 %collective-permute-start.3 = (f32[16,8,128]{2,1,0:T(8,128)S(1)}, f32[16,8,128]{2,1,0:T(8,128)S(1)}, u32[]{:S(2)}, u32[]{:S(2)}) collective-permute-start(f32[16,8,128]{2,1,0:T(8,128)S(1)} %get-tuple-element.31), channel_id=1, source_target_pairs={{0,4},{1,2},{2,1},{3,7},{4,0},{5,6},{6,5},{7,3},{8,12},{9,10},{10,... | collective-permute-start | bytes 196616 | tf_op jit(solution)/shard_map/ppermute | solution.py:492
  11.1 0.0 collective-permute-done.6.ba
  11.1 0.6 collective-permute-start.7
  11.6 0.9 %collective-permute-done.7.bb = f32[12,8,128]{2,1,0:T(8,128)S(1)} collective-permute-done((f32[12,8,128]{2,1,0:T(8,128)S(1)}, f32[12,8,128]{2,1,0:T(8,128)S(1)}, u32[]{:S(2)}, u32[]{:S(2)}) %collective-permute-start.7) | collective-permute-done | bytes 49184 | tf_op jit(solution)/shard_map/ppermute | solution.py:492
  12.5 1.3 %collective-permute-done.2.ya = f32[16,8,128]{2,1,0:T(8,128)S(1)} collective-permute-done((f32[16,8,128]{2,1,0:T(8,128)S(1)}, f32[16,8,128]{2,1,0:T(8,128)S(1)}, u32[]{:S(2)}, u32[]{:S(2)}) %collective-permute-start.2) | collective-permute-done | bytes 65568 | tf_op jit(solution)/shard_map/ppermute | solution.py:492
  13.8 0.0 collective-permute-done.3.yb
  13.8 0.0 collective-permute-done.xa
  13.8 0.0 collective-permute-done.1.xb
  13.8 3.9 %descend.1 = (f32[80,2,8,128]{3,2,1,0:T(8,128)S(1)}, f32[80,2,8,128]{3,2,1,0:T(8,128)S(1)}, f32[7,80,2,8,128]{4,3,2,1,0:T(8,128)S(1)}, f32[40,8,128]{2,1,0:T(8,1...) custom-call(s32[6]{0:T(128)S(1)} %stack.44.place_ref.refs_0_, ...), custom_call_target="tpu_custom_call" | custom-call | tf_op jit(solution)/shard_map/descend/pallas_call | solution.py:546
  17.7 18.2 %all_to_all.10.refs_2_ = f32[32,2,8,128]{3,2,1,0:T(8,128)S(1)} all-to-all(f32[32,2,8,128]{3,2,1,0:T(8,128)S(1)} %bitcast.15), channel_id=1, replica_groups=mesh['px'=8,'py'=4] {'px','py'}, dimensions={0} | all-to-all | bytes 524288 | tf_op jit(solution)/shard_map/all_to_all | solution.py:554
  36.0 0.4 collective-permute-start.8
  36.4 1.2 %collective-permute-done.8.refs_3_ = f32[32,2,8,128]{3,2,1,0:T(8,128)S(1)} collective-permute-done((f32[32,2,8,128]{3,2,1,0:T(8,128)S(1)}, f32[32,2,8,128]{3,2,1,0:T(8,128)S(1)}, u32[]{:S(2)}, u32[]{:S(2)}) %collective-permute-start.8) | collective-permute-done | bytes 262176 | tf_op jit(solution)/shard_map/ppermute | solution.py:555
  37.5 0.0 copy-done
  37.5 5.7 %middle.1 = (f32[80,2,8,128]{3,2,1,0:T(8,128)S(1)}, f32[40,8,128]{2,1,0:T(8,128)S(1)}, f32[40,8,128]{2,1,0:T(8,128)S(1)}, f32[2,1,8,128]{3,2,1,0:T(8,128)S(1)}, ...) custom-call(s32[6]{0:T(128)S(1)} %stack.44.place_ref.refs_0_, s32[4]{0:T(128)S(1)} %copy-done, ...), custom_call_target="tpu_custom_call" | custom-call | tf_op jit(solution)/shard_map/middle/pallas_call | solution.py:560
  43.2 10.9 %all_to_all.11.refs_2_ = f32[32,1,8,128]{3,2,1,0:T(8,128)S(1)} all-to-all(f32[32,1,8,128]{3,2,1,0:T(8,128)S(1)} %bitcast.16), channel_id=1, replica_groups=mesh['px'=8,'py'=4] {'px','py'}, dimensions={0} | all-to-all | bytes 262144 | tf_op jit(solution)/shard_map/all_to_all | solution.py:554
  54.1 0.0 collective-permute-start.9
  54.1 1.3 %collective-permute-done.9.refs_3_ = f32[32,1,8,128]{3,2,1,0:T(8,128)S(1)} collective-permute-done((f32[32,1,8,128]{3,2,1,0:T(8,128)S(1)}, f32[32,1,8,128]{3,2,1,0:T(8,128)S(1)}, u32[]{:S(2)}, u32[]{:S(2)}) %collective-permute-start.9) | collective-permute-done | bytes 131104 | tf_op jit(solution)/shard_map/ppermute | solution.py:555
  55.5 3.8 %last.1 = f32[256,128]{1,0:T(8,128)} custom-call(s32[6]{0:T(128)S(1)} %stack.44.place_ref.refs_0_, s32[4]{0:T(128)S(1)} %copy-done, f32[32,1,8,128]{3,2,1,0:T(8,128)S(1)} %all_to_all.11.refs_2_, f32[32,1,8,128]{3,2,1,0:T(8,128)S(1)} %collective-permute-done.9.refs_3_, f32[80,2,8,128]{3,2,1,0:T(8,128)S(1)} %get-tuple-element.44.refs_4_, ...), custom_call_target="tpu_custom_call" | custom-call | tf_op jit(solution)/shard_map/last/pallas_call | solution.py:564
  (2 shorter events, 0.0 us)
Async XLA Ops:
  0.0 37.5 %copy-start = (s32[4]{0:T(128)S(1)}, s32[4]{0:T(128)}, u32[]{:S(2)}) copy-start(s32[4]{0:T(128)} %refs_1_.3) | copy-start | bytes 52
  2.1 11.7 %collective-permute-start = (f32[24,2,8,128]{3,2,1,0:T(8,128)S(1)}, f32[24,2,8,128]{3,2,1,0:T(8,128)S(1)}, u32[]{:S(2)}, u32[]{:S(2)}) collective-permute-start(f32[24,2,8,128]{3,2,1,0:T(8,128)S(1)} %get-tuple-element.28), channel_id=1, source_target_pairs={{0,4},{1,5},{2,6},{3,7},{4,0},{5,1},{6,2},{7,3},{8,12},{9,13},{10,... | collective-permute-start | bytes 589832 | tf_op jit(solution)/shard_map/ppermute | solution.py:492
  2.6 11.2 %collective-permute-start.1 = (f32[24,2,8,128]{3,2,1,0:T(8,128)S(1)}, f32[24,2,8,128]{3,2,1,0:T(8,128)S(1)}, u32[]{:S(2)}, u32[]{:S(2)}) collective-permute-start(f32[24,2,8,128]{3,2,1,0:T(8,128)S(1)} %get-tuple-element.29), channel_id=1, source_target_pairs={{0,1},{1,0},{2,3},{3,2},{4,8},{5,9},{6,10},{7,11},{8,4},{9,5},{10,... | collective-permute-start | bytes 589832 | tf_op jit(solution)/shard_map/ppermute | solution.py:492
  5.3 4.1 %collective-permute-start.4 = (f32[12,8,128]{2,1,0:T(8,128)S(1)}, f32[12,8,128]{2,1,0:T(8,128)S(1)}, u32[]{:S(2)}, u32[]{:S(2)}) collective-permute-start(f32[12,8,128]{2,1,0:T(8,128)S(1)} %get-tuple-element.32), channel_id=1, source_target_pairs={{0,5},{1,4},{2,7},{3,6},{4,1},{5,0},{6,3},{7,2},{8,13},{9,12},{10,... | collective-permute-start | bytes 147464 | tf_op jit(solution)/shard_map/ppermute | solution.py:492
  6.5 3.0 %collective-permute-start.5 = (f32[12,8,128]{2,1,0:T(8,128)S(1)}, f32[12,8,128]{2,1,0:T(8,128)S(1)}, u32[]{:S(2)}, u32[]{:S(2)}) collective-permute-start(f32[12,8,128]{2,1,0:T(8,128)S(1)} %get-tuple-element.33), channel_id=1, source_target_pairs={{0,4},{1,6},{2,5},{3,7},{4,0},{5,2},{6,1},{7,3},{8,12},{9,14},{10,... | collective-permute-start | bytes 147464 | tf_op jit(solution)/shard_map/ppermute | solution.py:492
  6.5 4.6 %collective-permute-start.6 = (f32[12,8,128]{2,1,0:T(8,128)S(1)}, f32[12,8,128]{2,1,0:T(8,128)S(1)}, u32[]{:S(2)}, u32[]{:S(2)}) collective-permute-start(f32[12,8,128]{2,1,0:T(8,128)S(1)} %get-tuple-element.34), channel_id=1, source_target_pairs={{0,1},{1,0},{2,3},{3,2},{4,9},{5,8},{6,11},{7,10},{8,5},{9,4},{10,... | collective-permute-start | bytes 147464 | tf_op jit(solution)/shard_map/ppermute | solution.py:492
  9.4 4.4 %collective-permute-start.2 = (f32[16,8,128]{2,1,0:T(8,128)S(1)}, f32[16,8,128]{2,1,0:T(8,128)S(1)}, u32[]{:S(2)}, u32[]{:S(2)}) collective-permute-start(f32[16,8,128]{2,1,0:T(8,128)S(1)} %get-tuple-element.30), channel_id=1, source_target_pairs={{0,1},{1,0},{2,3},{3,2},{4,5},{5,4},{6,7},{7,6},{8,9},{9,8},{10,11... | collective-permute-start | bytes 196616 | tf_op jit(solution)/shard_map/ppermute | solution.py:492
  9.5 4.3 %collective-permute-start.3 = (f32[16,8,128]{2,1,0:T(8,128)S(1)}, f32[16,8,128]{2,1,0:T(8,128)S(1)}, u32[]{:S(2)}, u32[]{:S(2)}) collective-permute-start(f32[16,8,128]{2,1,0:T(8,128)S(1)} %get-tuple-element.31), channel_id=1, source_target_pairs={{0,4},{1,2},{2,1},{3,7},{4,0},{5,6},{6,5},{7,3},{8,12},{9,10},{10,... | collective-permute-start | bytes 196616 | tf_op jit(solution)/shard_map/ppermute | solution.py:492
  11.1 1.4 %collective-permute-start.7 = (f32[12,8,128]{2,1,0:T(8,128)S(1)}, f32[12,8,128]{2,1,0:T(8,128)S(1)}, u32[]{:S(2)}, u32[]{:S(2)}) collective-permute-start(f32[12,8,128]{2,1,0:T(8,128)S(1)} %get-tuple-element.35), channel_id=1, source_target_pairs={{0,4},{1,2},{2,1},{3,7},{4,0},{5,10},{6,9},{7,3},{8,12},{9,6},{10,... | collective-permute-start | bytes 147464 | tf_op jit(solution)/shard_map/ppermute | solution.py:492
  36.0 1.6 %collective-permute-start.8 = (f32[32,2,8,128]{3,2,1,0:T(8,128)S(1)}, f32[32,2,8,128]{3,2,1,0:T(8,128)S(1)}, u32[]{:S(2)}, u32[]{:S(2)}) collective-permute-start(f32[32,2,8,128]{3,2,1,0:T(8,128)S(1)} %all_to_all.10.refs_2_), channel_id=1, source_target_pairs={{0,4},{4,0},{8,12},{12,8},{16,20},{20,16},{24,28},{28,24},{1,5},{5... | collective-permute-start | bytes 786440 | tf_op jit(solution)/shard_map/ppermute | solution.py:555
  54.1 1.3 %collective-permute-start.9 = (f32[32,1,8,128]{3,2,1,0:T(8,128)S(1)}, f32[32,1,8,128]{3,2,1,0:T(8,128)S(1)}, u32[]{:S(2)}, u32[]{:S(2)}) collective-permute-start(f32[32,1,8,128]{3,2,1,0:T(8,128)S(1)} %all_to_all.11.refs_2_), channel_id=1, source_target_pairs={{0,4},{4,0},{8,12},{12,8},{16,20},{20,16},{24,28},{28,24},{1,5},{5... | collective-permute-start | bytes 393224 | tf_op jit(solution)/shard_map/ppermute | solution.py:555

commit v7 on v6

--- a/solution.py
+++ b/solution.py
@@ -118,14 +118,15 @@
 
 
 def swept_fine(v_ref, co, g_ref, at, size):
-    here, before, after = pl.ds(at, size), pl.ds(at - 1, size), pl.ds(at + 1, size)
-    v = [v_ref[here, s] for s in range(2)]
+    here = pl.ds(at, size)
+    around = v_ref[pl.ds(at - 1, size + 2)]
+    v = [around[1:-1, s] for s in range(2)]
     sides = ((shifted(v[1], 1, 2), v[1]), (v[0], shifted(v[0], -1, 2)))
     new = []
     for s in range(2):
         total = g_ref[here, s] + (1.0 - relaxation) * v[s]
-        total = total + co[W, here, s] * v_ref[before, s]
-        total = total + co[E, here, s] * v_ref[after, s]
+        total = total + co[W, here, s] * around[:-2, s]
+        total = total + co[E, here, s] * around[2:, s]
         total = total + co[D, here, s] * shifted(v[s], 1, 1)
         total = total + co[U, here, s] * shifted(v[s], -1, 1)
         total = total + co[S, here, s] * sides[s][0]
@@ -136,10 +137,11 @@
 
 def swept(v_ref, co, g_ref, at, size):
     here = pl.ds(at, size)
-    v = v_ref[here]
+    around = v_ref[pl.ds(at - 1, size + 2)]
+    v = around[1:-1]
     total = g_ref[here] + (1.0 - relaxation) * v
-    total = total + co[W, here] * v_ref[pl.ds(at - 1, size)]
-    total = total + co[E, here] * v_ref[pl.ds(at + 1, size)]
+    total = total + co[W, here] * around[:-2]
+    total = total + co[E, here] * around[2:]
     total = total + co[D, here] * shifted(v, 1, 1)
     total = total + co[U, here] * shifted(v, -1, 1)
     total = total + co[S, here] * shifted(v, 1, 2)
@@ -163,9 +165,9 @@
     rows_loop(low, high, CHUNK, body)
 
 
-FINE_CHUNK = 20
+FINE_CHUNK = 80
 CHUNK = 64
-DOWN_CHUNK = 10
+DOWN_CHUNK = 36
 FINE_SET = 19
 MID_SET = 18
 LOW_SET = 32
@@ -174,20 +176,11 @@
 
 def coarse_rows(values, place_ref):
     per = LANES // (HALF // 2)
-    turn = place_ref[3] % per
-    count = values.shape[0] // per
-    left = jnp.concatenate(
-        [jnp.concatenate([values[per * p + g] for g in range(per)], axis=1) for p in range(count)], axis=0
-    )
-
-    def place(row, col):
-        lane = row % LANES
-        quarter = (row // LANES + turn) % per
-        return (lane < HALF) & (lane % 2 == 0) & (col == quarter * (HALF // 2) + lane // 2)
-
-    packed = exact_dot(left, one_hot((per * LANES, LANES), place))
-    layers = values.shape[1]
-    return [packed[p * layers : (p + 1) * layers] for p in range(count)]
+    count, layers = values.shape[:2]
+    pick = one_hot((LANES, LANES), lambda row, col: (row < HALF) & (row == 2 * col))
+    cells = exact_dot(values.reshape(count * layers, LANES), pick).reshape(count // per, per, layers, LANES)
+    packed = [shifted(cells[:, g], (place_ref[3] + g) % per * (HALF // 2), 2) for g in range(per)]
+    return packed[0] + packed[1] + packed[2] + packed[3]
 
 
 RIGHT_SLOT = (0, 2, 1, 3)
@@ -280,13 +273,10 @@
     rows_loop(0, half, 20, coarser)
     fine_coefficients(k_ref, s_ref, fine_co, fine_g, h0 - 22, h0 + rows + 22, FINE_SET)
     mid_coefficients(k1, mid_co, h1 - 10, h1 + m + 10, MID_SET)
-    descend(rows, place_ref, fine_g, fine_u, fine_g, fine_co, mid_v, mid_g, mid_co, 10, packed)
-    k2 = 0.25 * pair_sum_lanes(pair_sum_rows(k1[pl.ds(h1, m)]))
-    for p, part in enumerate(coarse_rows(k2, place_ref)):
-        packed[p, 1] = part
-
-
-def descend(rows, place_ref, fine_first, fine_u, fine_g, fine_co, mid_v, mid_g, mid_co, reach, packed):
+    descend(rows, place_ref, fine_g, fine_u, fine_g, fine_co, mid_v, mid_g, mid_co, 10, packed, k1[pl.ds(h1, m)])
+
+
+def descend(rows, place_ref, fine_first, fine_u, fine_g, fine_co, mid_v, mid_g, mid_co, reach, packed, k1=None):
     h0, h1, m = HALO, HALO // 2, rows // 2
     sweep_fine(fine_first, fine_u, fine_co, fine_g, h0 - 2 * reach - 1, h0 + rows + 2 * reach + 1)
 
@@ -300,8 +290,11 @@
     sweep(mid_g, mid_v, mid_co, mid_g, h1 - reach + 1, h1 + m + reach - 1)
     v, new = swept(mid_v, mid_co, mid_g, h1, m)
     left = mid_co[BACK, pl.ds(h1, m)] * (new - v)
-    for p, part in enumerate(coarse_rows(pair_sum_lanes(pair_sum_rows(left)), place_ref)):
-        packed[p, 0] = part
+    low = left if k1 is None else jnp.concatenate([left, 0.25 * k1], axis=0)
+    low = coarse_rows(pair_sum_lanes(pair_sum_rows(low)), place_ref)
+    for which in range(low.shape[0] // packed.shape[0]):
+        for p in range(packed.shape[0]):
+            packed[p, which] = low[which * packed.shape[0] + p]
 
 
 def unpack(place_ref, mine, other, which, target, scale, npx, npy, block):

time: 59.4 us -> 58.1 us (0.978)
  Pallas kernels: 14.3 us -> 12.9 us
    pallas_call x1, Pallas kernels: 5.68 us -> 4.94 us  [shards(): call(sized(middle_kernel), 'middle', 2, 8, (fine, mid, mid, arr(2, 1, lay...]
where the time goes in v7:
time: 58.1 us; the launch traced here: 57.9 us
  blocking collectives  29.2 us (50%)
  Pallas kernels  12.9 us (22%)
  starting transfers between devices  9.12 us (16%)
  waiting for transfers between devices  5.49 us (9%)
  other arithmetic  1 us (2%)
    all_to_all x2, blocking collectives, gather(): half = lax.all_to_all(every, ('px', 'py'), 0, 0, tiled=True)  29.2 us
    ppermute x8, starting transfers between devices, swap(): return lax.ppermute(block, ('px', 'py'), pairs)  8.72 us
    pallas_call x1, Pallas kernels, shards(): call(sized(middle_kernel), 'middle', 2, 8, (fine, mid, mid, arr(2, 1, lay...  4.94 us
    pallas_call x1, Pallas kernels, shards(): call(sized(last_kernel), 'last', 2, 10, arr(layers * rows, LANES), (low,...  3.54 us
    pallas_call x1, Pallas kernels, shards(): call(descend_kernel, 'descend', 1, 9, (fine, fine, fine_cos, mid, mid, mi...  3.44 us
    ppermute x8, waiting for transfers between devices, swap(): return lax.ppermute(block, ('px', 'py'), pairs)  2.99 us
    ppermute x2, waiting for transfers between devices, gather(): return (half, lax.ppermute(half, 'px', [(i, i ^ 1) for i in range(npx)]))  2.51 us
  transfers between devices with their start and end apart: 10, of which 5 were waited for; matrix products, arithmetic and copies ran while one was open for 0% of the time, Pallas kernels for 0%

profile of v7, /device:TPU:0, one launch (start us, length us, event | category | flops | bytes accessed | tf_op | source)
XLA Modules:
  0.0 57.9 jit_solution(1337681086120467174)
XLA Ops:
  0.0 0.0 copy-start
  0.0 1.0 %pad_maximum_fusion = f32[2,8,32,128]{3,2,1,0:T(8,128)S(1)} fusion(f32[1,8,32,128]{3,2,1,0:T(8,128)} %bitcast.17, f32[1,8,32,128]{3,2,1,0:T(8,128)} %bitcast.18), kind=kLoop, calls=%fused_computation | loop fusion | flops 65536 | bytes 524288 | tf_op jit(solution)/shard_map/stack | solution.py:535
  1.0 0.1 stack.44.place_ref.refs_0_
  1.1 1.0 %cut.1 = (f32[32,2,8,128]{3,2,1,0:T(8,128)S(1)}, f32[24,2,8,128]{3,2,1,0:T(8,128)S(1)}, f32[24,2,8,128]{3,2,1,0:T(8,128)S(1)}, f32[16,8,128]{2,1,0:T(8,128)S(1)}...) custom-call(s32[6]{0:T(128)S(1)} %stack.44.place_ref.refs_0_, ...), custom_call_target="tpu_custom_call" | custom-call | tf_op jit(solution)/shard_map/cut/pallas_call | solution.py:536
  2.1 0.5 collective-permute-start
  2.6 2.7 %collective-permute-start.1 = (f32[24,2,8,128]{3,2,1,0:T(8,128)S(1)}, f32[24,2,8,128]{3,2,1,0:T(8,128)S(1)}, u32[]{:S(2)}, u32[]{:S(2)}) collective-permute-start(f32[24,2,8,128]{3,2,1,0:T(8,128)S(1)} %get-tuple-element.29), channel_id=1, source_target_pairs={{0,1},{1,0},{2,3},{3,2},{4,8},{5,9},{6,10},{7,11},{8,4},{9,5},{10,... | collective-permute-start | bytes 589832 | tf_op jit(solution)/shard_map/ppermute | solution.py:485
  5.3 1.2 %collective-permute-start.4 = (f32[12,8,128]{2,1,0:T(8,128)S(1)}, f32[12,8,128]{2,1,0:T(8,128)S(1)}, u32[]{:S(2)}, u32[]{:S(2)}) collective-permute-start(f32[12,8,128]{2,1,0:T(8,128)S(1)} %get-tuple-element.32), channel_id=1, source_target_pairs={{0,5},{1,4},{2,7},{3,6},{4,1},{5,0},{6,3},{7,2},{8,13},{9,12},{10,... | collective-permute-start | bytes 147464 | tf_op jit(solution)/shard_map/ppermute | solution.py:485
  6.5 0.0 collective-permute-start.5
  6.5 2.1 %collective-permute-start.6 = (f32[12,8,128]{2,1,0:T(8,128)S(1)}, f32[12,8,128]{2,1,0:T(8,128)S(1)}, u32[]{:S(2)}, u32[]{:S(2)}) collective-permute-start(f32[12,8,128]{2,1,0:T(8,128)S(1)} %get-tuple-element.34), channel_id=1, source_target_pairs={{0,1},{1,0},{2,3},{3,2},{4,9},{5,8},{6,11},{7,10},{8,5},{9,4},{10,... | collective-permute-start | bytes 147464 | tf_op jit(solution)/shard_map/ppermute | solution.py:485
  8.6 0.8 %collective-permute-done.4.aa = f32[12,8,128]{2,1,0:T(8,128)S(1)} collective-permute-done((f32[12,8,128]{2,1,0:T(8,128)S(1)}, f32[12,8,128]{2,1,0:T(8,128)S(1)}, u32[]{:S(2)}, u32[]{:S(2)}) %collective-permute-start.4) | collective-permute-done | bytes 49184 | tf_op jit(solution)/shard_map/ppermute | solution.py:485
  9.4 0.1 collective-permute-start.2
  9.5 0.0 collective-permute-done.5.ab
  9.5 1.5 %collective-permute-start.3 = (f32[16,8,128]{2,1,0:T(8,128)S(1)}, f32[16,8,128]{2,1,0:T(8,128)S(1)}, u32[]{:S(2)}, u32[]{:S(2)}) collective-permute-start(f32[16,8,128]{2,1,0:T(8,128)S(1)} %get-tuple-element.31), channel_id=1, source_target_pairs={{0,4},{1,2},{2,1},{3,7},{4,0},{5,6},{6,5},{7,3},{8,12},{9,10},{10,... | collective-permute-start | bytes 196616 | tf_op jit(solution)/shard_map/ppermute | solution.py:485
  11.1 0.0 collective-permute-done.6.ba
  11.1 0.6 collective-permute-start.7
  11.6 0.9 %collective-permute-done.7.bb = f32[12,8,128]{2,1,0:T(8,128)S(1)} collective-permute-done((f32[12,8,128]{2,1,0:T(8,128)S(1)}, f32[12,8,128]{2,1,0:T(8,128)S(1)}, u32[]{:S(2)}, u32[]{:S(2)}) %collective-permute-start.7) | collective-permute-done | bytes 49184 | tf_op jit(solution)/shard_map/ppermute | solution.py:485
  12.5 1.3 %collective-permute-done.2.ya = f32[16,8,128]{2,1,0:T(8,128)S(1)} collective-permute-done((f32[16,8,128]{2,1,0:T(8,128)S(1)}, f32[16,8,128]{2,1,0:T(8,128)S(1)}, u32[]{:S(2)}, u32[]{:S(2)}) %collective-permute-start.2) | collective-permute-done | bytes 65568 | tf_op jit(solution)/shard_map/ppermute | solution.py:485
  13.8 0.0 collective-permute-done.3.yb
  13.8 0.0 collective-permute-done.xa
  13.8 0.0 collective-permute-done.1.xb
  13.8 3.4 %descend.1 = (f32[80,2,8,128]{3,2,1,0:T(8,128)S(1)}, f32[80,2,8,128]{3,2,1,0:T(8,128)S(1)}, f32[7,80,2,8,128]{4,3,2,1,0:T(8,128)S(1)}, f32[40,8,128]{2,1,0:T(8,1...) custom-call(s32[6]{0:T(128)S(1)} %stack.44.place_ref.refs_0_, ...), custom_call_target="tpu_custom_call" | custom-call | tf_op jit(solution)/shard_map/descend/pallas_call | solution.py:539
  17.3 18.2 %all_to_all.10.refs_2_ = f32[32,2,8,128]{3,2,1,0:T(8,128)S(1)} all-to-all(f32[32,2,8,128]{3,2,1,0:T(8,128)S(1)} %bitcast.15), channel_id=1, replica_groups=mesh['px'=8,'py'=4] {'px','py'}, dimensions={0} | all-to-all | bytes 524288 | tf_op jit(solution)/shard_map/all_to_all | solution.py:547
  35.5 0.4 collective-permute-start.8
  35.9 1.2 %collective-permute-done.8.refs_3_ = f32[32,2,8,128]{3,2,1,0:T(8,128)S(1)} collective-permute-done((f32[32,2,8,128]{3,2,1,0:T(8,128)S(1)}, f32[32,2,8,128]{3,2,1,0:T(8,128)S(1)}, u32[]{:S(2)}, u32[]{:S(2)}) %collective-permute-start.8) | collective-permute-done | bytes 262176 | tf_op jit(solution)/shard_map/ppermute | solution.py:548
  37.1 0.0 copy-done
  37.1 4.9 %middle.1 = (f32[80,2,8,128]{3,2,1,0:T(8,128)S(1)}, f32[40,8,128]{2,1,0:T(8,128)S(1)}, f32[40,8,128]{2,1,0:T(8,128)S(1)}, f32[2,1,8,128]{3,2,1,0:T(8,128)S(1)}, ...) custom-call(s32[6]{0:T(128)S(1)} %stack.44.place_ref.refs_0_, s32[4]{0:T(128)S(1)} %copy-done, ...), custom_call_target="tpu_custom_call" | custom-call | tf_op jit(solution)/shard_map/middle/pallas_call | solution.py:553
  42.1 10.9 %all_to_all.11.refs_2_ = f32[32,1,8,128]{3,2,1,0:T(8,128)S(1)} all-to-all(f32[32,1,8,128]{3,2,1,0:T(8,128)S(1)} %bitcast.16), channel_id=1, replica_groups=mesh['px'=8,'py'=4] {'px','py'}, dimensions={0} | all-to-all | bytes 262144 | tf_op jit(solution)/shard_map/all_to_all | solution.py:547
  53.0 0.0 collective-permute-start.9
  53.0 1.3 %collective-permute-done.9.refs_3_ = f32[32,1,8,128]{3,2,1,0:T(8,128)S(1)} collective-permute-done((f32[32,1,8,128]{3,2,1,0:T(8,128)S(1)}, f32[32,1,8,128]{3,2,1,0:T(8,128)S(1)}, u32[]{:S(2)}, u32[]{:S(2)}) %collective-permute-start.9) | collective-permute-done | bytes 131104 | tf_op jit(solution)/shard_map/ppermute | solution.py:548
  54.3 3.5 %last.1 = f32[256,128]{1,0:T(8,128)} custom-call(s32[6]{0:T(128)S(1)} %stack.44.place_ref.refs_0_, s32[4]{0:T(128)S(1)} %copy-done, f32[32,1,8,128]{3,2,1,0:T(8,128)S(1)} %all_to_all.11.refs_2_, f32[32,1,8,128]{3,2,1,0:T(8,128)S(1)} %collective-permute-done.9.refs_3_, f32[80,2,8,128]{3,2,1,0:T(8,128)S(1)} %get-tuple-element.44.refs_4_, ...), custom_call_target="tpu_custom_call" | custom-call | tf_op jit(solution)/shard_map/last/pallas_call | solution.py:557
  (2 shorter events, 0.0 us)
Async XLA Ops:
  0.0 37.1 %copy-start = (s32[4]{0:T(128)S(1)}, s32[4]{0:T(128)}, u32[]{:S(2)}) copy-start(s32[4]{0:T(128)} %refs_1_.3) | copy-start | bytes 52
  2.1 11.7 %collective-permute-start = (f32[24,2,8,128]{3,2,1,0:T(8,128)S(1)}, f32[24,2,8,128]{3,2,1,0:T(8,128)S(1)}, u32[]{:S(2)}, u32[]{:S(2)}) collective-permute-start(f32[24,2,8,128]{3,2,1,0:T(8,128)S(1)} %get-tuple-element.28), channel_id=1, source_target_pairs={{0,4},{1,5},{2,6},{3,7},{4,0},{5,1},{6,2},{7,3},{8,12},{9,13},{10,... | collective-permute-start | bytes 589832 | tf_op jit(solution)/shard_map/ppermute | solution.py:485
  2.6 11.2 %collective-permute-start.1 = (f32[24,2,8,128]{3,2,1,0:T(8,128)S(1)}, f32[24,2,8,128]{3,2,1,0:T(8,128)S(1)}, u32[]{:S(2)}, u32[]{:S(2)}) collective-permute-start(f32[24,2,8,128]{3,2,1,0:T(8,128)S(1)} %get-tuple-element.29), channel_id=1, source_target_pairs={{0,1},{1,0},{2,3},{3,2},{4,8},{5,9},{6,10},{7,11},{8,4},{9,5},{10,... | collective-permute-start | bytes 589832 | tf_op jit(solution)/shard_map/ppermute | solution.py:485
  5.3 4.1 %collective-permute-start.4 = (f32[12,8,128]{2,1,0:T(8,128)S(1)}, f32[12,8,128]{2,1,0:T(8,128)S(1)}, u32[]{:S(2)}, u32[]{:S(2)}) collective-permute-start(f32[12,8,128]{2,1,0:T(8,128)S(1)} %get-tuple-element.32), channel_id=1, source_target_pairs={{0,5},{1,4},{2,7},{3,6},{4,1},{5,0},{6,3},{7,2},{8,13},{9,12},{10,... | collective-permute-start | bytes 147464 | tf_op jit(solution)/shard_map/ppermute | solution.py:485
  6.5 3.0 %collective-permute-start.5 = (f32[12,8,128]{2,1,0:T(8,128)S(1)}, f32[12,8,128]{2,1,0:T(8,128)S(1)}, u32[]{:S(2)}, u32[]{:S(2)}) collective-permute-start(f32[12,8,128]{2,1,0:T(8,128)S(1)} %get-tuple-element.33), channel_id=1, source_target_pairs={{0,4},{1,6},{2,5},{3,7},{4,0},{5,2},{6,1},{7,3},{8,12},{9,14},{10,... | collective-permute-start | bytes 147464 | tf_op jit(solution)/shard_map/ppermute | solution.py:485
  6.5 4.6 %collective-permute-start.6 = (f32[12,8,128]{2,1,0:T(8,128)S(1)}, f32[12,8,128]{2,1,0:T(8,128)S(1)}, u32[]{:S(2)}, u32[]{:S(2)}) collective-permute-start(f32[12,8,128]{2,1,0:T(8,128)S(1)} %get-tuple-element.34), channel_id=1, source_target_pairs={{0,1},{1,0},{2,3},{3,2},{4,9},{5,8},{6,11},{7,10},{8,5},{9,4},{10,... | collective-permute-start | bytes 147464 | tf_op jit(solution)/shard_map/ppermute | solution.py:485
  9.4 4.4 %collective-permute-start.2 = (f32[16,8,128]{2,1,0:T(8,128)S(1)}, f32[16,8,128]{2,1,0:T(8,128)S(1)}, u32[]{:S(2)}, u32[]{:S(2)}) collective-permute-start(f32[16,8,128]{2,1,0:T(8,128)S(1)} %get-tuple-element.30), channel_id=1, source_target_pairs={{0,1},{1,0},{2,3},{3,2},{4,5},{5,4},{6,7},{7,6},{8,9},{9,8},{10,11... | collective-permute-start | bytes 196616 | tf_op jit(solution)/shard_map/ppermute | solution.py:485
  9.5 4.3 %collective-permute-start.3 = (f32[16,8,128]{2,1,0:T(8,128)S(1)}, f32[16,8,128]{2,1,0:T(8,128)S(1)}, u32[]{:S(2)}, u32[]{:S(2)}) collective-permute-start(f32[16,8,128]{2,1,0:T(8,128)S(1)} %get-tuple-element.31), channel_id=1, source_target_pairs={{0,4},{1,2},{2,1},{3,7},{4,0},{5,6},{6,5},{7,3},{8,12},{9,10},{10,... | collective-permute-start | bytes 196616 | tf_op jit(solution)/shard_map/ppermute | solution.py:485
  11.1 1.4 %collective-permute-start.7 = (f32[12,8,128]{2,1,0:T(8,128)S(1)}, f32[12,8,128]{2,1,0:T(8,128)S(1)}, u32[]{:S(2)}, u32[]{:S(2)}) collective-permute-start(f32[12,8,128]{2,1,0:T(8,128)S(1)} %get-tuple-element.35), channel_id=1, source_target_pairs={{0,4},{1,2},{2,1},{3,7},{4,0},{5,10},{6,9},{7,3},{8,12},{9,6},{10,... | collective-permute-start | bytes 147464 | tf_op jit(solution)/shard_map/ppermute | solution.py:485
  35.5 1.6 %collective-permute-start.8 = (f32[32,2,8,128]{3,2,1,0:T(8,128)S(1)}, f32[32,2,8,128]{3,2,1,0:T(8,128)S(1)}, u32[]{:S(2)}, u32[]{:S(2)}) collective-permute-start(f32[32,2,8,128]{3,2,1,0:T(8,128)S(1)} %all_to_all.10.refs_2_), channel_id=1, source_target_pairs={{0,4},{4,0},{8,12},{12,8},{16,20},{20,16},{24,28},{28,24},{1,5},{5... | collective-permute-start | bytes 786440 | tf_op jit(solution)/shard_map/ppermute | solution.py:548
  53.0 1.3 %collective-permute-start.9 = (f32[32,1,8,128]{3,2,1,0:T(8,128)S(1)}, f32[32,1,8,128]{3,2,1,0:T(8,128)S(1)}, u32[]{:S(2)}, u32[]{:S(2)}) collective-permute-start(f32[32,1,8,128]{3,2,1,0:T(8,128)S(1)} %all_to_all.11.refs_2_), channel_id=1, source_target_pairs={{0,4},{4,0},{8,12},{12,8},{16,20},{20,16},{24,28},{28,24},{1,5},{5... | collective-permute-start | bytes 393224 | tf_op jit(solution)/shard_map/ppermute | solution.py:548

commit v8 on v7

--- a/solution.py
+++ b/solution.py
@@ -77,16 +77,17 @@
 
 def weights(k, west, east, south, north, z_factor):
     layer = iota_of(k, -2)
-    west, east, south, north = (0.5 * (k + other) for other in (west, east, south, north))
-    half = 0.5 * z_factor
+    west, east, south, north = (k + other for other in (west, east, south, north))
     axis = k.ndim - 2
-    down = jnp.where(layer == 0, 0.0, half * (k + shifted(k, 1, axis)))
-    up = jnp.where(layer == k.shape[axis] - 1, 0.0, half * (k + shifted(k, -1, axis)))
+    down = jnp.where(layer == 0, 0.0, z_factor * (k + shifted(k, 1, axis)))
+    up = jnp.where(layer == k.shape[axis] - 1, 0.0, z_factor * (k + shifted(k, -1, axis)))
     diagonal = west + east + south + north + down + up
-    inside = k > 0.0
-    inverse = jnp.where(inside, relaxation / jnp.where(inside, diagonal, 1.0), 0.0)
+    rough = pl.reciprocal(diagonal, approx=True)
+    rough = rough * (2.0 - diagonal * rough)
+    inverse = rough * (2.0 * relaxation - relaxation * (diagonal * rough))
+    inverse = jnp.where(k > 0.0, inverse, 0.0)
     scaled = [inverse * face for face in (west, east, south, north, down, up)]
-    return scaled + [(1.0 / relaxation) * diagonal, inverse]
+    return scaled + [(0.5 / relaxation) * diagonal, 2.0 * inverse]
 
 
 def fine_coefficients(k_ref, s_ref, co, g_ref, low, high, chunk):
@@ -168,9 +169,9 @@
 FINE_CHUNK = 80
 CHUNK = 64
 DOWN_CHUNK = 36
-FINE_SET = 19
-MID_SET = 18
-LOW_SET = 32
+FINE_SET = 80
+MID_SET = 40
+LOW_SET = 64
 ADD_CHUNK = 15
 
 
@@ -188,7 +189,7 @@
 PAIRS = HALO // 2
 
 
-def cut_kernel(rows, place_ref, both, own, xa, xb, ya, yb, aa, ab, ba, bb):
+def cut_kernel(rows, place_ref, both, own, xa, xb, ya, yb, ba, bb):
     layers = own.shape[2]
     pick = [[pl.ds(which * layers * rows + r, layers, stride=rows) for which in range(2)] for r in range(rows)]
     left = jnp.concatenate(
@@ -218,18 +219,18 @@
         last = left if g == 0 else jnp.where(slot == LEFT_SLOT[g] % 4, left, last)
     ya[...] = jnp.where(even_y, last, first)
     yb[...] = jnp.where(even_y, first, last)
-    for columns, with_a, with_b in ((ya, aa, ba), (yb, ab, bb)):
-        with_a[...] = columns[pl.ds(low // 2, PAIRS)]
-        with_b[...] = columns[pl.ds(high // 2, PAIRS)]
+    ba[...] = ya[pl.ds(high // 2, PAIRS)]
+    bb[...] = yb[pl.ds(high // 2, PAIRS)]
 
 
 def widen(rows, place_ref, own, xa, xb, ya, yb, aa, ab, ba, bb, s_ref, k_ref):
     even_x, even_y = place_ref[0] == 0, place_ref[1] == 0
     inner_x, inner_y = place_ref[4] != 0, place_ref[5] != 0
     inner_both = jnp.logical_and(inner_x, inner_y)
-    xa, ya, aa = xa[...], ya[...], aa[...]
+    beside = pl.ds(jnp.where(even_x, 0, rows // 2 - PAIRS), PAIRS)
+    xa, ya, aa, ab = xa[...], ya[...], aa[beside], ab[beside]
     xb, ba = (jnp.where(inner_x, ref[...], 0.0) for ref in (xb, ba))
-    yb, ab = (jnp.where(inner_y, ref[...], 0.0) for ref in (yb, ab))
+    yb, ab = (jnp.where(inner_y, part, 0.0) for part in (yb[...], ab))
     bb = jnp.where(inner_both, bb[...], 0.0)
     before = [jnp.where(even_x, b, a) for a, b in ((aa, ba), (ab, bb))]
     after = [jnp.where(even_x, a, b) for a, b in ((aa, ba), (ab, bb))]
@@ -361,8 +362,12 @@
 def strip_sums(values, strips_ref, rows2, scratch):
     whole = values[pl.ds(PAD, rows2)]
     row = iota_of(whole, 0)
-    for index, (start, end) in enumerate(strips(strips_ref)):
-        scratch[index] = jnp.sum(jnp.where((row >= start) & (row < end), whole, 0.0), axis=0)
+    before = 0.0
+    last = scratch.shape[0] - 1
+    for index, (_, end) in enumerate(strips(strips_ref)):
+        until = jnp.sum(whole if index == last else jnp.where(row < end, whole, 0.0), axis=0)
+        scratch[index] = until - before
+        before = until
     total = jnp.sum(jnp.sum(scratch[...], axis=2, keepdims=True), axis=1, keepdims=True)
     return jnp.broadcast_to(total, scratch.shape)
 
@@ -473,7 +478,7 @@
         out[pl.ds(r, layers, stride=rows), :] = natural[r * layers : (r + 1) * layers]
 
 
-def neighbour_swaps(xa, xb, ya, yb, aa, ab, ba, bb):
+def neighbour_swaps(xa, xb, ya, yb, ba, bb):
     npx, npy = lax.axis_size("px"), lax.axis_size("py")
 
     def swap(block, partner):
@@ -494,12 +499,12 @@
 
     ya = swap(ya, lambda x, y, inner_x, inner_y: (x, y ^ 1))
     xa = swap(xa, lambda x, y, inner_x, inner_y: (x ^ 1, y))
-    aa = swap(aa, lambda x, y, inner_x, inner_y: (x ^ 1, y ^ 1))
     yb = swap(yb, lambda x, y, inner_x, inner_y: (x, far(y)) if inner_y else (x ^ 1, y))
-    ab = swap(ab, lambda x, y, inner_x, inner_y: (x ^ 1, far(y) if inner_y else y))
-    ba = swap(ba, lambda x, y, inner_x, inner_y: (far(x) if inner_x else x, y ^ 1))
     xb = swap(xb, lambda x, y, inner_x, inner_y: (far(x), y) if inner_x else (x, y ^ 1))
     bb = swap(bb, corner)
+    ba, xa = lax.optimization_barrier((ba, xa))
+    ba = swap(ba, lambda x, y, inner_x, inner_y: (far(x) if inner_x else x, y ^ 1))
+    aa, ab = (swap(part, lambda x, y, inner_x, inner_y: (x ^ 1, y)) for part in (ya, yb))
     return xa, xb, ya, yb, aa, ab, ba, bb
 
 
@@ -534,7 +539,7 @@
 
     both = jnp.stack([source, coefficient]).reshape(2 * layers * rows, LANES)
     own, *sent = call(
-        cut_kernel, "cut", 1, 1, (arr(rows, 2, layers, LANES),) + (halo,) * 2 + (columns,) * 2 + (corner,) * 4, ()
+        cut_kernel, "cut", 1, 1, (arr(rows, 2, layers, LANES),) + (halo,) * 2 + (columns,) * 2 + (corner,) * 2, ()
     )(place, both)
     fine_u, fine_g, fine_co, mid_v, mid_g, mid_co, packed = call(
         descend_kernel, "descend", 1, 9, (fine, fine, fine_cos, mid, mid, mid_cos, arr(2, 2, layers, LANES)),

time: 58.1 us -> 56.8 us (0.978)
  blocking collectives: 29.2 us -> 25.6 us
  waiting for transfers between devices: 5.49 us -> 8.49 us
  Pallas kernels: 12.9 us -> 12.3 us
    all_to_all x2, blocking collectives: 29.2 us -> 25.6 us  [gather(): half = lax.all_to_all(every, ('px', 'py'), 0, 0, tiled=True)]
    ppermute x8, waiting for transfers between devices: 2.99 us -> 5.98 us  [swap(): return lax.ppermute(block, ('px', 'py'), pairs)]
  transfers between devices with their start and end apart: 10 -> 10, of which waited for: 5 -> 4; matrix products, arithmetic and copies ran while one was open for 0% -> 0% of each run, Pallas kernels for 0% -> 0%
where the time goes in v8:
time: 56.8 us; the launch traced here: 56.7 us
  blocking collectives  25.6 us (45%)
  Pallas kernels  12.3 us (22%)
  starting transfers between devices  9 us (16%)
  waiting for transfers between devices  8.49 us (15%)
  other arithmetic  1 us (2%)
    all_to_all x2, blocking collectives, gather(): half = lax.all_to_all(every, ('px', 'py'), 0, 0, tiled=True)  25.6 us
    ppermute x8, starting transfers between devices, swap(): return lax.ppermute(block, ('px', 'py'), pairs)  8.6 us
    ppermute x8, waiting for transfers between devices, swap(): return lax.ppermute(block, ('px', 'py'), pairs)  5.98 us
    pallas_call x1, Pallas kernels, shards(): call(sized(middle_kernel), 'middle', 2, 8, (fine, mid, mid, arr(2, 1, lay...  4.75 us
    pallas_call x1, Pallas kernels, shards(): call(sized(last_kernel), 'last', 2, 10, arr(layers * rows, LANES), (low,...  3.47 us
    pallas_call x1, Pallas kernels, shards(): call(descend_kernel, 'descend', 1, 9, (fine, fine, fine_cos, mid, mid, mi...  3.12 us
    ppermute x2, waiting for transfers between devices, gather(): return (half, lax.ppermute(half, 'px', [(i, i ^ 1) for i in range(npx)]))  2.51 us
  transfers between devices with their start and end apart: 10, of which 4 were waited for; matrix products, arithmetic and copies ran while one was open for 0% of the time, Pallas kernels for 0%

profile of v8, /device:TPU:0, one launch (start us, length us, event | category | flops | bytes accessed | tf_op | source)
XLA Modules:
  0.0 56.7 jit_solution(18294238490858658125)
XLA Ops:
  0.0 0.0 copy-start
  0.0 1.0 %pad_maximum_fusion = f32[2,8,32,128]{3,2,1,0:T(8,128)S(1)} fusion(f32[1,8,32,128]{3,2,1,0:T(8,128)} %bitcast.17, f32[1,8,32,128]{3,2,1,0:T(8,128)} %bitcast.18), kind=kLoop, calls=%fused_computation | loop fusion | flops 65536 | bytes 524288 | tf_op jit(solution)/shard_map/stack | solution.py:540
  1.0 0.1 stack.44.place_ref.refs_0_
  1.1 1.0 %cut.1 = (f32[32,2,8,128]{3,2,1,0:T(8,128)S(1)}, f32[24,2,8,128]{3,2,1,0:T(8,128)S(1)}, f32[24,2,8,128]{3,2,1,0:T(8,128)S(1)}, f32[16,8,128]{2,1,0:T(8,128)S(1)}...) custom-call(s32[6]{0:T(128)S(1)} %stack.44.place_ref.refs_0_, ...), custom_call_target="tpu_custom_call" | custom-call | tf_op jit(solution)/shard_map/cut/pallas_call | solution.py:541
  2.1 0.5 collective-permute-start
  2.6 2.6 %collective-permute-start.1 = (f32[24,2,8,128]{3,2,1,0:T(8,128)S(1)}, f32[24,2,8,128]{3,2,1,0:T(8,128)S(1)}, u32[]{:S(2)}, u32[]{:S(2)}) collective-permute-start(f32[24,2,8,128]{3,2,1,0:T(8,128)S(1)} %get-tuple-element.31), channel_id=1, source_target_pairs={{0,1},{1,0},{2,3},{3,2},{4,8},{5,9},{6,10},{7,11},{8,4},{9,5},{10,... | collective-permute-start | bytes 589832 | tf_op jit(solution)/shard_map/ppermute | solution.py:490
  5.3 0.1 collective-permute-start.2
  5.4 1.2 %collective-permute-start.3 = (f32[16,8,128]{2,1,0:T(8,128)S(1)}, f32[16,8,128]{2,1,0:T(8,128)S(1)}, u32[]{:S(2)}, u32[]{:S(2)}) collective-permute-start(f32[16,8,128]{2,1,0:T(8,128)S(1)} %get-tuple-element.33), channel_id=1, source_target_pairs={{0,4},{1,2},{2,1},{3,7},{4,0},{5,6},{6,5},{7,3},{8,12},{9,10},{10,... | collective-permute-start | bytes 196616 | tf_op jit(solution)/shard_map/ppermute | solution.py:490
  6.6 3.7 %collective-permute-done.2.ya = f32[16,8,128]{2,1,0:T(8,128)S(1)} collective-permute-done((f32[16,8,128]{2,1,0:T(8,128)S(1)}, f32[16,8,128]{2,1,0:T(8,128)S(1)}, u32[]{:S(2)}, u32[]{:S(2)}) %collective-permute-start.2) | collective-permute-done | bytes 65568 | tf_op jit(solution)/shard_map/ppermute | solution.py:490
  10.3 0.0 collective-permute-start.4
  10.3 0.0 collective-permute-done.3.yb
  10.3 0.5 collective-permute-start.5
  10.8 0.0 collective-permute-start.7
  10.9 0.0 collective-permute-done.xa
  10.9 3.6 %collective-permute-start.6 = (f32[12,8,128]{2,1,0:T(8,128)S(1)}, f32[12,8,128]{2,1,0:T(8,128)S(1)}, u32[]{:S(2)}, u32[]{:S(2)}) collective-permute-start(f32[12,8,128]{2,1,0:T(8,128)S(1)} %get-tuple-element.34), channel_id=1, source_target_pairs={{0,1},{1,0},{2,3},{3,2},{4,9},{5,8},{6,11},{7,10},{8,5},{9,4},{10,... | collective-permute-start | bytes 147464 | tf_op jit(solution)/shard_map/ppermute | solution.py:490
  14.4 0.0 collective-permute-done.7.bb
  14.5 0.0 collective-permute-done.4.aa
  14.5 0.0 collective-permute-done.5.ab
  14.5 0.0 collective-permute-done.1.xb
  14.5 2.2 %collective-permute-done.6.ba = f32[12,8,128]{2,1,0:T(8,128)S(1)} collective-permute-done((f32[12,8,128]{2,1,0:T(8,128)S(1)}, f32[12,8,128]{2,1,0:T(8,128)S(1)}, u32[]{:S(2)}, u32[]{:S(2)}) %collective-permute-start.6) | collective-permute-done | bytes 49184 | tf_op jit(solution)/shard_map/ppermute | solution.py:490
  16.7 3.1 %descend.1 = (f32[80,2,8,128]{3,2,1,0:T(8,128)S(1)}, f32[80,2,8,128]{3,2,1,0:T(8,128)S(1)}, f32[7,80,2,8,128]{4,3,2,1,0:T(8,128)S(1)}, f32[40,8,128]{2,1,0:T(8,1...) custom-call(s32[6]{0:T(128)S(1)} %stack.44.place_ref.refs_0_, ...), custom_call_target="tpu_custom_call" | custom-call | tf_op jit(solution)/shard_map/descend/pallas_call | solution.py:544
  19.9 14.7 %all_to_all.10.refs_2_ = f32[32,2,8,128]{3,2,1,0:T(8,128)S(1)} all-to-all(f32[32,2,8,128]{3,2,1,0:T(8,128)S(1)} %bitcast.15), channel_id=1, replica_groups=mesh['px'=8,'py'=4] {'px','py'}, dimensions={0} | all-to-all | bytes 524288 | tf_op jit(solution)/shard_map/all_to_all | solution.py:552
  34.6 0.4 collective-permute-start.8
  35.0 1.2 %collective-permute-done.8.refs_3_ = f32[32,2,8,128]{3,2,1,0:T(8,128)S(1)} collective-permute-done((f32[32,2,8,128]{3,2,1,0:T(8,128)S(1)}, f32[32,2,8,128]{3,2,1,0:T(8,128)S(1)}, u32[]{:S(2)}, u32[]{:S(2)}) %collective-permute-start.8) | collective-permute-done | bytes 262176 | tf_op jit(solution)/shard_map/ppermute | solution.py:553
  36.2 0.0 copy-done
  36.2 4.7 %middle.1 = (f32[80,2,8,128]{3,2,1,0:T(8,128)S(1)}, f32[40,8,128]{2,1,0:T(8,128)S(1)}, f32[40,8,128]{2,1,0:T(8,128)S(1)}, f32[2,1,8,128]{3,2,1,0:T(8,128)S(1)}, ...) custom-call(s32[6]{0:T(128)S(1)} %stack.44.place_ref.refs_0_, s32[4]{0:T(128)S(1)} %copy-done, ...), custom_call_target="tpu_custom_call" | custom-call | tf_op jit(solution)/shard_map/middle/pallas_call | solution.py:558
  40.9 10.9 %all_to_all.11.refs_2_ = f32[32,1,8,128]{3,2,1,0:T(8,128)S(1)} all-to-all(f32[32,1,8,128]{3,2,1,0:T(8,128)S(1)} %bitcast.16), channel_id=1, replica_groups=mesh['px'=8,'py'=4] {'px','py'}, dimensions={0} | all-to-all | bytes 262144 | tf_op jit(solution)/shard_map/all_to_all | solution.py:552
  51.8 0.0 collective-permute-start.9
  51.8 1.3 %collective-permute-done.9.refs_3_ = f32[32,1,8,128]{3,2,1,0:T(8,128)S(1)} collective-permute-done((f32[32,1,8,128]{3,2,1,0:T(8,128)S(1)}, f32[32,1,8,128]{3,2,1,0:T(8,128)S(1)}, u32[]{:S(2)}, u32[]{:S(2)}) %collective-permute-start.9) | collective-permute-done | bytes 131104 | tf_op jit(solution)/shard_map/ppermute | solution.py:553
  53.2 3.5 %last.1 = f32[256,128]{1,0:T(8,128)} custom-call(s32[6]{0:T(128)S(1)} %stack.44.place_ref.refs_0_, s32[4]{0:T(128)S(1)} %copy-done, f32[32,1,8,128]{3,2,1,0:T(8,128)S(1)} %all_to_all.11.refs_2_, f32[32,1,8,128]{3,2,1,0:T(8,128)S(1)} %collective-permute-done.9.refs_3_, f32[80,2,8,128]{3,2,1,0:T(8,128)S(1)} %get-tuple-element.44.refs_4_, ...), custom_call_target="tpu_custom_call" | custom-call | tf_op jit(solution)/shard_map/last/pallas_call | solution.py:562
  (2 shorter events, 0.0 us)
Async XLA Ops:
  0.0 36.2 %copy-start = (s32[4]{0:T(128)S(1)}, s32[4]{0:T(128)}, u32[]{:S(2)}) copy-start(s32[4]{0:T(128)} %refs_1_.3) | copy-start | bytes 52
  2.1 8.7 %collective-permute-start = (f32[24,2,8,128]{3,2,1,0:T(8,128)S(1)}, f32[24,2,8,128]{3,2,1,0:T(8,128)S(1)}, u32[]{:S(2)}, u32[]{:S(2)}) collective-permute-start(f32[24,2,8,128]{3,2,1,0:T(8,128)S(1)} %get-tuple-element.29), channel_id=1, source_target_pairs={{0,4},{1,5},{2,6},{3,7},{4,0},{5,1},{6,2},{7,3},{8,12},{9,13},{10,... | collective-permute-start | bytes 589832 | tf_op jit(solution)/shard_map/ppermute | solution.py:490
  2.6 11.8 %collective-permute-start.1 = (f32[24,2,8,128]{3,2,1,0:T(8,128)S(1)}, f32[24,2,8,128]{3,2,1,0:T(8,128)S(1)}, u32[]{:S(2)}, u32[]{:S(2)}) collective-permute-start(f32[24,2,8,128]{3,2,1,0:T(8,128)S(1)} %get-tuple-element.31), channel_id=1, source_target_pairs={{0,1},{1,0},{2,3},{3,2},{4,8},{5,9},{6,10},{7,11},{8,4},{9,5},{10,... | collective-permute-start | bytes 589832 | tf_op jit(solution)/shard_map/ppermute | solution.py:490
  5.3 5.1 %collective-permute-start.2 = (f32[16,8,128]{2,1,0:T(8,128)S(1)}, f32[16,8,128]{2,1,0:T(8,128)S(1)}, u32[]{:S(2)}, u32[]{:S(2)}) collective-permute-start(f32[16,8,128]{2,1,0:T(8,128)S(1)} %get-tuple-element.32), channel_id=1, source_target_pairs={{0,1},{1,0},{2,3},{3,2},{4,5},{5,4},{6,7},{7,6},{8,9},{9,8},{10,11... | collective-permute-start | bytes 196616 | tf_op jit(solution)/shard_map/ppermute | solution.py:490
  5.4 5.0 %collective-permute-start.3 = (f32[16,8,128]{2,1,0:T(8,128)S(1)}, f32[16,8,128]{2,1,0:T(8,128)S(1)}, u32[]{:S(2)}, u32[]{:S(2)}) collective-permute-start(f32[16,8,128]{2,1,0:T(8,128)S(1)} %get-tuple-element.33), channel_id=1, source_target_pairs={{0,4},{1,2},{2,1},{3,7},{4,0},{5,6},{6,5},{7,3},{8,12},{9,10},{10,... | collective-permute-start | bytes 196616 | tf_op jit(solution)/shard_map/ppermute | solution.py:490
  10.3 4.1 %collective-permute-start.4 = (f32[16,8,128]{2,1,0:T(8,128)S(1)}, f32[16,8,128]{2,1,0:T(8,128)S(1)}, u32[]{:S(2)}, u32[]{:S(2)}) collective-permute-start(f32[16,8,128]{2,1,0:T(8,128)S(1)} %collective-permute-done.2.ya), channel_id=1, source_target_pairs={{0,4},{1,5},{2,6},{3,7},{4,0},{5,1},{6,2},{7,3},{8,12},{9,13},{10,... | collective-permute-start | bytes 196616 | tf_op jit(solution)/shard_map/ppermute | solution.py:490
  10.3 4.1 %collective-permute-start.5 = (f32[16,8,128]{2,1,0:T(8,128)S(1)}, f32[16,8,128]{2,1,0:T(8,128)S(1)}, u32[]{:S(2)}, u32[]{:S(2)}) collective-permute-start(f32[16,8,128]{2,1,0:T(8,128)S(1)} %collective-permute-done.3.yb), channel_id=1, source_target_pairs={{0,4},{1,5},{2,6},{3,7},{4,0},{5,1},{6,2},{7,3},{8,12},{9,13},{10,... | collective-permute-start | bytes 196616 | tf_op jit(solution)/shard_map/ppermute | solution.py:490
  10.8 3.6 %collective-permute-start.7 = (f32[12,8,128]{2,1,0:T(8,128)S(1)}, f32[12,8,128]{2,1,0:T(8,128)S(1)}, u32[]{:S(2)}, u32[]{:S(2)}) collective-permute-start(f32[12,8,128]{2,1,0:T(8,128)S(1)} %get-tuple-element.35), channel_id=1, source_target_pairs={{0,4},{1,2},{2,1},{3,7},{4,0},{5,10},{6,9},{7,3},{8,12},{9,6},{10,... | collective-permute-start | bytes 147464 | tf_op jit(solution)/shard_map/ppermute | solution.py:490
  10.9 5.9 %collective-permute-start.6 = (f32[12,8,128]{2,1,0:T(8,128)S(1)}, f32[12,8,128]{2,1,0:T(8,128)S(1)}, u32[]{:S(2)}, u32[]{:S(2)}) collective-permute-start(f32[12,8,128]{2,1,0:T(8,128)S(1)} %get-tuple-element.34), channel_id=1, source_target_pairs={{0,1},{1,0},{2,3},{3,2},{4,9},{5,8},{6,11},{7,10},{8,5},{9,4},{10,... | collective-permute-start | bytes 147464 | tf_op jit(solution)/shard_map/ppermute | solution.py:490
  34.6 1.6 %collective-permute-start.8 = (f32[32,2,8,128]{3,2,1,0:T(8,128)S(1)}, f32[32,2,8,128]{3,2,1,0:T(8,128)S(1)}, u32[]{:S(2)}, u32[]{:S(2)}) collective-permute-start(f32[32,2,8,128]{3,2,1,0:T(8,128)S(1)} %all_to_all.10.refs_2_), channel_id=1, source_target_pairs={{0,4},{4,0},{8,12},{12,8},{16,20},{20,16},{24,28},{28,24},{1,5},{5... | collective-permute-start | bytes 786440 | tf_op jit(solution)/shard_map/ppermute | solution.py:553
  51.8 1.3 %collective-permute-start.9 = (f32[32,1,8,128]{3,2,1,0:T(8,128)S(1)}, f32[32,1,8,128]{3,2,1,0:T(8,128)S(1)}, u32[]{:S(2)}, u32[]{:S(2)}) collective-permute-start(f32[32,1,8,128]{3,2,1,0:T(8,128)S(1)} %all_to_all.11.refs_2_), channel_id=1, source_target_pairs={{0,4},{4,0},{8,12},{12,8},{16,20},{20,16},{24,28},{28,24},{1,5},{5... | collective-permute-start | bytes 393224 | tf_op jit(solution)/shard_map/ppermute | solution.py:553

commit v9 on v8

--- a/solution.py
+++ b/solution.py
@@ -172,7 +172,9 @@
 FINE_SET = 80
 MID_SET = 40
 LOW_SET = 64
-ADD_CHUNK = 15
+ADD_CHUNK = 40
+K1_CHUNK = 40
+BLOCKS = 8
 
 
 def coarse_rows(values, place_ref):
@@ -271,7 +273,7 @@
         here = pl.ds(2 * at, 2 * size)
         k1[pl.ds(at, size)] = 0.25 * pair_sum_rows(k_ref[here, 0] + k_ref[here, 1])
 
-    rows_loop(0, half, 20, coarser)
+    rows_loop(0, half, K1_CHUNK, coarser)
     fine_coefficients(k_ref, s_ref, fine_co, fine_g, h0 - 22, h0 + rows + 22, FINE_SET)
     mid_coefficients(k1, mid_co, h1 - 10, h1 + m + 10, MID_SET)
     descend(rows, place_ref, fine_g, fine_u, fine_g, fine_co, mid_v, mid_g, mid_co, 10, packed, k1[pl.ds(h1, m)])
@@ -302,7 +304,7 @@
     even_x = place_ref[0] == 0
     per = 4
     width = LANES // per
-    group_of = 4 if npx % 4 == 0 else 1
+    group_of = BLOCKS if npx % BLOCKS == 0 else 1
 
     def body(step, carry):
         for i in range(group_of):
@@ -325,7 +327,10 @@
                         target[at, :, lanes] = row
         return carry
 
-    lax.fori_loop(0, npx // group_of, body, 0)
+    if npx == group_of:
+        body(0, 0)
+    else:
+        lax.fori_loop(0, npx // group_of, body, 0)
 
 
 def coarse_coefficients(rows2, strips_ref, k2, co, sums):
@@ -501,8 +506,8 @@
     xa = swap(xa, lambda x, y, inner_x, inner_y: (x ^ 1, y))
     yb = swap(yb, lambda x, y, inner_x, inner_y: (x, far(y)) if inner_y else (x ^ 1, y))
     xb = swap(xb, lambda x, y, inner_x, inner_y: (far(x), y) if inner_x else (x, y ^ 1))
+    ba, bb, xa = lax.optimization_barrier((ba, bb, xa))
     bb = swap(bb, corner)
-    ba, xa = lax.optimization_barrier((ba, xa))
     ba = swap(ba, lambda x, y, inner_x, inner_y: (far(x) if inner_x else x, y ^ 1))
     aa, ab = (swap(part, lambda x, y, inner_x, inner_y: (x ^ 1, y)) for part in (ya, yb))
     return xa, xb, ya, yb, aa, ab, ba, bb

time: 56.8 us -> 56 us (0.986)
  blocking collectives: 25.6 us -> 27.4 us
  starting transfers between devices: 9 us -> 7.6 us
  Pallas kernels: 12.3 us -> 11.5 us
    all_to_all x2, blocking collectives: 25.6 us -> 27.4 us  [gather(): half = lax.all_to_all(every, ('px', 'py'), 0, 0, tiled=True)]
    ppermute x8, starting transfers between devices: 8.6 us -> 7.2 us  [swap(): return lax.ppermute(block, ('px', 'py'), pairs)]
where the time goes in v9:
time: 56 us; the launch traced here: 55.8 us
  blocking collectives  27.4 us (49%)
  Pallas kernels  11.5 us (21%)
  waiting for transfers between devices  8.13 us (15%)
  starting transfers between devices  7.6 us (14%)
  other arithmetic  1 us (2%)
    all_to_all x2, blocking collectives, gather(): half = lax.all_to_all(every, ('px', 'py'), 0, 0, tiled=True)  27.4 us
    ppermute x8, starting transfers between devices, swap(): return lax.ppermute(block, ('px', 'py'), pairs)  7.2 us
    ppermute x8, waiting for transfers between devices, swap(): return lax.ppermute(block, ('px', 'py'), pairs)  5.63 us
    pallas_call x1, Pallas kernels, shards(): call(sized(middle_kernel), 'middle', 2, 8, (fine, mid, mid, arr(2, 1, lay...  4.22 us
    pallas_call x1, Pallas kernels, shards(): call(sized(last_kernel), 'last', 2, 10, arr(layers * rows, LANES), (low,...  3.23 us
    pallas_call x1, Pallas kernels, shards(): call(descend_kernel, 'descend', 1, 9, (fine, fine, fine_cos, mid, mid, mi...  3.07 us
    ppermute x2, waiting for transfers between devices, gather(): return (half, lax.ppermute(half, 'px', [(i, i ^ 1) for i in range(npx)]))  2.51 us
  transfers between devices with their start and end apart: 10, of which 4 were waited for; matrix products, arithmetic and copies ran while one was open for 0% of the time, Pallas kernels for 0%

profile of v9, /device:TPU:0, one launch (start us, length us, event | category | flops | bytes accessed | tf_op | source)
XLA Modules:
  0.0 55.8 jit_solution(4470463979375660799)
XLA Ops:
  0.0 0.0 copy-start
  0.0 1.0 %pad_maximum_fusion = f32[2,8,32,128]{3,2,1,0:T(8,128)S(1)} fusion(f32[1,8,32,128]{3,2,1,0:T(8,128)} %bitcast.17, f32[1,8,32,128]{3,2,1,0:T(8,128)} %bitcast.18), kind=kLoop, calls=%fused_computation | loop fusion | flops 65536 | bytes 524288 | tf_op jit(solution)/shard_map/stack | solution.py:545
  1.0 0.1 stack.44.place_ref.refs_0_
  1.1 1.0 %cut.1 = (f32[32,2,8,128]{3,2,1,0:T(8,128)S(1)}, f32[24,2,8,128]{3,2,1,0:T(8,128)S(1)}, f32[24,2,8,128]{3,2,1,0:T(8,128)S(1)}, f32[16,8,128]{2,1,0:T(8,128)S(1)}...) custom-call(s32[6]{0:T(128)S(1)} %stack.44.place_ref.refs_0_, ...), custom_call_target="tpu_custom_call" | custom-call | tf_op jit(solution)/shard_map/cut/pallas_call | solution.py:546
  2.1 0.5 collective-permute-start
  2.6 2.6 %collective-permute-start.1 = (f32[24,2,8,128]{3,2,1,0:T(8,128)S(1)}, f32[24,2,8,128]{3,2,1,0:T(8,128)S(1)}, u32[]{:S(2)}, u32[]{:S(2)}) collective-permute-start(f32[24,2,8,128]{3,2,1,0:T(8,128)S(1)} %get-tuple-element.33), channel_id=1, source_target_pairs={{0,1},{1,0},{2,3},{3,2},{4,8},{5,9},{6,10},{7,11},{8,4},{9,5},{10,... | collective-permute-start | bytes 589832 | tf_op jit(solution)/shard_map/ppermute | solution.py:495
  5.3 0.1 collective-permute-start.2
  5.4 1.2 %collective-permute-start.3 = (f32[16,8,128]{2,1,0:T(8,128)S(1)}, f32[16,8,128]{2,1,0:T(8,128)S(1)}, u32[]{:S(2)}, u32[]{:S(2)}) collective-permute-start(f32[16,8,128]{2,1,0:T(8,128)S(1)} %get-tuple-element.35), channel_id=1, source_target_pairs={{0,4},{1,2},{2,1},{3,7},{4,0},{5,6},{6,5},{7,3},{8,12},{9,10},{10,... | collective-permute-start | bytes 196616 | tf_op jit(solution)/shard_map/ppermute | solution.py:495
  6.6 3.7 %collective-permute-done.2.ya = f32[16,8,128]{2,1,0:T(8,128)S(1)} collective-permute-done((f32[16,8,128]{2,1,0:T(8,128)S(1)}, f32[16,8,128]{2,1,0:T(8,128)S(1)}, u32[]{:S(2)}, u32[]{:S(2)}) %collective-permute-start.2) | collective-permute-done | bytes 65568 | tf_op jit(solution)/shard_map/ppermute | solution.py:495
  10.3 0.0 collective-permute-start.4
  10.3 0.0 collective-permute-done.3.yb
  10.3 0.5 collective-permute-start.5
  10.8 0.0 collective-permute-done.xa
  10.9 2.0 %collective-permute-start.6 = (f32[12,8,128]{2,1,0:T(8,128)S(1)}, f32[12,8,128]{2,1,0:T(8,128)S(1)}, u32[]{:S(2)}, u32[]{:S(2)}) collective-permute-start(f32[12,8,128]{2,1,0:T(8,128)S(1)} %get-tuple-element.36), channel_id=1, source_target_pairs={{0,1},{1,0},{2,3},{3,2},{4,9},{5,8},{6,11},{7,10},{8,5},{9,4},{10,... | collective-permute-start | bytes 147464 | tf_op jit(solution)/shard_map/ppermute | solution.py:495
  12.9 0.2 collective-permute-start.7
  13.0 0.0 collective-permute-done.4.aa
  13.0 0.0 collective-permute-done.5.ab
  13.1 0.0 collective-permute-done.1.xb
  13.1 1.9 %collective-permute-done.6.ba = f32[12,8,128]{2,1,0:T(8,128)S(1)} collective-permute-done((f32[12,8,128]{2,1,0:T(8,128)S(1)}, f32[12,8,128]{2,1,0:T(8,128)S(1)}, u32[]{:S(2)}, u32[]{:S(2)}) %collective-permute-start.6) | collective-permute-done | bytes 49184 | tf_op jit(solution)/shard_map/ppermute | solution.py:495
  14.9 0.0 collective-permute-done.7.bb
  14.9 3.1 %descend.1 = (f32[80,2,8,128]{3,2,1,0:T(8,128)S(1)}, f32[80,2,8,128]{3,2,1,0:T(8,128)S(1)}, f32[7,80,2,8,128]{4,3,2,1,0:T(8,128)S(1)}, f32[40,8,128]{2,1,0:T(8,1...) custom-call(s32[6]{0:T(128)S(1)} %stack.44.place_ref.refs_0_, ...), custom_call_target="tpu_custom_call" | custom-call | tf_op jit(solution)/shard_map/descend/pallas_call | solution.py:549
  18.0 16.5 %all_to_all.10.refs_2_ = f32[32,2,8,128]{3,2,1,0:T(8,128)S(1)} all-to-all(f32[32,2,8,128]{3,2,1,0:T(8,128)S(1)} %bitcast.15), channel_id=1, replica_groups=mesh['px'=8,'py'=4] {'px','py'}, dimensions={0} | all-to-all | bytes 524288 | tf_op jit(solution)/shard_map/all_to_all | solution.py:557
  34.5 0.4 collective-permute-start.8
  34.9 1.2 %collective-permute-done.8.refs_3_ = f32[32,2,8,128]{3,2,1,0:T(8,128)S(1)} collective-permute-done((f32[32,2,8,128]{3,2,1,0:T(8,128)S(1)}, f32[32,2,8,128]{3,2,1,0:T(8,128)S(1)}, u32[]{:S(2)}, u32[]{:S(2)}) %collective-permute-start.8) | collective-permute-done | bytes 262176 | tf_op jit(solution)/shard_map/ppermute | solution.py:558
  36.1 0.0 copy-done
  36.1 4.2 %middle.1 = (f32[80,2,8,128]{3,2,1,0:T(8,128)S(1)}, f32[40,8,128]{2,1,0:T(8,128)S(1)}, f32[40,8,128]{2,1,0:T(8,128)S(1)}, f32[2,1,8,128]{3,2,1,0:T(8,128)S(1)}, ...) custom-call(s32[6]{0:T(128)S(1)} %stack.44.place_ref.refs_0_, s32[4]{0:T(128)S(1)} %copy-done, ...), custom_call_target="tpu_custom_call" | custom-call | tf_op jit(solution)/shard_map/middle/pallas_call | solution.py:563
  40.3 10.9 %all_to_all.11.refs_2_ = f32[32,1,8,128]{3,2,1,0:T(8,128)S(1)} all-to-all(f32[32,1,8,128]{3,2,1,0:T(8,128)S(1)} %bitcast.16), channel_id=1, replica_groups=mesh['px'=8,'py'=4] {'px','py'}, dimensions={0} | all-to-all | bytes 262144 | tf_op jit(solution)/shard_map/all_to_all | solution.py:557
  51.2 0.0 collective-permute-start.9
  51.2 1.3 %collective-permute-done.9.refs_3_ = f32[32,1,8,128]{3,2,1,0:T(8,128)S(1)} collective-permute-done((f32[32,1,8,128]{3,2,1,0:T(8,128)S(1)}, f32[32,1,8,128]{3,2,1,0:T(8,128)S(1)}, u32[]{:S(2)}, u32[]{:S(2)}) %collective-permute-start.9) | collective-permute-done | bytes 131104 | tf_op jit(solution)/shard_map/ppermute | solution.py:558
  52.6 3.2 %last.1 = f32[256,128]{1,0:T(8,128)} custom-call(s32[6]{0:T(128)S(1)} %stack.44.place_ref.refs_0_, s32[4]{0:T(128)S(1)} %copy-done, f32[32,1,8,128]{3,2,1,0:T(8,128)S(1)} %all_to_all.11.refs_2_, f32[32,1,8,128]{3,2,1,0:T(8,128)S(1)} %collective-permute-done.9.refs_3_, f32[80,2,8,128]{3,2,1,0:T(8,128)S(1)} %get-tuple-element.46.refs_4_, ...), custom_call_target="tpu_custom_call" | custom-call | tf_op jit(solution)/shard_map/last/pallas_call | solution.py:567
  (2 shorter events, 0.0 us)
Async XLA Ops:
  0.0 36.1 %copy-start = (s32[4]{0:T(128)S(1)}, s32[4]{0:T(128)}, u32[]{:S(2)}) copy-start(s32[4]{0:T(128)} %refs_1_.3) | copy-start | bytes 52
  2.1 8.7 %collective-permute-start = (f32[24,2,8,128]{3,2,1,0:T(8,128)S(1)}, f32[24,2,8,128]{3,2,1,0:T(8,128)S(1)}, u32[]{:S(2)}, u32[]{:S(2)}) collective-permute-start(f32[24,2,8,128]{3,2,1,0:T(8,128)S(1)} %get-tuple-element.31), channel_id=1, source_target_pairs={{0,4},{1,5},{2,6},{3,7},{4,0},{5,1},{6,2},{7,3},{8,12},{9,13},{10,... | collective-permute-start | bytes 589832 | tf_op jit(solution)/shard_map/ppermute | solution.py:495
  2.6 10.4 %collective-permute-start.1 = (f32[24,2,8,128]{3,2,1,0:T(8,128)S(1)}, f32[24,2,8,128]{3,2,1,0:T(8,128)S(1)}, u32[]{:S(2)}, u32[]{:S(2)}) collective-permute-start(f32[24,2,8,128]{3,2,1,0:T(8,128)S(1)} %get-tuple-element.33), channel_id=1, source_target_pairs={{0,1},{1,0},{2,3},{3,2},{4,8},{5,9},{6,10},{7,11},{8,4},{9,5},{10,... | collective-permute-start | bytes 589832 | tf_op jit(solution)/shard_map/ppermute | solution.py:495
  5.3 5.1 %collective-permute-start.2 = (f32[16,8,128]{2,1,0:T(8,128)S(1)}, f32[16,8,128]{2,1,0:T(8,128)S(1)}, u32[]{:S(2)}, u32[]{:S(2)}) collective-permute-start(f32[16,8,128]{2,1,0:T(8,128)S(1)} %get-tuple-element.34), channel_id=1, source_target_pairs={{0,1},{1,0},{2,3},{3,2},{4,5},{5,4},{6,7},{7,6},{8,9},{9,8},{10,11... | collective-permute-start | bytes 196616 | tf_op jit(solution)/shard_map/ppermute | solution.py:495
  5.4 5.0 %collective-permute-start.3 = (f32[16,8,128]{2,1,0:T(8,128)S(1)}, f32[16,8,128]{2,1,0:T(8,128)S(1)}, u32[]{:S(2)}, u32[]{:S(2)}) collective-permute-start(f32[16,8,128]{2,1,0:T(8,128)S(1)} %get-tuple-element.35), channel_id=1, source_target_pairs={{0,4},{1,2},{2,1},{3,7},{4,0},{5,6},{6,5},{7,3},{8,12},{9,10},{10,... | collective-permute-start | bytes 196616 | tf_op jit(solution)/shard_map/ppermute | solution.py:495
  10.3 2.7 %collective-permute-start.4 = (f32[16,8,128]{2,1,0:T(8,128)S(1)}, f32[16,8,128]{2,1,0:T(8,128)S(1)}, u32[]{:S(2)}, u32[]{:S(2)}) collective-permute-start(f32[16,8,128]{2,1,0:T(8,128)S(1)} %collective-permute-done.2.ya), channel_id=1, source_target_pairs={{0,4},{1,5},{2,6},{3,7},{4,0},{5,1},{6,2},{7,3},{8,12},{9,13},{10,... | collective-permute-start | bytes 196616 | tf_op jit(solution)/shard_map/ppermute | solution.py:495
  10.3 2.7 %collective-permute-start.5 = (f32[16,8,128]{2,1,0:T(8,128)S(1)}, f32[16,8,128]{2,1,0:T(8,128)S(1)}, u32[]{:S(2)}, u32[]{:S(2)}) collective-permute-start(f32[16,8,128]{2,1,0:T(8,128)S(1)} %collective-permute-done.3.yb), channel_id=1, source_target_pairs={{0,4},{1,5},{2,6},{3,7},{4,0},{5,1},{6,2},{7,3},{8,12},{9,13},{10,... | collective-permute-start | bytes 196616 | tf_op jit(solution)/shard_map/ppermute | solution.py:495
  10.9 4.1 %collective-permute-start.6 = (f32[12,8,128]{2,1,0:T(8,128)S(1)}, f32[12,8,128]{2,1,0:T(8,128)S(1)}, u32[]{:S(2)}, u32[]{:S(2)}) collective-permute-start(f32[12,8,128]{2,1,0:T(8,128)S(1)} %get-tuple-element.36), channel_id=1, source_target_pairs={{0,1},{1,0},{2,3},{3,2},{4,9},{5,8},{6,11},{7,10},{8,5},{9,4},{10,... | collective-permute-start | bytes 147464 | tf_op jit(solution)/shard_map/ppermute | solution.py:495
  12.9 2.1 %collective-permute-start.7 = (f32[12,8,128]{2,1,0:T(8,128)S(1)}, f32[12,8,128]{2,1,0:T(8,128)S(1)}, u32[]{:S(2)}, u32[]{:S(2)}) collective-permute-start(f32[12,8,128]{2,1,0:T(8,128)S(1)} %get-tuple-element.37), channel_id=1, source_target_pairs={{0,4},{1,2},{2,1},{3,7},{4,0},{5,10},{6,9},{7,3},{8,12},{9,6},{10,... | collective-permute-start | bytes 147464 | tf_op jit(solution)/shard_map/ppermute | solution.py:495
  34.5 1.6 %collective-permute-start.8 = (f32[32,2,8,128]{3,2,1,0:T(8,128)S(1)}, f32[32,2,8,128]{3,2,1,0:T(8,128)S(1)}, u32[]{:S(2)}, u32[]{:S(2)}) collective-permute-start(f32[32,2,8,128]{3,2,1,0:T(8,128)S(1)} %all_to_all.10.refs_2_), channel_id=1, source_target_pairs={{0,4},{4,0},{8,12},{12,8},{16,20},{20,16},{24,28},{28,24},{1,5},{5... | collective-permute-start | bytes 786440 | tf_op jit(solution)/shard_map/ppermute | solution.py:558
  51.2 1.3 %collective-permute-start.9 = (f32[32,1,8,128]{3,2,1,0:T(8,128)S(1)}, f32[32,1,8,128]{3,2,1,0:T(8,128)S(1)}, u32[]{:S(2)}, u32[]{:S(2)}) collective-permute-start(f32[32,1,8,128]{3,2,1,0:T(8,128)S(1)} %all_to_all.11.refs_2_), channel_id=1, source_target_pairs={{0,4},{4,0},{8,12},{12,8},{16,20},{20,16},{24,28},{28,24},{1,5},{5... | collective-permute-start | bytes 393224 | tf_op jit(solution)/shard_map/ppermute | solution.py:558

commit v10 on v9

--- a/solution.py
+++ b/solution.py
@@ -193,19 +193,11 @@
 
 def cut_kernel(rows, place_ref, both, own, xa, xb, ya, yb, ba, bb):
     layers = own.shape[2]
-    pick = [[pl.ds(which * layers * rows + r, layers, stride=rows) for which in range(2)] for r in range(rows)]
-    left = jnp.concatenate(
-        [jnp.concatenate([both[at, :] for at in pair], axis=1) for pair in pick], axis=0
-    )
-
-    def place(row, col):
-        y = row % LANES
-        return col == (row // LANES) * LANES + (y % 2) * HALF + y // 2
-
-    sorted_y = exact_dot(left, one_hot((2 * LANES, 2 * LANES), place))
+    order = one_hot((LANES, LANES), lambda row, col: col == (row % 2) * HALF + row // 2)
     parts = []
     for which in range(2):
-        part = sorted_y[:, which * LANES : (which + 1) * LANES].reshape(rows, layers, LANES)
+        natural = [both[pl.ds(which * layers * rows + r, layers, stride=rows), :] for r in range(rows)]
+        part = exact_dot(jnp.concatenate(natural, axis=0), order).reshape(rows, layers, LANES)
         own[:, which] = part
         pairs = part.reshape(rows // 2, 2, layers, LANES)
         parts += [pairs[:, 0], pairs[:, 1]]

time: 56 us -> 56 us (level)
  no operation moved by 1% of the time
where the time goes in v10:
time: 56 us; the launch traced here: 55.8 us
  blocking collectives  27.4 us (49%)
  Pallas kernels  11.6 us (21%)
  waiting for transfers between devices  8.13 us (15%)
  starting transfers between devices  7.6 us (14%)
  other arithmetic  1 us (2%)
    all_to_all x2, blocking collectives, gather(): half = lax.all_to_all(every, ('px', 'py'), 0, 0, tiled=True)  27.4 us
    ppermute x8, starting transfers between devices, swap(): return lax.ppermute(block, ('px', 'py'), pairs)  7.2 us
    ppermute x8, waiting for transfers between devices, swap(): return lax.ppermute(block, ('px', 'py'), pairs)  5.63 us
    pallas_call x1, Pallas kernels, shards(): call(sized(middle_kernel), 'middle', 2, 8, (fine, mid, mid, arr(2, 1, lay...  4.22 us
    pallas_call x1, Pallas kernels, shards(): call(sized(last_kernel), 'last', 2, 10, arr(layers * rows, LANES), (low,...  3.23 us
    pallas_call x1, Pallas kernels, shards(): call(descend_kernel, 'descend', 1, 9, (fine, fine, fine_cos, mid, mid, mi...  3.07 us
    ppermute x2, waiting for transfers between devices, gather(): return (half, lax.ppermute(half, 'px', [(i, i ^ 1) for i in range(npx)]))  2.51 us
  transfers between devices with their start and end apart: 10, of which 4 were waited for; matrix products, arithmetic and copies ran while one was open for 0% of the time, Pallas kernels for 0%

profile of v10, /device:TPU:0, one launch (start us, length us, event | category | flops | bytes accessed | tf_op | source)
XLA Modules:
  0.0 55.8 jit_solution(16446852393247489947)
XLA Ops:
  0.0 0.0 copy-start
  0.0 1.0 %pad_maximum_fusion = f32[2,8,32,128]{3,2,1,0:T(8,128)S(1)} fusion(f32[1,8,32,128]{3,2,1,0:T(8,128)} %bitcast.17, f32[1,8,32,128]{3,2,1,0:T(8,128)} %bitcast.18), kind=kLoop, calls=%fused_computation | loop fusion | flops 65536 | bytes 524288 | tf_op jit(solution)/shard_map/stack | solution.py:537
  1.0 0.1 stack.44.place_ref.refs_0_
  1.1 1.0 %cut.1 = (f32[32,2,8,128]{3,2,1,0:T(8,128)S(1)}, f32[24,2,8,128]{3,2,1,0:T(8,128)S(1)}, f32[24,2,8,128]{3,2,1,0:T(8,128)S(1)}, f32[16,8,128]{2,1,0:T(8,128)S(1)}...) custom-call(s32[6]{0:T(128)S(1)} %stack.44.place_ref.refs_0_, ...), custom_call_target="tpu_custom_call" | custom-call | tf_op jit(solution)/shard_map/cut/pallas_call | solution.py:538
  2.1 0.5 collective-permute-start
  2.7 2.6 %collective-permute-start.1 = (f32[24,2,8,128]{3,2,1,0:T(8,128)S(1)}, f32[24,2,8,128]{3,2,1,0:T(8,128)S(1)}, u32[]{:S(2)}, u32[]{:S(2)}) collective-permute-start(f32[24,2,8,128]{3,2,1,0:T(8,128)S(1)} %get-tuple-element.33), channel_id=1, source_target_pairs={{0,1},{1,0},{2,3},{3,2},{4,8},{5,9},{6,10},{7,11},{8,4},{9,5},{10,... | collective-permute-start | bytes 589832 | tf_op jit(solution)/shard_map/ppermute | solution.py:487
  5.3 0.1 collective-permute-start.2
  5.4 1.2 %collective-permute-start.3 = (f32[16,8,128]{2,1,0:T(8,128)S(1)}, f32[16,8,128]{2,1,0:T(8,128)S(1)}, u32[]{:S(2)}, u32[]{:S(2)}) collective-permute-start(f32[16,8,128]{2,1,0:T(8,128)S(1)} %get-tuple-element.35), channel_id=1, source_target_pairs={{0,4},{1,2},{2,1},{3,7},{4,0},{5,6},{6,5},{7,3},{8,12},{9,10},{10,... | collective-permute-start | bytes 196616 | tf_op jit(solution)/shard_map/ppermute | solution.py:487
  6.6 3.7 %collective-permute-done.2.ya = f32[16,8,128]{2,1,0:T(8,128)S(1)} collective-permute-done((f32[16,8,128]{2,1,0:T(8,128)S(1)}, f32[16,8,128]{2,1,0:T(8,128)S(1)}, u32[]{:S(2)}, u32[]{:S(2)}) %collective-permute-start.2) | collective-permute-done | bytes 65568 | tf_op jit(solution)/shard_map/ppermute | solution.py:487
  10.4 0.0 collective-permute-start.4
  10.4 0.0 collective-permute-done.3.yb
  10.4 0.5 collective-permute-start.5
  10.9 0.0 collective-permute-done.xa
  10.9 2.0 %collective-permute-start.6 = (f32[12,8,128]{2,1,0:T(8,128)S(1)}, f32[12,8,128]{2,1,0:T(8,128)S(1)}, u32[]{:S(2)}, u32[]{:S(2)}) collective-permute-start(f32[12,8,128]{2,1,0:T(8,128)S(1)} %get-tuple-element.36), channel_id=1, source_target_pairs={{0,1},{1,0},{2,3},{3,2},{4,9},{5,8},{6,11},{7,10},{8,5},{9,4},{10,... | collective-permute-start | bytes 147464 | tf_op jit(solution)/shard_map/ppermute | solution.py:487
  12.9 0.2 collective-permute-start.7
  13.1 0.0 collective-permute-done.4.aa
  13.1 0.0 collective-permute-done.5.ab
  13.1 0.0 collective-permute-done.1.xb
  13.1 1.9 %collective-permute-done.6.ba = f32[12,8,128]{2,1,0:T(8,128)S(1)} collective-permute-done((f32[12,8,128]{2,1,0:T(8,128)S(1)}, f32[12,8,128]{2,1,0:T(8,128)S(1)}, u32[]{:S(2)}, u32[]{:S(2)}) %collective-permute-start.6) | collective-permute-done | bytes 49184 | tf_op jit(solution)/shard_map/ppermute | solution.py:487
  15.0 0.0 collective-permute-done.7.bb
  15.0 3.1 %descend.1 = (f32[80,2,8,128]{3,2,1,0:T(8,128)S(1)}, f32[80,2,8,128]{3,2,1,0:T(8,128)S(1)}, f32[7,80,2,8,128]{4,3,2,1,0:T(8,128)S(1)}, f32[40,8,128]{2,1,0:T(8,1...) custom-call(s32[6]{0:T(128)S(1)} %stack.44.place_ref.refs_0_, ...), custom_call_target="tpu_custom_call" | custom-call | tf_op jit(solution)/shard_map/descend/pallas_call | solution.py:541
  18.1 16.5 %all_to_all.10.refs_2_ = f32[32,2,8,128]{3,2,1,0:T(8,128)S(1)} all-to-all(f32[32,2,8,128]{3,2,1,0:T(8,128)S(1)} %bitcast.15), channel_id=1, replica_groups=mesh['px'=8,'py'=4] {'px','py'}, dimensions={0} | all-to-all | bytes 524288 | tf_op jit(solution)/shard_map/all_to_all | solution.py:549
  34.5 0.4 collective-permute-start.8
  34.9 1.2 %collective-permute-done.8.refs_3_ = f32[32,2,8,128]{3,2,1,0:T(8,128)S(1)} collective-permute-done((f32[32,2,8,128]{3,2,1,0:T(8,128)S(1)}, f32[32,2,8,128]{3,2,1,0:T(8,128)S(1)}, u32[]{:S(2)}, u32[]{:S(2)}) %collective-permute-start.8) | collective-permute-done | bytes 262176 | tf_op jit(solution)/shard_map/ppermute | solution.py:550
  36.1 0.0 copy-done
  36.1 4.2 %middle.1 = (f32[80,2,8,128]{3,2,1,0:T(8,128)S(1)}, f32[40,8,128]{2,1,0:T(8,128)S(1)}, f32[40,8,128]{2,1,0:T(8,128)S(1)}, f32[2,1,8,128]{3,2,1,0:T(8,128)S(1)}, ...) custom-call(s32[6]{0:T(128)S(1)} %stack.44.place_ref.refs_0_, s32[4]{0:T(128)S(1)} %copy-done, ...), custom_call_target="tpu_custom_call" | custom-call | tf_op jit(solution)/shard_map/middle/pallas_call | solution.py:555
  40.3 10.9 %all_to_all.11.refs_2_ = f32[32,1,8,128]{3,2,1,0:T(8,128)S(1)} all-to-all(f32[32,1,8,128]{3,2,1,0:T(8,128)S(1)} %bitcast.16), channel_id=1, replica_groups=mesh['px'=8,'py'=4] {'px','py'}, dimensions={0} | all-to-all | bytes 262144 | tf_op jit(solution)/shard_map/all_to_all | solution.py:549
  51.2 0.0 collective-permute-start.9
  51.2 1.3 %collective-permute-done.9.refs_3_ = f32[32,1,8,128]{3,2,1,0:T(8,128)S(1)} collective-permute-done((f32[32,1,8,128]{3,2,1,0:T(8,128)S(1)}, f32[32,1,8,128]{3,2,1,0:T(8,128)S(1)}, u32[]{:S(2)}, u32[]{:S(2)}) %collective-permute-start.9) | collective-permute-done | bytes 131104 | tf_op jit(solution)/shard_map/ppermute | solution.py:550
  52.6 3.2 %last.1 = f32[256,128]{1,0:T(8,128)} custom-call(s32[6]{0:T(128)S(1)} %stack.44.place_ref.refs_0_, s32[4]{0:T(128)S(1)} %copy-done, f32[32,1,8,128]{3,2,1,0:T(8,128)S(1)} %all_to_all.11.refs_2_, f32[32,1,8,128]{3,2,1,0:T(8,128)S(1)} %collective-permute-done.9.refs_3_, f32[80,2,8,128]{3,2,1,0:T(8,128)S(1)} %get-tuple-element.46.refs_4_, ...), custom_call_target="tpu_custom_call" | custom-call | tf_op jit(solution)/shard_map/last/pallas_call | solution.py:559
  (2 shorter events, 0.0 us)
Async XLA Ops:
  0.0 36.1 %copy-start = (s32[4]{0:T(128)S(1)}, s32[4]{0:T(128)}, u32[]{:S(2)}) copy-start(s32[4]{0:T(128)} %refs_1_.3) | copy-start | bytes 52
  2.1 8.7 %collective-permute-start = (f32[24,2,8,128]{3,2,1,0:T(8,128)S(1)}, f32[24,2,8,128]{3,2,1,0:T(8,128)S(1)}, u32[]{:S(2)}, u32[]{:S(2)}) collective-permute-start(f32[24,2,8,128]{3,2,1,0:T(8,128)S(1)} %get-tuple-element.31), channel_id=1, source_target_pairs={{0,4},{1,5},{2,6},{3,7},{4,0},{5,1},{6,2},{7,3},{8,12},{9,13},{10,... | collective-permute-start | bytes 589832 | tf_op jit(solution)/shard_map/ppermute | solution.py:487
  2.7 10.4 %collective-permute-start.1 = (f32[24,2,8,128]{3,2,1,0:T(8,128)S(1)}, f32[24,2,8,128]{3,2,1,0:T(8,128)S(1)}, u32[]{:S(2)}, u32[]{:S(2)}) collective-permute-start(f32[24,2,8,128]{3,2,1,0:T(8,128)S(1)} %get-tuple-element.33), channel_id=1, source_target_pairs={{0,1},{1,0},{2,3},{3,2},{4,8},{5,9},{6,10},{7,11},{8,4},{9,5},{10,... | collective-permute-start | bytes 589832 | tf_op jit(solution)/shard_map/ppermute | solution.py:487
  5.3 5.1 %collective-permute-start.2 = (f32[16,8,128]{2,1,0:T(8,128)S(1)}, f32[16,8,128]{2,1,0:T(8,128)S(1)}, u32[]{:S(2)}, u32[]{:S(2)}) collective-permute-start(f32[16,8,128]{2,1,0:T(8,128)S(1)} %get-tuple-element.34), channel_id=1, source_target_pairs={{0,1},{1,0},{2,3},{3,2},{4,5},{5,4},{6,7},{7,6},{8,9},{9,8},{10,11... | collective-permute-start | bytes 196616 | tf_op jit(solution)/shard_map/ppermute | solution.py:487
  5.4 5.0 %collective-permute-start.3 = (f32[16,8,128]{2,1,0:T(8,128)S(1)}, f32[16,8,128]{2,1,0:T(8,128)S(1)}, u32[]{:S(2)}, u32[]{:S(2)}) collective-permute-start(f32[16,8,128]{2,1,0:T(8,128)S(1)} %get-tuple-element.35), channel_id=1, source_target_pairs={{0,4},{1,2},{2,1},{3,7},{4,0},{5,6},{6,5},{7,3},{8,12},{9,10},{10,... | collective-permute-start | bytes 196616 | tf_op jit(solution)/shard_map/ppermute | solution.py:487
  10.4 2.7 %collective-permute-start.4 = (f32[16,8,128]{2,1,0:T(8,128)S(1)}, f32[16,8,128]{2,1,0:T(8,128)S(1)}, u32[]{:S(2)}, u32[]{:S(2)}) collective-permute-start(f32[16,8,128]{2,1,0:T(8,128)S(1)} %collective-permute-done.2.ya), channel_id=1, source_target_pairs={{0,4},{1,5},{2,6},{3,7},{4,0},{5,1},{6,2},{7,3},{8,12},{9,13},{10,... | collective-permute-start | bytes 196616 | tf_op jit(solution)/shard_map/ppermute | solution.py:487
  10.4 2.7 %collective-permute-start.5 = (f32[16,8,128]{2,1,0:T(8,128)S(1)}, f32[16,8,128]{2,1,0:T(8,128)S(1)}, u32[]{:S(2)}, u32[]{:S(2)}) collective-permute-start(f32[16,8,128]{2,1,0:T(8,128)S(1)} %collective-permute-done.3.yb), channel_id=1, source_target_pairs={{0,4},{1,5},{2,6},{3,7},{4,0},{5,1},{6,2},{7,3},{8,12},{9,13},{10,... | collective-permute-start | bytes 196616 | tf_op jit(solution)/shard_map/ppermute | solution.py:487
  10.9 4.1 %collective-permute-start.6 = (f32[12,8,128]{2,1,0:T(8,128)S(1)}, f32[12,8,128]{2,1,0:T(8,128)S(1)}, u32[]{:S(2)}, u32[]{:S(2)}) collective-permute-start(f32[12,8,128]{2,1,0:T(8,128)S(1)} %get-tuple-element.36), channel_id=1, source_target_pairs={{0,1},{1,0},{2,3},{3,2},{4,9},{5,8},{6,11},{7,10},{8,5},{9,4},{10,... | collective-permute-start | bytes 147464 | tf_op jit(solution)/shard_map/ppermute | solution.py:487
  12.9 2.1 %collective-permute-start.7 = (f32[12,8,128]{2,1,0:T(8,128)S(1)}, f32[12,8,128]{2,1,0:T(8,128)S(1)}, u32[]{:S(2)}, u32[]{:S(2)}) collective-permute-start(f32[12,8,128]{2,1,0:T(8,128)S(1)} %get-tuple-element.37), channel_id=1, source_target_pairs={{0,4},{1,2},{2,1},{3,7},{4,0},{5,10},{6,9},{7,3},{8,12},{9,6},{10,... | collective-permute-start | bytes 147464 | tf_op jit(solution)/shard_map/ppermute | solution.py:487
  34.5 1.6 %collective-permute-start.8 = (f32[32,2,8,128]{3,2,1,0:T(8,128)S(1)}, f32[32,2,8,128]{3,2,1,0:T(8,128)S(1)}, u32[]{:S(2)}, u32[]{:S(2)}) collective-permute-start(f32[32,2,8,128]{3,2,1,0:T(8,128)S(1)} %all_to_all.10.refs_2_), channel_id=1, source_target_pairs={{0,4},{4,0},{8,12},{12,8},{16,20},{20,16},{24,28},{28,24},{1,5},{5... | collective-permute-start | bytes 786440 | tf_op jit(solution)/shard_map/ppermute | solution.py:550
  51.2 1.3 %collective-permute-start.9 = (f32[32,1,8,128]{3,2,1,0:T(8,128)S(1)}, f32[32,1,8,128]{3,2,1,0:T(8,128)S(1)}, u32[]{:S(2)}, u32[]{:S(2)}) collective-permute-start(f32[32,1,8,128]{3,2,1,0:T(8,128)S(1)} %all_to_all.11.refs_2_), channel_id=1, source_target_pairs={{0,4},{4,0},{8,12},{12,8},{16,20},{20,16},{24,28},{28,24},{1,5},{5... | collective-permute-start | bytes 393224 | tf_op jit(solution)/shard_map/ppermute | solution.py:550

commit v11 on v9

--- a/solution.py
+++ b/solution.py
@@ -502,13 +502,13 @@
             return x ^ 1, y
         return far(x) if inner_x else x, far(y)
 
+    xa = swap(xa, lambda x, y, inner_x, inner_y: (x ^ 1, y))
+    xb = swap(xb, lambda x, y, inner_x, inner_y: (far(x), y) if inner_x else (x, y ^ 1))
+    ya, yb, ba, bb, xa = lax.optimization_barrier((ya, yb, ba, bb, xa))
     ya = swap(ya, lambda x, y, inner_x, inner_y: (x, y ^ 1))
-    xa = swap(xa, lambda x, y, inner_x, inner_y: (x ^ 1, y))
     yb = swap(yb, lambda x, y, inner_x, inner_y: (x, far(y)) if inner_y else (x ^ 1, y))
-    xb = swap(xb, lambda x, y, inner_x, inner_y: (far(x), y) if inner_x else (x, y ^ 1))
-    ba, bb, xa = lax.optimization_barrier((ba, bb, xa))
+    ba = swap(ba, lambda x, y, inner_x, inner_y: (far(x) if inner_x else x, y ^ 1))
     bb = swap(bb, corner)
-    ba = swap(ba, lambda x, y, inner_x, inner_y: (far(x) if inner_x else x, y ^ 1))
     aa, ab = (swap(part, lambda x, y, inner_x, inner_y: (x ^ 1, y)) for part in (ya, yb))
     return xa, xb, ya, yb, aa, ab, ba, bb
 

time: 56 us -> 56 us (level)
  no operation moved by 1% of the time
where the time goes in v11:
time: 56 us; the launch traced here: 55.9 us
  blocking collectives  27.4 us (49%)
  Pallas kernels  11.5 us (21%)
  waiting for transfers between devices  8.06 us (14%)
  starting transfers between devices  7.68 us (14%)
  other arithmetic  1 us (2%)
    all_to_all x2, blocking collectives, gather(): half = lax.all_to_all(every, ('px', 'py'), 0, 0, tiled=True)  27.4 us
    ppermute x8, starting transfers between devices, swap(): return lax.ppermute(block, ('px', 'py'), pairs)  7.28 us
    ppermute x8, waiting for transfers between devices, swap(): return lax.ppermute(block, ('px', 'py'), pairs)  5.55 us
    pallas_call x1, Pallas kernels, shards(): call(sized(middle_kernel), 'middle', 2, 8, (fine, mid, mid, arr(2, 1, lay...  4.22 us
    pallas_call x1, Pallas kernels, shards(): call(sized(last_kernel), 'last', 2, 10, arr(layers * rows, LANES), (low,...  3.23 us
    pallas_call x1, Pallas kernels, shards(): call(descend_kernel, 'descend', 1, 9, (fine, fine, fine_cos, mid, mid, mi...  3.08 us
    ppermute x2, waiting for transfers between devices, gather(): return (half, lax.ppermute(half, 'px', [(i, i ^ 1) for i in range(npx)]))  2.51 us
  transfers between devices with their start and end apart: 10, of which 4 were waited for; matrix products, arithmetic and copies ran while one was open for 0% of the time, Pallas kernels for 0%

profile of v11, /device:TPU:0, one launch (start us, length us, event | category | flops | bytes accessed | tf_op | source)
XLA Modules:
  0.0 55.9 jit_solution(10372555952416348826)
XLA Ops:
  0.0 0.0 copy-start
  0.0 1.0 %pad_maximum_fusion = f32[2,8,32,128]{3,2,1,0:T(8,128)S(1)} fusion(f32[1,8,32,128]{3,2,1,0:T(8,128)} %bitcast.17, f32[1,8,32,128]{3,2,1,0:T(8,128)} %bitcast.18), kind=kLoop, calls=%fused_computation | loop fusion | flops 65536 | bytes 524288 | tf_op jit(solution)/shard_map/stack | solution.py:545
  1.0 0.1 stack.44.place_ref.refs_0_
  1.1 1.0 %cut.1 = (f32[32,2,8,128]{3,2,1,0:T(8,128)S(1)}, f32[24,2,8,128]{3,2,1,0:T(8,128)S(1)}, f32[24,2,8,128]{3,2,1,0:T(8,128)S(1)}, f32[16,8,128]{2,1,0:T(8,128)S(1)}...) custom-call(s32[6]{0:T(128)S(1)} %stack.44.place_ref.refs_0_, ...), custom_call_target="tpu_custom_call" | custom-call | tf_op jit(solution)/shard_map/cut/pallas_call | solution.py:546
  2.1 0.5 collective-permute-start
  2.6 2.6 %collective-permute-start.1 = (f32[24,2,8,128]{3,2,1,0:T(8,128)S(1)}, f32[24,2,8,128]{3,2,1,0:T(8,128)S(1)}, u32[]{:S(2)}, u32[]{:S(2)}) collective-permute-start(f32[24,2,8,128]{3,2,1,0:T(8,128)S(1)} %get-tuple-element.37), channel_id=1, source_target_pairs={{0,1},{1,0},{2,3},{3,2},{4,8},{5,9},{6,10},{7,11},{8,4},{9,5},{10,... | collective-permute-start | bytes 589832 | tf_op jit(solution)/shard_map/ppermute | solution.py:495
  5.3 0.0 collective-permute-done.xa
  5.3 1.4 %collective-permute-start.2 = (f32[16,8,128]{2,1,0:T(8,128)S(1)}, f32[16,8,128]{2,1,0:T(8,128)S(1)}, u32[]{:S(2)}, u32[]{:S(2)}) collective-permute-start(f32[16,8,128]{2,1,0:T(8,128)S(1)} %get-tuple-element.38), channel_id=1, source_target_pairs={{0,1},{1,0},{2,3},{3,2},{4,5},{5,4},{6,7},{7,6},{8,9},{9,8},{10,11... | collective-permute-start | bytes 196616 | tf_op jit(solution)/shard_map/ppermute | solution.py:495
  6.6 0.0 collective-permute-start.3
  6.6 3.7 %collective-permute-done.2.ya = f32[16,8,128]{2,1,0:T(8,128)S(1)} collective-permute-done((f32[16,8,128]{2,1,0:T(8,128)S(1)}, f32[16,8,128]{2,1,0:T(8,128)S(1)}, u32[]{:S(2)}, u32[]{:S(2)}) %collective-permute-start.2) | collective-permute-done | bytes 65568 | tf_op jit(solution)/shard_map/ppermute | solution.py:495
  10.3 0.0 collective-permute-start.4
  10.3 0.0 collective-permute-done.3.yb
  10.3 0.5 collective-permute-start.5
  10.8 2.0 %collective-permute-start.6 = (f32[12,8,128]{2,1,0:T(8,128)S(1)}, f32[12,8,128]{2,1,0:T(8,128)S(1)}, u32[]{:S(2)}, u32[]{:S(2)}) collective-permute-start(f32[12,8,128]{2,1,0:T(8,128)S(1)} %get-tuple-element.40), channel_id=1, source_target_pairs={{0,1},{1,0},{2,3},{3,2},{4,9},{5,8},{6,11},{7,10},{8,5},{9,4},{10,... | collective-permute-start | bytes 147464 | tf_op jit(solution)/shard_map/ppermute | solution.py:495
  12.9 0.2 collective-permute-start.7
  13.1 0.0 collective-permute-done.1.xb
  13.1 1.8 %collective-permute-done.6.ba = f32[12,8,128]{2,1,0:T(8,128)S(1)} collective-permute-done((f32[12,8,128]{2,1,0:T(8,128)S(1)}, f32[12,8,128]{2,1,0:T(8,128)S(1)}, u32[]{:S(2)}, u32[]{:S(2)}) %collective-permute-start.6) | collective-permute-done | bytes 49184 | tf_op jit(solution)/shard_map/ppermute | solution.py:495
  14.9 0.0 collective-permute-done.7.bb
  14.9 0.0 collective-permute-done.4.aa
  14.9 0.0 collective-permute-done.5.ab
  15.0 3.1 %descend.1 = (f32[80,2,8,128]{3,2,1,0:T(8,128)S(1)}, f32[80,2,8,128]{3,2,1,0:T(8,128)S(1)}, f32[7,80,2,8,128]{4,3,2,1,0:T(8,128)S(1)}, f32[40,8,128]{2,1,0:T(8,1...) custom-call(s32[6]{0:T(128)S(1)} %stack.44.place_ref.refs_0_, ...), custom_call_target="tpu_custom_call" | custom-call | tf_op jit(solution)/shard_map/descend/pallas_call | solution.py:549
  18.1 16.5 %all_to_all.10.refs_2_ = f32[32,2,8,128]{3,2,1,0:T(8,128)S(1)} all-to-all(f32[32,2,8,128]{3,2,1,0:T(8,128)S(1)} %bitcast.15), channel_id=1, replica_groups=mesh['px'=8,'py'=4] {'px','py'}, dimensions={0} | all-to-all | bytes 524288 | tf_op jit(solution)/shard_map/all_to_all | solution.py:557
  34.6 0.4 collective-permute-start.8
  35.0 1.2 %collective-permute-done.8.refs_3_ = f32[32,2,8,128]{3,2,1,0:T(8,128)S(1)} collective-permute-done((f32[32,2,8,128]{3,2,1,0:T(8,128)S(1)}, f32[32,2,8,128]{3,2,1,0:T(8,128)S(1)}, u32[]{:S(2)}, u32[]{:S(2)}) %collective-permute-start.8) | collective-permute-done | bytes 262176 | tf_op jit(solution)/shard_map/ppermute | solution.py:558
  36.1 0.0 copy-done
  36.1 4.2 %middle.1 = (f32[80,2,8,128]{3,2,1,0:T(8,128)S(1)}, f32[40,8,128]{2,1,0:T(8,128)S(1)}, f32[40,8,128]{2,1,0:T(8,128)S(1)}, f32[2,1,8,128]{3,2,1,0:T(8,128)S(1)}, ...) custom-call(s32[6]{0:T(128)S(1)} %stack.44.place_ref.refs_0_, s32[4]{0:T(128)S(1)} %copy-done, ...), custom_call_target="tpu_custom_call" | custom-call | tf_op jit(solution)/shard_map/middle/pallas_call | solution.py:563
  40.4 10.9 %all_to_all.11.refs_2_ = f32[32,1,8,128]{3,2,1,0:T(8,128)S(1)} all-to-all(f32[32,1,8,128]{3,2,1,0:T(8,128)S(1)} %bitcast.16), channel_id=1, replica_groups=mesh['px'=8,'py'=4] {'px','py'}, dimensions={0} | all-to-all | bytes 262144 | tf_op jit(solution)/shard_map/all_to_all | solution.py:557
  51.3 0.0 collective-permute-start.9
  51.3 1.3 %collective-permute-done.9.refs_3_ = f32[32,1,8,128]{3,2,1,0:T(8,128)S(1)} collective-permute-done((f32[32,1,8,128]{3,2,1,0:T(8,128)S(1)}, f32[32,1,8,128]{3,2,1,0:T(8,128)S(1)}, u32[]{:S(2)}, u32[]{:S(2)}) %collective-permute-start.9) | collective-permute-done | bytes 131104 | tf_op jit(solution)/shard_map/ppermute | solution.py:558
  52.6 3.2 %last.1 = f32[256,128]{1,0:T(8,128)} custom-call(s32[6]{0:T(128)S(1)} %stack.44.place_ref.refs_0_, s32[4]{0:T(128)S(1)} %copy-done, f32[32,1,8,128]{3,2,1,0:T(8,128)S(1)} %all_to_all.11.refs_2_, f32[32,1,8,128]{3,2,1,0:T(8,128)S(1)} %collective-permute-done.9.refs_3_, f32[80,2,8,128]{3,2,1,0:T(8,128)S(1)} %get-tuple-element.50.refs_4_, ...), custom_call_target="tpu_custom_call" | custom-call | tf_op jit(solution)/shard_map/last/pallas_call | solution.py:567
  (2 shorter events, 0.0 us)
Async XLA Ops:
  0.0 36.1 %copy-start = (s32[4]{0:T(128)S(1)}, s32[4]{0:T(128)}, u32[]{:S(2)}) copy-start(s32[4]{0:T(128)} %refs_1_.3) | copy-start | bytes 52
  2.1 3.2 %collective-permute-start = (f32[24,2,8,128]{3,2,1,0:T(8,128)S(1)}, f32[24,2,8,128]{3,2,1,0:T(8,128)S(1)}, u32[]{:S(2)}, u32[]{:S(2)}) collective-permute-start(f32[24,2,8,128]{3,2,1,0:T(8,128)S(1)} %get-tuple-element.35), channel_id=1, source_target_pairs={{0,4},{1,5},{2,6},{3,7},{4,0},{5,1},{6,2},{7,3},{8,12},{9,13},{10,... | collective-permute-start | bytes 589832 | tf_op jit(solution)/shard_map/ppermute | solution.py:495
  2.6 10.5 %collective-permute-start.1 = (f32[24,2,8,128]{3,2,1,0:T(8,128)S(1)}, f32[24,2,8,128]{3,2,1,0:T(8,128)S(1)}, u32[]{:S(2)}, u32[]{:S(2)}) collective-permute-start(f32[24,2,8,128]{3,2,1,0:T(8,128)S(1)} %get-tuple-element.37), channel_id=1, source_target_pairs={{0,1},{1,0},{2,3},{3,2},{4,8},{5,9},{6,10},{7,11},{8,4},{9,5},{10,... | collective-permute-start | bytes 589832 | tf_op jit(solution)/shard_map/ppermute | solution.py:495
  5.3 5.1 %collective-permute-start.2 = (f32[16,8,128]{2,1,0:T(8,128)S(1)}, f32[16,8,128]{2,1,0:T(8,128)S(1)}, u32[]{:S(2)}, u32[]{:S(2)}) collective-permute-start(f32[16,8,128]{2,1,0:T(8,128)S(1)} %get-tuple-element.38), channel_id=1, source_target_pairs={{0,1},{1,0},{2,3},{3,2},{4,5},{5,4},{6,7},{7,6},{8,9},{9,8},{10,11... | collective-permute-start | bytes 196616 | tf_op jit(solution)/shard_map/ppermute | solution.py:495
  6.6 3.7 %collective-permute-start.3 = (f32[16,8,128]{2,1,0:T(8,128)S(1)}, f32[16,8,128]{2,1,0:T(8,128)S(1)}, u32[]{:S(2)}, u32[]{:S(2)}) collective-permute-start(f32[16,8,128]{2,1,0:T(8,128)S(1)} %get-tuple-element.39), channel_id=1, source_target_pairs={{0,4},{1,2},{2,1},{3,7},{4,0},{5,6},{6,5},{7,3},{8,12},{9,10},{10,... | collective-permute-start | bytes 196616 | tf_op jit(solution)/shard_map/ppermute | solution.py:495
  10.3 4.6 %collective-permute-start.4 = (f32[16,8,128]{2,1,0:T(8,128)S(1)}, f32[16,8,128]{2,1,0:T(8,128)S(1)}, u32[]{:S(2)}, u32[]{:S(2)}) collective-permute-start(f32[16,8,128]{2,1,0:T(8,128)S(1)} %collective-permute-done.2.ya), channel_id=1, source_target_pairs={{0,4},{1,5},{2,6},{3,7},{4,0},{5,1},{6,2},{7,3},{8,12},{9,13},{10,... | collective-permute-start | bytes 196616 | tf_op jit(solution)/shard_map/ppermute | solution.py:495
  10.3 4.6 %collective-permute-start.5 = (f32[16,8,128]{2,1,0:T(8,128)S(1)}, f32[16,8,128]{2,1,0:T(8,128)S(1)}, u32[]{:S(2)}, u32[]{:S(2)}) collective-permute-start(f32[16,8,128]{2,1,0:T(8,128)S(1)} %collective-permute-done.3.yb), channel_id=1, source_target_pairs={{0,4},{1,5},{2,6},{3,7},{4,0},{5,1},{6,2},{7,3},{8,12},{9,13},{10,... | collective-permute-start | bytes 196616 | tf_op jit(solution)/shard_map/ppermute | solution.py:495
  10.8 4.1 %collective-permute-start.6 = (f32[12,8,128]{2,1,0:T(8,128)S(1)}, f32[12,8,128]{2,1,0:T(8,128)S(1)}, u32[]{:S(2)}, u32[]{:S(2)}) collective-permute-start(f32[12,8,128]{2,1,0:T(8,128)S(1)} %get-tuple-element.40), channel_id=1, source_target_pairs={{0,1},{1,0},{2,3},{3,2},{4,9},{5,8},{6,11},{7,10},{8,5},{9,4},{10,... | collective-permute-start | bytes 147464 | tf_op jit(solution)/shard_map/ppermute | solution.py:495
  12.9 2.1 %collective-permute-start.7 = (f32[12,8,128]{2,1,0:T(8,128)S(1)}, f32[12,8,128]{2,1,0:T(8,128)S(1)}, u32[]{:S(2)}, u32[]{:S(2)}) collective-permute-start(f32[12,8,128]{2,1,0:T(8,128)S(1)} %get-tuple-element.41), channel_id=1, source_target_pairs={{0,4},{1,2},{2,1},{3,7},{4,0},{5,10},{6,9},{7,3},{8,12},{9,6},{10,... | collective-permute-start | bytes 147464 | tf_op jit(solution)/shard_map/ppermute | solution.py:495
  34.6 1.6 %collective-permute-start.8 = (f32[32,2,8,128]{3,2,1,0:T(8,128)S(1)}, f32[32,2,8,128]{3,2,1,0:T(8,128)S(1)}, u32[]{:S(2)}, u32[]{:S(2)}) collective-permute-start(f32[32,2,8,128]{3,2,1,0:T(8,128)S(1)} %all_to_all.10.refs_2_), channel_id=1, source_target_pairs={{0,4},{4,0},{8,12},{12,8},{16,20},{20,16},{24,28},{28,24},{1,5},{5... | collective-permute-start | bytes 786440 | tf_op jit(solution)/shard_map/ppermute | solution.py:558
  51.3 1.3 %collective-permute-start.9 = (f32[32,1,8,128]{3,2,1,0:T(8,128)S(1)}, f32[32,1,8,128]{3,2,1,0:T(8,128)S(1)}, u32[]{:S(2)}, u32[]{:S(2)}) collective-permute-start(f32[32,1,8,128]{3,2,1,0:T(8,128)S(1)} %all_to_all.11.refs_2_), channel_id=1, source_target_pairs={{0,4},{4,0},{8,12},{12,8},{16,20},{20,16},{24,28},{28,24},{1,5},{5... | collective-permute-start | bytes 393224 | tf_op jit(solution)/shard_map/ppermute | solution.py:558
